TPU v7x, 32 devices: a whole 2x2x4 slice. The times are simulated.
32 devices in a mesh: groups: 2 (over y), space: 16 (over z, x, core).
Axes of the slice: x: 2, y: 2, z: 4, core: 2. Of those that a mesh axis runs over, the one named last changes fastest.
Arguments:
- modes: float32 [4, 128, 32, 64], P('groups', None, 'space'), parts along dimension 0, may hold values from -6 to 6
- cell_weight: float32 [32, 128], P('space', 'groups'), parts along dimension 1, may hold values from 0.5 to 2
- seeds: int32 [256], P(('groups', 'space')), parts along dimension 0, may hold values from 0 to 255
- coeff_table: float32 [256, 128], replicated, may hold values from -6 to 6
- force_table: float32 [256, 128], replicated, may hold values from -6 to 6
- visc_table: float32 [256], replicated, may hold values from 0.02 to 0.2
Outputs:
- coefficients: float32 [256, 128], P(('groups', 'space')), parts along dimension 0
There are 2 independent parts, one for each index of `groups`. A program takes and returns all parts, laid end to end along the dimension named above; an argument that names none is the same for every part. Nothing has to cross between parts.
All inputs are finite; a program needn't handle non-finite values.
Results may differ from a plain program's by a relative error of at most 0.00013.
Values sent between devices are 32-bit elements; how exact they have to be, the bound alone decides.
No kernel may reach another device: no remote copies, remote signals or barrier semaphores. Data moves between devices by JAX's collectives and lax.ppermute only.
A program may use at most 64 MiB of HBM per device.

v0:
```python
import math

import jax
import jax.numpy as jnp
from jax import lax
from jax.sharding import PartitionSpec as P

STEPS = 2


TIME_STEP = 0.5


def padded_2(array, sides, width):
    for axis, dim in sides:
        devices, length = (lax.axis_size(axis), array.shape[dim])
        up = [(i, (i + 1) % devices) for i in range(devices)]
        down = [(j, i) for i, j in up]
        last = lax.slice_in_dim(array, length - width, length, axis=dim)
        first = lax.slice_in_dim(array, 0, width, axis=dim)
        before = lax.ppermute(last, axis, up)
        after = lax.ppermute(first, axis, down)
        array = jnp.concatenate([before, array, after], axis=dim)
    return array


def shards(modes, cell_weight, seeds, coeff_table, force_table, visc_table):
    mode_count = modes.shape[1]
    slab_cells = modes.shape[2]
    across = modes.shape[3]
    devices = lax.axis_size("space")
    cell_count = slab_cells * across
    total_cells = cell_count * devices
    padded = padded_2(modes, (("space", 2),), 2)
    slope_along = (
        padded[:, :, 0:slab_cells]
        - 8.0 * padded[:, :, 1 : slab_cells + 1]
        + 8.0 * padded[:, :, 3 : slab_cells + 3]
        - padded[:, :, 4 : slab_cells + 4]
    ) / 12.0
    slope_across = (
        jnp.roll(modes, 2, 3)
        - 8.0 * jnp.roll(modes, 1, 3)
        + 8.0 * jnp.roll(modes, -1, 3)
        - jnp.roll(modes, -2, 3)
    ) / 12.0
    slopes = jnp.stack([slope_along, slope_across]).reshape(2, 2, mode_count, cell_count)
    velocity = modes.reshape(2, mode_count, cell_count)
    cell_scale = cell_weight.reshape(cell_count) / total_cells
    weighted = velocity * cell_scale[None, None, :]
    diffusion = lax.psum(
        jnp.einsum(
            "taic,tajc->ij",
            slopes * cell_scale[None, None, None, :],
            slopes,
            precision=lax.Precision.HIGHEST,
        ),
        "space",
    )
    selector = (
        seeds[:, None] == jnp.arange(coeff_table.shape[0], dtype=jnp.int32)[None, :]
    ).astype(jnp.float32)
    coeffs = jnp.dot(selector, coeff_table, precision=lax.Precision.HIGHEST)
    forcing = jnp.dot(selector, force_table, precision=lax.Precision.HIGHEST)
    viscosity = jnp.dot(selector, visc_table, precision=lax.Precision.HIGHEST)
    own_count = coeffs.shape[0]

    def field_block(coeff_rows):
        flow = jnp.einsum("ni,aic->anc", coeff_rows, velocity, precision=lax.Precision.HIGHEST)
        grads = jnp.einsum("nk,takc->tanc", coeff_rows, slopes, precision=lax.Precision.HIGHEST)
        carried = jnp.sum(flow[:, None, :, :] * grads, axis=0)
        return jnp.einsum("aic,anc->ni", weighted, carried, precision=lax.Precision.HIGHEST)

    for repeat in range(STEPS):
        everyone = lax.all_gather(coeffs, "space", axis=0, tiled=True)
        rows_each = math.gcd(own_count * lax.axis_size("space"), 128)
        stacked = everyone.reshape(
            own_count * lax.axis_size("space") // rows_each, rows_each, mode_count
        )
        quadratic = lax.psum_scatter(
            lax.map(field_block, stacked).reshape(own_count * lax.axis_size("space"), mode_count),
            "space",
            scatter_dimension=0,
            tiled=True,
        )
        linear = jnp.dot(coeffs, diffusion, precision=lax.Precision.HIGHEST)
        coeffs = coeffs + TIME_STEP * (forcing - viscosity[:, None] * linear - quadratic)
    return coeffs


def solution(mesh):
    placed = (
        P("groups", None, "space", None),
        P("space", "groups"),
        P(("groups", "space")),
        P(),
        P(),
        P(),
    )
    return jax.shard_map(
        shards, mesh=mesh, in_specs=placed, out_specs=P(("groups", "space"), None), check_vma=False
    )
```

profile of v0, /device:TPU:0, one launch (start us, length us, event | category | flops | bytes accessed | tf_op | source)
XLA Modules:
  0.0 239.6 jit_solution(18027088971304564999)
XLA Ops:
  6.5 0.0 copy-start
  6.5 0.0 copy-start.1
  6.5 0.0 all-reduce.8.cloned.1.call-start
  6.5 0.5 collective-permute-start
  7.0 5.0 %collective-permute-start.1 = (f32[2,128,2,64]{1,3,2,0:T(8,128)}, f32[2,128,2,64]{1,3,2,0:T(8,128)S(1)}, u32[]{:S(2)}, u32[]{:S(2)}) collective-permute-start(f32[2,128,2,64]{1,3,2,0:T(8,128)} %param.6), channel_id=1, source_target_pairs={{1,0},{2,1},{3,2},{4,3},{5,4},{6,5},{7,6},{8,7},{9,8},{10,9},{11,1... | collective-permute-start | bytes 393224 | tf_op jit(solution)/shard_map/ppermute | solution.py:22
  12.0 1.0 slice_bitcast_fusion
  13.0 0.0 copy-done.1
  13.1 0.1 fusion.23
  13.2 0.0 copy-start.4
  13.2 0.1 copy.35
  13.3 0.0 copy-done
  13.3 0.5 copy-done.4
  13.8 0.2 fusion.34
  14.0 19.5 %all_gather.6 = f32[128,128]{1,0:T(8,128)S(1)} all-gather(f32[8,128]{1,0:T(8,128)S(1)} %fusion.34), channel_id=1, replica_groups=mesh['groups'=2,'space'=16] {'space'}, dimensions={0}, use_global_device_ids=true | all-gather | bytes 69632 | tf_op jit(solution)/shard_map/all_gather | solution.py:75
  33.5 0.1 copy.39
  33.6 0.3 convolution_bitcast_fusion.3
  33.9 0.0 copy-start.5
  33.9 0.0 copy-start.3
  33.9 0.1 copy.37
  34.0 0.6 copy-done.5
  34.6 0.1 div.18
  34.7 0.0 copy-start.7
  34.7 0.7 copy-done.7
  35.3 0.6 dynamic-slice.2
  36.5 0.0 copy-done.3
  36.6 0.2 fusion.33
  36.8 0.0 collective-permute-done
  36.8 0.0 collective-permute-done.1
  36.8 0.1 copy.34
  36.9 0.6 fusion.2
  37.5 1.0 convolution_bitcast_fusion.6
  38.5 1.0 convolution_bitcast_fusion.5
  39.5 0.0 all-reduce.8.cloned.1.call-update
  39.6 0.0 copy-start.6
  39.6 0.0 all-reduce.6.cloned.1.call-start
  39.6 0.6 copy-done.6
  40.2 0.2 convolution_bitcast_fusion.7
  40.4 83.7 %all-reduce.8.cloned.1.call-done = (f32[128,128]{1,0:T(8,128)}, f32[128,128]{1,0:T(8,128)}) async-done(((f32[128,128]{1,0:T(8,128)}, f32[128,128]{1,0:T(8,128)}), (f32[128,128]{1,0:T(8,128)}, f32[128,128]{1,0:T(8,128)})) %all-reduce.8.cloned.1.call-update) | async-done | bytes 131088 | tf_op jit(solution)/shard_map/psum | solution.py:51
  124.1 1.0 fusion.11
  125.1 22.3 %all_gather.7 = f32[128,128]{1,0:T(8,128)S(1)} all-gather(f32[8,128]{1,0:T(8,128)S(1)} %fusion.11), channel_id=1, replica_groups=mesh['groups'=2,'space'=16] {'space'}, dimensions={0}, use_global_device_ids=true | all-gather | bytes 69632 | tf_op jit(solution)/shard_map/all_gather | solution.py:75
  147.4 0.3 convolution_bitcast_fusion.2
  147.7 0.1 copy.42
  147.8 0.6 fusion.3
  148.4 1.0 convolution_bitcast_fusion.4
  149.4 0.0 copy-start.2
  149.4 0.0 all-reduce.6.cloned.1.call-update
  149.4 81.9 %all-reduce.6.cloned.1.call-done = f32[128,128]{1,0:T(8,128)} async-done(((f32[128,128]{1,0:T(8,128)}), f32[128,128]{1,0:T(8,128)}) %all-reduce.6.cloned.1.call-update) | async-done | bytes 65552
  231.3 0.0 copy-done.2
  231.3 1.4 fusion.7
  (5 shorter events, 0.1 us)
Async XLA Ops:
  6.5 6.7 %copy-start = (f32[256,128]{1,0:T(8,128)S(1)}, f32[256,128]{1,0:T(8,128)}, u32[]{:S(2)}) copy-start(f32[256,128]{1,0:T(8,128)} %param.9) | copy-start | bytes 393220
  6.5 6.5 %copy-start.1 = (f32[2,128,2,64]{1,3,2,0:T(8,128)S(1)}, f32[2,128,2,64]{1,3,2,0:T(8,128)}, u32[]{:S(2)}) copy-start(f32[2,128,2,64]{1,3,2,0:T(8,128)} %param.6) | copy-start | bytes 393220
  6.5 117.6 %all-reduce.8.cloned.1.call-start = ((), (), s32[]{:S(2)}) async-start(), calls=%async_computation.1 | async-start | bytes 262144 | tf_op jit(solution)/shard_map/psum | solution.py:51
  6.5 30.2 %collective-permute-start = (f32[2,128,2,64]{1,3,2,0:T(8,128)}, f32[2,128,2,64]{1,3,2,0:T(8,128)S(1)}, u32[]{:S(2)}, u32[]{:S(2)}) collective-permute-start(f32[2,128,2,64]{1,3,2,0:T(8,128)} %param.6), channel_id=1, source_target_pairs={{0,1},{1,2},{2,3},{3,4},{4,5},{5,6},{6,7},{7,8},{8,9},{9,10},{10,1... | collective-permute-start | bytes 393224 | tf_op jit(solution)/shard_map/ppermute | solution.py:21
  7.0 29.8 %collective-permute-start.1 = (f32[2,128,2,64]{1,3,2,0:T(8,128)}, f32[2,128,2,64]{1,3,2,0:T(8,128)S(1)}, u32[]{:S(2)}, u32[]{:S(2)}) collective-permute-start(f32[2,128,2,64]{1,3,2,0:T(8,128)} %param.6), channel_id=1, source_target_pairs={{1,0},{2,1},{3,2},{4,3},{5,4},{6,5},{7,6},{8,7},{9,8},{10,9},{11,1... | collective-permute-start | bytes 393224 | tf_op jit(solution)/shard_map/ppermute | solution.py:22
  13.2 0.7 copy-start.4
  33.9 0.7 copy-start.5
  33.9 2.7 %copy-start.3 = (f32[256,128]{1,0:T(8,128)S(1)}, f32[256,128]{1,0:T(8,128)}, u32[]{:S(2)}) copy-start(f32[256,128]{1,0:T(8,128)} %param.10) | copy-start | bytes 393220
  34.7 0.7 copy-start.7
  39.6 0.7 copy-start.6
  39.6 191.8 %all-reduce.6.cloned.1.call-start = ((), (), s32[]{:S(2)}) async-start(), calls=%async_computation | async-start | bytes 131072
  149.4 81.9 %copy-start.2 = (f32[128,128]{1,0:T(8,128)S(1)}, f32[128,128]{1,0:T(8,128)}, u32[]{:S(2)}) copy-start(f32[128,128]{1,0:T(8,128)} %get-tuple-element.27) | copy-start | bytes 196612
Sparse Core Ops, SparseCore 0:
  39.7 84.3 all-reduce.7
  149.6 81.7 all-reduce.5
where the time goes:
time: 241 us; the launch traced here: 240 us
  waiting for transfers between devices  166 us (69%)
  blocking collectives  41.8 us (17%)
  between operations  14.2 us (6%)
  matrix products  7.8 us (3%)
  starting transfers between devices  5.52 us (2%)
  local copies, waits for them, and re-layouts  4.56 us (2%)
    psum x1, waiting for transfers between devices, shards(): lax.psum(jnp.einsum('taic,tajc->ij', slopes * cell_scale[None, None, None...  83.7 us
    unnamed x3, waiting for transfers between devices  81.9 us
    all_gather x2, blocking collectives, shards(): everyone = lax.all_gather(coeffs, 'space', axis=0, tiled=True)  41.8 us
    ppermute x1, starting transfers between devices, padded_2(): after = lax.ppermute(first, axis, down)  5.02 us
  transfers between devices with their start and end apart: 4, of which 2 were waited for; matrix products, arithmetic and copies ran while one was open for 1% of the time, Pallas kernels for 0%

commit v1 on v0

v1 whole, which is shorter than its diff:
```python
import functools

import jax
import jax.numpy as jnp
from jax import lax
from jax.experimental import pallas as pl
from jax.experimental.pallas import tpu as pltpu
from jax.sharding import PartitionSpec as P

STEPS = 2


TIME_STEP = 0.5
SPARE_ROWS = 8


def pack_kernel(modes_ref, weight_ref, chunk_ref):
    components, mode_count, layers, across = modes_ref.shape
    for a in range(components):
        for layer in range(layers):
            chunk_ref[a * mode_count : (a + 1) * mode_count, layer * across : (layer + 1) * across] = modes_ref[
                a, :, layer, :
            ]
    rows = components * mode_count
    for layer in range(layers):
        chunk_ref[rows : rows + SPARE_ROWS, layer * across : (layer + 1) * across] = jnp.broadcast_to(
            weight_ref[layer : layer + 1, :], (SPARE_ROWS, across)
        )


def pack(modes, cell_weight):
    components, mode_count, layers, across = modes.shape
    return pl.pallas_call(
        pack_kernel,
        out_shape=jax.ShapeDtypeStruct((components * mode_count + SPARE_ROWS, layers * across), jnp.float32),
        name="pack",
    )(modes, cell_weight)


def exchange(array, mask):
    devices = lax.axis_size("space")
    return lax.ppermute(array, "space", [(i, i ^ mask) for i in range(devices)])


def spread(array, masks):
    held = {0: array}
    for mask in masks:
        for place in list(held):
            held[place ^ mask] = exchange(held[place], mask)
    return held


def gather(chunk):
    devices = lax.axis_size("space")
    if devices < 16 or devices & (devices - 1):
        everyone = lax.all_gather(chunk, "space")
        return [everyone[j] for j in range(devices)], False
    near = devices // 4
    far = devices // 2 + near
    side = []
    while 2 << len(side) < near:
        side.append(2 << len(side))
    opposite = exchange(chunk, far)
    held = spread(chunk, side + [near])
    for place, array in spread(opposite, [near] + side).items():
        held[far ^ place] = array
    for place in list(held):
        held[place ^ 1] = exchange(held[place], 1)
    return [held[j] for j in range(devices)], True


def halves(array):
    high = array.astype(jnp.bfloat16)
    low = (array - high.astype(jnp.float32)).astype(jnp.bfloat16)
    return high, low


def step_kernel(
    layers, across, me_ref, seeds_ref, visc_ref, coeff_ref, force_ref, *refs
):
    *chunk_refs, out_ref, mode_ref, weight_ref, start_ref, force_rows_ref = refs
    devices = len(chunk_refs)
    own, mode_count = out_ref.shape
    components = mode_ref.shape[0]
    lanes = layers * across
    total_cells = devices * lanes

    me = me_ref[0]
    for j, chunk_ref in enumerate(chunk_refs):
        place = jnp.bitwise_xor(me, j)
        columns = pl.ds(pl.multiple_of(place * lanes, lanes), lanes)
        for a in range(components):
            high, low = halves(chunk_ref[a * mode_count : (a + 1) * mode_count, :])
            mode_ref[a, 0:mode_count, columns] = high
            mode_ref[a, mode_count : 2 * mode_count, columns] = low
        rows = components * mode_count
        weight_ref[:, columns] = chunk_ref[rows : rows + SPARE_ROWS, :] / total_cells

    row_id = lax.broadcasted_iota(jnp.int32, (own, lanes), 0)
    visc = jnp.zeros((own, lanes), jnp.float32)
    for n in range(own):
        seed = seeds_ref[n]
        start_ref[n : n + 1, :] = coeff_ref[pl.ds(seed, 1), :]
        force_rows_ref[n : n + 1, :] = force_ref[pl.ds(seed, 1), :]
        visc = jnp.where(row_id == n, visc_ref[seed], visc)
    coeffs = start_ref[...]
    forcing = force_rows_ref[...]

    lane = lax.broadcasted_iota(jnp.int32, (own, lanes), 1)
    y = lane % across

    def along(field, shift):
        whole, part = divmod(shift, layers)
        if part == 0:
            return [field[(p + whole) % devices] for p in range(devices)]
        rolled = [pltpu.roll(f, (lanes - part * across) % lanes, 1) for f in field]
        inside = lane < (layers - part) * across
        return [
            jnp.where(inside, rolled[(p + whole) % devices], rolled[(p + whole + 1) % devices]) for p in range(devices)
        ]

    def across_by(f, shift):
        plain = pltpu.roll(f, -shift % lanes, 1)
        if shift > 0:
            return jnp.where(y < across - shift, plain, pltpu.roll(f, (across - shift) % lanes, 1))
        return jnp.where(y >= -shift, plain, pltpu.roll(f, (lanes - across - shift) % lanes, 1))

    def slope(m2, m1, p1, p2):
        return (m2 - 8.0 * m1 + 8.0 * p1 - p2) / 12.0

    def slope_along(field):
        shifted = [along(field, s) for s in (-2, -1, 1, 2)]
        return [slope(*(s[p] for s in shifted)) for p in range(devices)]

    def slope_across(field):
        return [slope(*(across_by(f, s) for s in (-2, -1, 1, 2))) for f in field]

    weight = [weight_ref[0:1, p * lanes : (p + 1) * lanes] for p in range(devices)]

    for repeat in range(STEPS):
        high, low = halves(coeffs)
        left = jnp.concatenate(
            [jnp.concatenate([high, high], axis=1), jnp.concatenate([low, low], axis=1)], axis=0
        )
        flow = []
        for a in range(components):
            both = jnp.dot(left, mode_ref[a], preferred_element_type=jnp.float32)
            both = both[:own] + both[own:]
            flow.append([both[:, p * lanes : (p + 1) * lanes] for p in range(devices)])
        change = jnp.zeros((own, mode_count), jnp.float32)
        for a in range(components):
            x_slope = slope_along(flow[a])
            y_slope = slope_across(flow[a])
            x_flux = [weight[p] * x_slope[p] for p in range(devices)]
            y_flux = [weight[p] * y_slope[p] for p in range(devices)]
            x_spread = slope_along(x_flux)
            y_spread = slope_across(y_flux)
            source = jnp.concatenate(
                [
                    flow[0][p] * x_flux[p] + flow[1][p] * y_flux[p] - visc * (x_spread[p] + y_spread[p])
                    for p in range(devices)
                ],
                axis=1,
            )
            high, low = halves(source)
            right = lax.dot_general(
                jnp.concatenate([high, low], axis=0),
                mode_ref[a],
                (((1,), (1,)), ((), ())),
                preferred_element_type=jnp.float32,
            )
            right = right[:own] + right[own:]
            change = change + right[:, :mode_count] + right[:, mode_count:]
        coeffs = coeffs + TIME_STEP * (forcing - change)
    out_ref[...] = coeffs


def shards(modes, cell_weight, seeds, coeff_table, force_table, visc_table):
    components, mode_count, layers, across = modes.shape
    own = seeds.shape[0]
    chunks, by_offset = gather(pack(modes, cell_weight))
    me = jnp.full((1,), lax.axis_index("space") if by_offset else 0, jnp.int32)
    smem = pl.BlockSpec(memory_space=pltpu.SMEM)
    vmem = pl.BlockSpec(memory_space=pltpu.VMEM)
    cells = len(chunks) * layers * across
    return pl.pallas_call(
        functools.partial(step_kernel, layers, across),
        out_shape=jax.ShapeDtypeStruct((own, mode_count), jnp.float32),
        in_specs=[smem] * 3 + [vmem] * (2 + len(chunks)),
        out_specs=vmem,
        scratch_shapes=[
            pltpu.VMEM((components, 2 * mode_count, cells), jnp.bfloat16),
            pltpu.VMEM((SPARE_ROWS, cells), jnp.float32),
            pltpu.VMEM((own, mode_count), jnp.float32),
            pltpu.VMEM((own, mode_count), jnp.float32),
        ],
        compiler_params=pltpu.CompilerParams(vmem_limit_bytes=56 * 1024 * 1024),
        name="steps",
    )(me, seeds, visc_table, coeff_table, force_table, *chunks)


def solution(mesh):
    placed = (
        P("groups", None, "space", None),
        P("space", "groups"),
        P(("groups", "space")),
        P(),
        P(),
        P(),
    )
    return jax.shard_map(
        shards, mesh=mesh, in_specs=placed, out_specs=P(("groups", "space"), None), check_vma=False
    )
```

time: 241 us -> 32.4 us (0.13)
  waiting for transfers between devices: 166 us -> 8.68 us
  blocking collectives: 41.8 us -> 0 us
  between operations: 14.2 us -> 0.19 us
  starting transfers between devices: 5.52 us -> 13.4 us
  matrix products: 7.8 us -> 0 us
  Pallas kernels: 0 us -> 7.68 us
    psum x1 -> x0, waiting for transfers between devices: 83.7 us -> none  [shards(): lax.psum(jnp.einsum('taic,tajc->ij', slopes * cell_scale[None, None, None...]
    unnamed x3 -> x0, waiting for transfers between devices: 81.9 us -> none
    all_gather x2 -> x0, blocking collectives: 41.8 us -> none  [shards(): everyone = lax.all_gather(coeffs, 'space', axis=0, tiled=True)]
    ppermute x2 -> x15, waiting for transfers between devices: 0.01 us -> 8.68 us  [exchange(): return lax.ppermute(array, 'space', [(i, i ^ mask) for i in range(devices)])]
    ppermute x2 -> x15, starting transfers between devices: 5.48 us -> 13.4 us  [exchange(): return lax.ppermute(array, 'space', [(i, i ^ mask) for i in range(devices)])]
    dot_general x12 -> x0, matrix products: 7.8 us -> none  [the longest x2 2.43 us: shards(): linear = jnp.dot(coeffs, diffusion, precision=lax.Precision.HIGHEST)]
    pallas_call x0 -> x2, Pallas kernels: none -> 7.68 us  [the longest x1 5.94 us: shards(): pl.pallas_call(functools.partial(step_kernel, layers, across), out_shape=...]
  transfers between devices with their start and end apart: 4 -> 15, of which waited for: 2 -> 5; matrix products, arithmetic and copies ran while one was open for 1% -> 0% of each run, Pallas kernels for 0% -> 0%
where the time goes in v1:
time: 32.4 us; the launch traced here: 32.3 us
  starting transfers between devices  13.4 us (41%)
  waiting for transfers between devices  8.68 us (27%)
  Pallas kernels  7.68 us (24%)
  local copies, waits for them, and re-layouts  2.34 us (7%)
    ppermute x15, starting transfers between devices, exchange(): return lax.ppermute(array, 'space', [(i, i ^ mask) for i in range(devices)])  13.4 us
    ppermute x15, waiting for transfers between devices, exchange(): return lax.ppermute(array, 'space', [(i, i ^ mask) for i in range(devices)])  8.68 us
    pallas_call x1, Pallas kernels, shards(): pl.pallas_call(functools.partial(step_kernel, layers, across), out_shape=...  5.94 us
    unnamed x31, local copies, waits for them, and re-layouts  2.34 us
    pallas_call x1, Pallas kernels, pack(): pl.pallas_call(pack_kernel, out_shape=jax.ShapeDtypeStruct((components *...  1.75 us
  transfers between devices with their start and end apart: 15, of which 5 were waited for; matrix products, arithmetic and copies ran while one was open for 0% of the time, Pallas kernels for 0%

profile of v1, /device:TPU:0, one launch (start us, length us, event | category | flops | bytes accessed | tf_op | source)
XLA Modules:
  0.0 32.3 jit_solution(17181317423826698003)
XLA Ops:
  0.0 1.7 %copy.7.modes_ref = f32[2,128,2,64]{3,2,1,0:T(2,128)} copy(f32[2,128,2,64]{1,3,2,0:T(8,128)} %param.6) | data formatting | bytes 262144 | tf_op args[0]
  1.7 1.7 %pack.1.refs_0_ = f32[264,128]{1,0:T(8,128)} custom-call(f32[2,128,2,64]{3,2,1,0:T(2,128)} %copy.7.modes_ref, f32[2,64]{1,0:T(2,128)} %weight_ref.1), custom_call_target="tpu_custom_call" | custom-call | tf_op jit(solution)/shard_map/pack/pallas_call | solution.py:33
  3.5 5.0 %collective-permute-start.7 = (f32[264,128]{1,0:T(8,128)}, f32[264,128]{1,0:T(8,128)S(1)}, u32[]{:S(2)}, u32[]{:S(2)}) collective-permute-start(f32[264,128]{1,0:T(8,128)} %pack.1.refs_0_), channel_id=1, source_target_pairs={{0,12},{1,13},{2,14},{3,15},{4,8},{5,9},{6,10},{7,11},{8,4},{9,5},... | collective-permute-start | bytes 405512 | tf_op jit(solution)/shard_map/ppermute | solution.py:42
  8.5 1.5 %collective-permute-start.1 = (f32[264,128]{1,0:T(8,128)}, f32[264,128]{1,0:T(8,128)S(1)}, u32[]{:S(2)}, u32[]{:S(2)}) collective-permute-start(f32[264,128]{1,0:T(8,128)} %pack.1.refs_0_), channel_id=1, source_target_pairs={{0,2},{1,3},{2,0},{3,1},{4,6},{5,7},{6,4},{7,5},{8,10},{9,11},{10,... | collective-permute-start | bytes 405512 | tf_op jit(solution)/shard_map/ppermute | solution.py:42
  10.0 0.0 collective-permute-start.3
  10.0 0.0 collective-permute-start
  10.0 3.2 %collective-permute-done.7.refs_12_ = f32[264,128]{1,0:T(8,128)S(1)} collective-permute-done((f32[264,128]{1,0:T(8,128)}, f32[264,128]{1,0:T(8,128)S(1)}, u32[]{:S(2)}, u32[]{:S(2)}) %collective-permute-start.7) | collective-permute-done | bytes 135200 | tf_op jit(solution)/shard_map/ppermute | solution.py:42
  13.2 0.0 copy-start
  13.2 1.8 %collective-permute-start.8 = (f32[264,128]{1,0:T(8,128)S(1)}, f32[264,128]{1,0:T(8,128)S(1)}, u32[]{:S(2)}, u32[]{:S(2)}) collective-permute-start(f32[264,128]{1,0:T(8,128)S(1)} %collective-permute-done.7.refs_12_), channel_id=1, source_target_pairs={{0,4},{1,5},{2,6},{3,7},{4,0},{5,1},{6,2},{7,3},{8,12},{9,13},{10,... | collective-permute-start | bytes 405512 | tf_op jit(solution)/shard_map/ppermute | solution.py:42
  15.0 1.5 %collective-permute-start.13 = (f32[264,128]{1,0:T(8,128)S(1)}, f32[264,128]{1,0:T(8,128)S(1)}, u32[]{:S(2)}, u32[]{:S(2)}) collective-permute-start(f32[264,128]{1,0:T(8,128)S(1)} %collective-permute-done.7.refs_12_), channel_id=1, source_target_pairs={{0,2},{1,3},{2,0},{3,1},{4,6},{5,7},{6,4},{7,5},{8,10},{9,11},{10,... | collective-permute-start | bytes 405512 | tf_op jit(solution)/shard_map/ppermute | solution.py:42
  16.4 0.0 collective-permute-done.1.refs_2_
  16.4 0.0 copy-start.1
  16.4 0.5 %collective-permute-start.5 = (f32[264,128]{1,0:T(8,128)S(1)}, f32[264,128]{1,0:T(8,128)S(1)}, u32[]{:S(2)}, u32[]{:S(2)}) collective-permute-start(f32[264,128]{1,0:T(8,128)S(1)} %collective-permute-done.1.refs_2_), channel_id=1, source_target_pairs={{0,4},{1,5},{2,6},{3,7},{4,0},{5,1},{6,2},{7,3},{8,12},{9,13},{10,... | collective-permute-start | bytes 405512 | tf_op jit(solution)/shard_map/ppermute | solution.py:42
  16.9 0.0 collective-permute-done.3.refs_4_
  16.9 0.0 copy-start.2
  16.9 0.0 collective-permute-start.12
  16.9 0.0 collective-permute-done.refs_1_
  17.0 0.0 copy-start.3
  17.0 0.5 %collective-permute-start.2 = (f32[264,128]{1,0:T(8,128)S(1)}, f32[264,128]{1,0:T(8,128)S(1)}, u32[]{:S(2)}, u32[]{:S(2)}) collective-permute-start(f32[264,128]{1,0:T(8,128)S(1)} %collective-permute-done.1.refs_2_), channel_id=1, source_target_pairs={{0,1},{1,0},{2,3},{3,2},{4,5},{5,4},{6,7},{7,6},{8,9},{9,8},{10,11... | collective-permute-start | bytes 405512 | tf_op jit(solution)/shard_map/ppermute | solution.py:42
  17.5 1.8 %collective-permute-done.8.refs_8_ = f32[264,128]{1,0:T(8,128)S(1)} collective-permute-done((f32[264,128]{1,0:T(8,128)S(1)}, f32[264,128]{1,0:T(8,128)S(1)}, u32[]{:S(2)}, u32[]{:S(2)}) %collective-permute-start.8) | collective-permute-done | bytes 135200 | tf_op jit(solution)/shard_map/ppermute | solution.py:42
  19.3 0.0 copy-start.4
  19.3 1.9 %collective-permute-start.10 = (f32[264,128]{1,0:T(8,128)S(1)}, f32[264,128]{1,0:T(8,128)S(1)}, u32[]{:S(2)}, u32[]{:S(2)}) collective-permute-start(f32[264,128]{1,0:T(8,128)S(1)} %collective-permute-done.8.refs_8_), channel_id=1, source_target_pairs={{0,2},{1,3},{2,0},{3,1},{4,6},{5,7},{6,4},{7,5},{8,10},{9,11},{10,... | collective-permute-start | bytes 405512 | tf_op jit(solution)/shard_map/ppermute | solution.py:42
  21.2 0.0 collective-permute-done.13.refs_14_
  21.2 0.0 copy-start.5
  21.2 0.0 collective-permute-start.4
  21.2 0.3 collective-permute-done.5.refs_6_
  21.5 0.0 copy-start.6
  21.5 0.2 collective-permute-start.9
  21.7 0.0 collective-permute-done.12.refs_13_
  21.7 0.0 copy-start.7
  21.7 0.3 collective-permute-start.14
  22.0 0.0 collective-permute-done.2.refs_3_
  22.0 0.0 copy-start.8
  22.0 0.2 collective-permute-start.6
  22.2 2.1 %collective-permute-done.10.refs_10_ = f32[264,128]{1,0:T(8,128)S(1)} collective-permute-done((f32[264,128]{1,0:T(8,128)S(1)}, f32[264,128]{1,0:T(8,128)S(1)}, u32[]{:S(2)}, u32[]{:S(2)}) %collective-permute-start.10) | collective-permute-done | bytes 135200 | tf_op jit(solution)/shard_map/ppermute | solution.py:42
  24.3 0.0 copy-start.9
  24.3 0.0 collective-permute-start.11
  24.3 0.0 collective-permute-done.4.refs_5_
  24.3 0.0 copy-start.10
  24.3 0.0 collective-permute-done.9.refs_9_
  24.3 0.0 copy-start.11
  24.4 0.0 collective-permute-done.14.refs_15_
  24.4 0.0 copy-start.12
  24.4 0.0 collective-permute-done.6.refs_7_
  24.4 0.0 copy-start.13
  24.4 1.3 %collective-permute-done.11.refs_11_ = f32[264,128]{1,0:T(8,128)S(1)} collective-permute-done((f32[264,128]{1,0:T(8,128)S(1)}, f32[264,128]{1,0:T(8,128)S(1)}, u32[]{:S(2)}, u32[]{:S(2)}) %collective-permute-start.11) | collective-permute-done | bytes 135200 | tf_op jit(solution)/shard_map/ppermute | solution.py:42
  25.7 0.0 copy-start.14
  25.7 0.0 copy-done
  25.7 0.0 copy-done.1
  25.7 0.0 copy-done.2
  25.7 0.0 copy-done.3
  25.7 0.0 copy-done.4
  25.7 0.0 copy-done.5
  25.7 0.0 copy-done.6
  25.7 0.0 copy-done.7
  25.7 0.0 copy-done.8
  25.7 0.0 copy-done.9
  25.7 0.0 copy-done.10
  25.8 0.0 copy-done.11
  25.8 0.0 copy-done.12
  25.8 0.0 copy-done.13
  25.8 0.5 %copy-done.14 = f32[264,128]{1,0:T(8,128)} copy-done((f32[264,128]{1,0:T(8,128)}, f32[264,128]{1,0:T(8,128)S(1)}, u32[]{:S(2)}) %copy-start.14) | copy-done | bytes 135192
  26.3 5.9 %steps.1 = f32[8,128]{1,0:T(8,128)} custom-call(s32[1]{0:T(128)} %bitcast.me_ref, s32[8]{0:T(128)} %seeds_ref.1, f32[256]{0:T(256)} %visc_ref.1, f32[256,128]{1,0:T(8,128)} %coeff_ref.1, f32[256,128]{1,0:T(8,128)} %force_ref.1, f32[264,128]{1,0:T(8,128)} %pack.1.refs_0_, f32[264,128]{1,0:T(8,128)} %copy-done.3, f32[264,128]{1,0:T(8,128)} %copy-done.1, ...), custom_call_target="tpu_custom_call" | custom-call | tf_op jit(solution)/shard_map/steps/pallas_call | solution.py:186
Async XLA Ops:
  3.5 9.7 %collective-permute-start.7 = (f32[264,128]{1,0:T(8,128)}, f32[264,128]{1,0:T(8,128)S(1)}, u32[]{:S(2)}, u32[]{:S(2)}) collective-permute-start(f32[264,128]{1,0:T(8,128)} %pack.1.refs_0_), channel_id=1, source_target_pairs={{0,12},{1,13},{2,14},{3,15},{4,8},{5,9},{6,10},{7,11},{8,4},{9,5},... | collective-permute-start | bytes 405512 | tf_op jit(solution)/shard_map/ppermute | solution.py:42
  8.5 7.9 %collective-permute-start.1 = (f32[264,128]{1,0:T(8,128)}, f32[264,128]{1,0:T(8,128)S(1)}, u32[]{:S(2)}, u32[]{:S(2)}) collective-permute-start(f32[264,128]{1,0:T(8,128)} %pack.1.refs_0_), channel_id=1, source_target_pairs={{0,2},{1,3},{2,0},{3,1},{4,6},{5,7},{6,4},{7,5},{8,10},{9,11},{10,... | collective-permute-start | bytes 405512 | tf_op jit(solution)/shard_map/ppermute | solution.py:42
  10.0 6.9 %collective-permute-start.3 = (f32[264,128]{1,0:T(8,128)}, f32[264,128]{1,0:T(8,128)S(1)}, u32[]{:S(2)}, u32[]{:S(2)}) collective-permute-start(f32[264,128]{1,0:T(8,128)} %pack.1.refs_0_), channel_id=1, source_target_pairs={{0,4},{1,5},{2,6},{3,7},{4,0},{5,1},{6,2},{7,3},{8,12},{9,13},{10,... | collective-permute-start | bytes 405512 | tf_op jit(solution)/shard_map/ppermute | solution.py:42
  10.0 6.9 %collective-permute-start = (f32[264,128]{1,0:T(8,128)}, f32[264,128]{1,0:T(8,128)S(1)}, u32[]{:S(2)}, u32[]{:S(2)}) collective-permute-start(f32[264,128]{1,0:T(8,128)} %pack.1.refs_0_), channel_id=1, source_target_pairs={{0,1},{1,0},{2,3},{3,2},{4,5},{5,4},{6,7},{7,6},{8,9},{9,8},{10,11... | collective-permute-start | bytes 405512 | tf_op jit(solution)/shard_map/ppermute | solution.py:42
  13.2 12.5 %copy-start = (f32[264,128]{1,0:T(8,128)}, f32[264,128]{1,0:T(8,128)S(1)}, u32[]{:S(2)}) copy-start(f32[264,128]{1,0:T(8,128)S(1)} %collective-permute-done.7.refs_12_) | copy-start | bytes 405508
  13.2 6.1 %collective-permute-start.8 = (f32[264,128]{1,0:T(8,128)S(1)}, f32[264,128]{1,0:T(8,128)S(1)}, u32[]{:S(2)}, u32[]{:S(2)}) collective-permute-start(f32[264,128]{1,0:T(8,128)S(1)} %collective-permute-done.7.refs_12_), channel_id=1, source_target_pairs={{0,4},{1,5},{2,6},{3,7},{4,0},{5,1},{6,2},{7,3},{8,12},{9,13},{10,... | collective-permute-start | bytes 405512 | tf_op jit(solution)/shard_map/ppermute | solution.py:42
  15.0 6.2 %collective-permute-start.13 = (f32[264,128]{1,0:T(8,128)S(1)}, f32[264,128]{1,0:T(8,128)S(1)}, u32[]{:S(2)}, u32[]{:S(2)}) collective-permute-start(f32[264,128]{1,0:T(8,128)S(1)} %collective-permute-done.7.refs_12_), channel_id=1, source_target_pairs={{0,2},{1,3},{2,0},{3,1},{4,6},{5,7},{6,4},{7,5},{8,10},{9,11},{10,... | collective-permute-start | bytes 405512 | tf_op jit(solution)/shard_map/ppermute | solution.py:42
  16.4 9.2 %copy-start.1 = (f32[264,128]{1,0:T(8,128)}, f32[264,128]{1,0:T(8,128)S(1)}, u32[]{:S(2)}) copy-start(f32[264,128]{1,0:T(8,128)S(1)} %collective-permute-done.1.refs_2_) | copy-start | bytes 405508
  16.4 5.0 %collective-permute-start.5 = (f32[264,128]{1,0:T(8,128)S(1)}, f32[264,128]{1,0:T(8,128)S(1)}, u32[]{:S(2)}, u32[]{:S(2)}) collective-permute-start(f32[264,128]{1,0:T(8,128)S(1)} %collective-permute-done.1.refs_2_), channel_id=1, source_target_pairs={{0,4},{1,5},{2,6},{3,7},{4,0},{5,1},{6,2},{7,3},{8,12},{9,13},{10,... | collective-permute-start | bytes 405512 | tf_op jit(solution)/shard_map/ppermute | solution.py:42
  16.9 8.7 %copy-start.2 = (f32[264,128]{1,0:T(8,128)}, f32[264,128]{1,0:T(8,128)S(1)}, u32[]{:S(2)}) copy-start(f32[264,128]{1,0:T(8,128)S(1)} %collective-permute-done.3.refs_4_) | copy-start | bytes 405508
  16.9 4.8 %collective-permute-start.12 = (f32[264,128]{1,0:T(8,128)S(1)}, f32[264,128]{1,0:T(8,128)S(1)}, u32[]{:S(2)}, u32[]{:S(2)}) collective-permute-start(f32[264,128]{1,0:T(8,128)S(1)} %collective-permute-done.7.refs_12_), channel_id=1, source_target_pairs={{0,1},{1,0},{2,3},{3,2},{4,5},{5,4},{6,7},{7,6},{8,9},{9,8},{10,11... | collective-permute-start | bytes 405512 | tf_op jit(solution)/shard_map/ppermute | solution.py:42
  17.0 8.7 %copy-start.3 = (f32[264,128]{1,0:T(8,128)}, f32[264,128]{1,0:T(8,128)S(1)}, u32[]{:S(2)}) copy-start(f32[264,128]{1,0:T(8,128)S(1)} %collective-permute-done.refs_1_) | copy-start | bytes 405508
  17.0 5.0 %collective-permute-start.2 = (f32[264,128]{1,0:T(8,128)S(1)}, f32[264,128]{1,0:T(8,128)S(1)}, u32[]{:S(2)}, u32[]{:S(2)}) collective-permute-start(f32[264,128]{1,0:T(8,128)S(1)} %collective-permute-done.1.refs_2_), channel_id=1, source_target_pairs={{0,1},{1,0},{2,3},{3,2},{4,5},{5,4},{6,7},{7,6},{8,9},{9,8},{10,11... | collective-permute-start | bytes 405512 | tf_op jit(solution)/shard_map/ppermute | solution.py:42
  19.3 6.4 %copy-start.4 = (f32[264,128]{1,0:T(8,128)}, f32[264,128]{1,0:T(8,128)S(1)}, u32[]{:S(2)}) copy-start(f32[264,128]{1,0:T(8,128)S(1)} %collective-permute-done.8.refs_8_) | copy-start | bytes 405508
  19.3 5.0 %collective-permute-start.10 = (f32[264,128]{1,0:T(8,128)S(1)}, f32[264,128]{1,0:T(8,128)S(1)}, u32[]{:S(2)}, u32[]{:S(2)}) collective-permute-start(f32[264,128]{1,0:T(8,128)S(1)} %collective-permute-done.8.refs_8_), channel_id=1, source_target_pairs={{0,2},{1,3},{2,0},{3,1},{4,6},{5,7},{6,4},{7,5},{8,10},{9,11},{10,... | collective-permute-start | bytes 405512 | tf_op jit(solution)/shard_map/ppermute | solution.py:42
  21.2 4.5 %copy-start.5 = (f32[264,128]{1,0:T(8,128)}, f32[264,128]{1,0:T(8,128)S(1)}, u32[]{:S(2)}) copy-start(f32[264,128]{1,0:T(8,128)S(1)} %collective-permute-done.13.refs_14_) | copy-start | bytes 405508
  21.2 3.1 %collective-permute-start.4 = (f32[264,128]{1,0:T(8,128)S(1)}, f32[264,128]{1,0:T(8,128)S(1)}, u32[]{:S(2)}, u32[]{:S(2)}) collective-permute-start(f32[264,128]{1,0:T(8,128)S(1)} %collective-permute-done.3.refs_4_), channel_id=1, source_target_pairs={{0,1},{1,0},{2,3},{3,2},{4,5},{5,4},{6,7},{7,6},{8,9},{9,8},{10,11... | collective-permute-start | bytes 405512 | tf_op jit(solution)/shard_map/ppermute | solution.py:42
  21.5 4.3 %copy-start.6 = (f32[264,128]{1,0:T(8,128)}, f32[264,128]{1,0:T(8,128)S(1)}, u32[]{:S(2)}) copy-start(f32[264,128]{1,0:T(8,128)S(1)} %collective-permute-done.5.refs_6_) | copy-start | bytes 405508
  21.5 2.9 %collective-permute-start.9 = (f32[264,128]{1,0:T(8,128)S(1)}, f32[264,128]{1,0:T(8,128)S(1)}, u32[]{:S(2)}, u32[]{:S(2)}) collective-permute-start(f32[264,128]{1,0:T(8,128)S(1)} %collective-permute-done.8.refs_8_), channel_id=1, source_target_pairs={{0,1},{1,0},{2,3},{3,2},{4,5},{5,4},{6,7},{7,6},{8,9},{9,8},{10,11... | collective-permute-start | bytes 405512 | tf_op jit(solution)/shard_map/ppermute | solution.py:42
  21.7 4.0 %copy-start.7 = (f32[264,128]{1,0:T(8,128)}, f32[264,128]{1,0:T(8,128)S(1)}, u32[]{:S(2)}) copy-start(f32[264,128]{1,0:T(8,128)S(1)} %collective-permute-done.12.refs_13_) | copy-start | bytes 405508
  21.7 2.7 %collective-permute-start.14 = (f32[264,128]{1,0:T(8,128)S(1)}, f32[264,128]{1,0:T(8,128)S(1)}, u32[]{:S(2)}, u32[]{:S(2)}) collective-permute-start(f32[264,128]{1,0:T(8,128)S(1)} %collective-permute-done.13.refs_14_), channel_id=1, source_target_pairs={{0,1},{1,0},{2,3},{3,2},{4,5},{5,4},{6,7},{7,6},{8,9},{9,8},{10,11... | collective-permute-start | bytes 405512 | tf_op jit(solution)/shard_map/ppermute | solution.py:42
  22.0 3.8 %copy-start.8 = (f32[264,128]{1,0:T(8,128)}, f32[264,128]{1,0:T(8,128)S(1)}, u32[]{:S(2)}) copy-start(f32[264,128]{1,0:T(8,128)S(1)} %collective-permute-done.2.refs_3_) | copy-start | bytes 405508
  22.0 2.4 %collective-permute-start.6 = (f32[264,128]{1,0:T(8,128)S(1)}, f32[264,128]{1,0:T(8,128)S(1)}, u32[]{:S(2)}, u32[]{:S(2)}) collective-permute-start(f32[264,128]{1,0:T(8,128)S(1)} %collective-permute-done.5.refs_6_), channel_id=1, source_target_pairs={{0,1},{1,0},{2,3},{3,2},{4,5},{5,4},{6,7},{7,6},{8,9},{9,8},{10,11... | collective-permute-start | bytes 405512 | tf_op jit(solution)/shard_map/ppermute | solution.py:42
  24.3 1.4 %copy-start.9 = (f32[264,128]{1,0:T(8,128)}, f32[264,128]{1,0:T(8,128)S(1)}, u32[]{:S(2)}) copy-start(f32[264,128]{1,0:T(8,128)S(1)} %collective-permute-done.10.refs_10_) | copy-start | bytes 405508
  24.3 1.4 %collective-permute-start.11 = (f32[264,128]{1,0:T(8,128)S(1)}, f32[264,128]{1,0:T(8,128)S(1)}, u32[]{:S(2)}, u32[]{:S(2)}) collective-permute-start(f32[264,128]{1,0:T(8,128)S(1)} %collective-permute-done.10.refs_10_), channel_id=1, source_target_pairs={{0,1},{1,0},{2,3},{3,2},{4,5},{5,4},{6,7},{7,6},{8,9},{9,8},{10,11... | collective-permute-start | bytes 405512 | tf_op jit(solution)/shard_map/ppermute | solution.py:42
  24.3 1.4 %copy-start.10 = (f32[264,128]{1,0:T(8,128)}, f32[264,128]{1,0:T(8,128)S(1)}, u32[]{:S(2)}) copy-start(f32[264,128]{1,0:T(8,128)S(1)} %collective-permute-done.4.refs_5_) | copy-start | bytes 405508
  24.3 1.4 %copy-start.11 = (f32[264,128]{1,0:T(8,128)}, f32[264,128]{1,0:T(8,128)S(1)}, u32[]{:S(2)}) copy-start(f32[264,128]{1,0:T(8,128)S(1)} %collective-permute-done.9.refs_9_) | copy-start | bytes 405508
  24.4 1.4 %copy-start.12 = (f32[264,128]{1,0:T(8,128)}, f32[264,128]{1,0:T(8,128)S(1)}, u32[]{:S(2)}) copy-start(f32[264,128]{1,0:T(8,128)S(1)} %collective-permute-done.14.refs_15_) | copy-start | bytes 405508
  24.4 1.4 %copy-start.13 = (f32[264,128]{1,0:T(8,128)}, f32[264,128]{1,0:T(8,128)S(1)}, u32[]{:S(2)}) copy-start(f32[264,128]{1,0:T(8,128)S(1)} %collective-permute-done.6.refs_7_) | copy-start | bytes 405508
  25.7 0.7 %copy-start.14 = (f32[264,128]{1,0:T(8,128)}, f32[264,128]{1,0:T(8,128)S(1)}, u32[]{:S(2)}) copy-start(f32[264,128]{1,0:T(8,128)S(1)} %collective-permute-done.11.refs_11_) | copy-start | bytes 405508

commit v2 on v1

v2 whole, which is shorter than its diff:
```python
import functools

import jax
import jax.numpy as jnp
from jax import lax
from jax.experimental import pallas as pl
from jax.experimental.pallas import tpu as pltpu
from jax.sharding import PartitionSpec as P

STEPS = 2


TIME_STEP = 0.5
SPARE_ROWS = 8


def pack_kernel(modes_ref, weight_ref, chunk_ref):
    rows = modes_ref.shape[0]
    layers, across = weight_ref.shape
    chunk_ref[0:rows, :] = modes_ref[...]
    for layer in range(layers):
        chunk_ref[rows : rows + SPARE_ROWS, layer * across : (layer + 1) * across] = jnp.broadcast_to(
            weight_ref[layer : layer + 1, :], (SPARE_ROWS, across)
        )


def pack(modes, cell_weight):
    rows, mode_count = modes.shape
    return pl.pallas_call(
        pack_kernel,
        out_shape=jax.ShapeDtypeStruct((rows + SPARE_ROWS, mode_count), jnp.float32),
        in_specs=[pl.BlockSpec(memory_space=pltpu.VMEM)] * 2,
        out_specs=pl.BlockSpec(memory_space=pltpu.VMEM),
        compiler_params=pltpu.CompilerParams(vmem_limit_bytes=2 * 1024 * 1024),
        name="pack",
    )(modes, cell_weight)


def exchange(held, even_mask, odd_mask):
    array, even, odd = held
    devices = lax.axis_size("space")
    pairs = [(i, i ^ (odd_mask if i & 1 else even_mask)) for i in range(devices)]
    array = lax.ppermute(array, "space", pairs)
    if even_mask & 1:
        even, odd = odd, even
    return array, even ^ even_mask, odd ^ odd_mask


def gather(modes, cell_weight, first_needed):
    components, mode_count, layers, across = modes.shape
    rows = modes.transpose(0, 2, 3, 1).reshape(components * layers * across, mode_count)
    devices = lax.axis_size("space")
    if devices < 16 or devices & (devices - 1):
        everyone = lax.all_gather(pack(rows, cell_weight), "space")
        return [(everyone[j], j, j) for j in range(devices)], False
    far = devices // 2
    near = far // 2
    side = near // 2
    far_rows, even, odd = exchange((rows, 0, 0), far, far)
    far_weight = exchange((cell_weight, 0, 0), far, far)[0]
    own = (pack(rows, cell_weight), 0, 0)
    far_rows, *_ = lax.optimization_barrier((far_rows, *first_needed))
    opposite = (pack(far_rows, far_weight), even, odd)
    held = []
    for start in (own, opposite):
        first = exchange(start, near, side)
        second = exchange(start, side, near)
        held += [start, first, second, exchange(first, side, near)]
    mask = side // 2
    while mask:
        held += [exchange(one, mask, mask) for one in held]
        mask //= 2
    return held, True


def halves(array):
    high = array.astype(jnp.bfloat16)
    low = (array - high.astype(jnp.float32)).astype(jnp.bfloat16)
    return high, low


def select_kernel(seeds_ref, visc_table_ref, coeff_table_ref, force_table_ref, coeff_ref, force_ref, visc_ref):
    own, mode_count = coeff_ref.shape
    row_id = lax.broadcasted_iota(jnp.int32, (own, mode_count), 0)
    visc = jnp.zeros((own, mode_count), jnp.float32)
    for n in range(own):
        seed = seeds_ref[n]
        coeff_ref[n : n + 1, :] = coeff_table_ref[pl.ds(seed, 1), :]
        force_ref[n : n + 1, :] = force_table_ref[pl.ds(seed, 1), :]
        visc = jnp.where(row_id == n, visc_table_ref[seed], visc)
    visc_ref[...] = visc


def select(seeds, coeff_table, force_table, visc_table):
    smem = pl.BlockSpec(memory_space=pltpu.SMEM)
    vmem = pl.BlockSpec(memory_space=pltpu.VMEM)
    rows = jax.ShapeDtypeStruct((seeds.shape[0], coeff_table.shape[1]), jnp.float32)
    return pl.pallas_call(
        select_kernel,
        out_shape=(rows, rows, rows),
        in_specs=[smem, smem, vmem, vmem],
        out_specs=(vmem, vmem, vmem),
        compiler_params=pltpu.CompilerParams(vmem_limit_bytes=2 * 1024 * 1024),
        name="select",
    )(seeds, visc_table, coeff_table, force_table)


def step_kernel(offsets, across, me_ref, coeff_ref, force_ref, visc_ref, *refs):
    *chunk_refs, out_ref, mode_ref, weight_ref = refs
    own, mode_count = out_ref.shape
    components = mode_ref.shape[0]
    devices, lanes = weight_ref.shape
    layers = lanes // across
    total_cells = devices * lanes

    me = me_ref[0, 0]
    odd = me % 2 == 1

    for (even_offset, odd_offset), chunk_ref in zip(offsets, chunk_refs):
        place = jnp.bitwise_xor(me, jnp.where(odd, odd_offset, even_offset))
        rows = pl.ds(pl.multiple_of(place * lanes, lanes), lanes)
        for a in range(components):
            high, low = halves(chunk_ref[a * lanes : (a + 1) * lanes, :])
            mode_ref[a, rows, 0:mode_count] = high
            mode_ref[a, rows, mode_count : 2 * mode_count] = low
        weight_ref[pl.ds(place, 1), :] = chunk_ref[components * lanes : components * lanes + 1, :] / total_cells

    visc = visc_ref[...]
    coeffs = coeff_ref[...]
    forcing = force_ref[...]

    lane = lax.broadcasted_iota(jnp.int32, (own, lanes), 1)
    y = lane % across

    def along(field, shift):
        whole, part = divmod(shift, layers)
        if part == 0:
            return [field[(p + whole) % devices] for p in range(devices)]
        rolled = [pltpu.roll(f, (lanes - part * across) % lanes, 1) for f in field]
        inside = lane < (layers - part) * across
        return [
            jnp.where(inside, rolled[(p + whole) % devices], rolled[(p + whole + 1) % devices]) for p in range(devices)
        ]

    def across_by(f, shift):
        plain = pltpu.roll(f, -shift % lanes, 1)
        if shift > 0:
            return jnp.where(y < across - shift, plain, pltpu.roll(f, (across - shift) % lanes, 1))
        return jnp.where(y >= -shift, plain, pltpu.roll(f, (lanes - across - shift) % lanes, 1))

    def slope(m2, m1, p1, p2):
        return (m2 - 8.0 * m1 + 8.0 * p1 - p2) / 12.0

    def slope_along(field):
        shifted = [along(field, s) for s in (-2, -1, 1, 2)]
        return [slope(*(s[p] for s in shifted)) for p in range(devices)]

    def slope_across(field):
        return [slope(*(across_by(f, s) for s in (-2, -1, 1, 2))) for f in field]

    weight = [weight_ref[p : p + 1, :] for p in range(devices)]

    for repeat in range(STEPS):
        high, low = halves(coeffs)
        left = jnp.concatenate(
            [jnp.concatenate([high, high], axis=1), jnp.concatenate([low, low], axis=1)], axis=0
        )
        flow = []
        for a in range(components):
            both = lax.dot_general(
                left, mode_ref[a], (((1,), (1,)), ((), ())), preferred_element_type=jnp.float32
            )
            both = both[:own] + both[own:]
            flow.append([both[:, p * lanes : (p + 1) * lanes] for p in range(devices)])
        change = jnp.zeros((own, mode_count), jnp.float32)
        for a in range(components):
            x_slope = slope_along(flow[a])
            y_slope = slope_across(flow[a])
            x_flux = [weight[p] * x_slope[p] for p in range(devices)]
            y_flux = [weight[p] * y_slope[p] for p in range(devices)]
            x_spread = slope_along(x_flux)
            y_spread = slope_across(y_flux)
            source = jnp.concatenate(
                [
                    flow[0][p] * x_flux[p] + flow[1][p] * y_flux[p] - visc * (x_spread[p] + y_spread[p])
                    for p in range(devices)
                ],
                axis=1,
            )
            high, low = halves(source)
            right = jnp.dot(
                jnp.concatenate([high, low], axis=0), mode_ref[a], preferred_element_type=jnp.float32
            )
            right = right[:own] + right[own:]
            change = change + right[:, :mode_count] + right[:, mode_count:]
        coeffs = coeffs + TIME_STEP * (forcing - change)
    out_ref[...] = coeffs


def shards(modes, cell_weight, seeds, coeff_table, force_table, visc_table):
    components, mode_count, layers, across = modes.shape
    own = seeds.shape[0]
    lanes = layers * across
    devices = lax.axis_size("space")
    rows = select(seeds, coeff_table, force_table, visc_table)
    chunks, by_offset = gather(modes, cell_weight, rows)
    position = lax.axis_index("space") if by_offset else 0
    me = jnp.full((1, 128), position, jnp.int32)
    vmem = pl.BlockSpec(memory_space=pltpu.VMEM)
    operands = (me, *rows, *(one[0] for one in chunks))
    gathered = 4 * components * devices * lanes * mode_count
    return pl.pallas_call(
        functools.partial(
            step_kernel,
            [one[1:] for one in chunks],
            across,
        ),
        out_shape=jax.ShapeDtypeStruct((own, mode_count), jnp.float32),
        in_specs=[vmem] * len(operands),
        out_specs=vmem,
        scratch_shapes=[
            pltpu.VMEM((components, devices * lanes, 2 * mode_count), jnp.bfloat16),
            pltpu.VMEM((devices, lanes), jnp.float32),
        ],
        compiler_params=pltpu.CompilerParams(vmem_limit_bytes=2 * gathered + 8 * 1024 * 1024),
        name="steps",
    )(*operands)


def solution(mesh):
    placed = (
        P("groups", None, "space", None),
        P("space", "groups"),
        P(("groups", "space")),
        P(),
        P(),
        P(),
    )
    return jax.shard_map(
        shards, mesh=mesh, in_specs=placed, out_specs=P(("groups", "space"), None), check_vma=False
    )
```

time: 32.4 us -> 26.4 us (0.81)
  Pallas kernels: 7.68 us -> 4.03 us
  waiting for transfers between devices: 8.68 us -> 7.53 us
  local copies, waits for them, and re-layouts: 2.34 us -> 1.6 us
  starting transfers between devices: 13.4 us -> 13 us
    pallas_call x2 -> x4, Pallas kernels: 7.68 us -> 4.03 us  [the longest x1 3.32 us: shards(): pl.pallas_call(functools.partial(step_kernel, [one[1:] for one in chunks]...]
    ppermute x15 -> x16, waiting for transfers between devices: 8.68 us -> 7.53 us  [exchange(): array = lax.ppermute(array, 'space', pairs)]
    unnamed x31 -> x12, local copies, waits for them, and re-layouts: 2.34 us -> 1.6 us
    ppermute x15 -> x16, starting transfers between devices: 13.4 us -> 13 us  [exchange(): array = lax.ppermute(array, 'space', pairs)]
  transfers between devices with their start and end apart: 15 -> 16, of which waited for: 5 -> 7; matrix products, arithmetic and copies ran while one was open for 0% -> 0% of each run, Pallas kernels for 0% -> 3%
where the time goes in v2:
time: 26.4 us; the launch traced here: 26.3 us
  starting transfers between devices  13 us (49%)
  waiting for transfers between devices  7.53 us (29%)
  Pallas kernels  4.03 us (15%)
  local copies, waits for them, and re-layouts  1.6 us (6%)
    ppermute x16, starting transfers between devices, exchange(): array = lax.ppermute(array, 'space', pairs)  13 us
    ppermute x16, waiting for transfers between devices, exchange(): array = lax.ppermute(array, 'space', pairs)  7.53 us
    pallas_call x1, Pallas kernels, shards(): pl.pallas_call(functools.partial(step_kernel, [one[1:] for one in chunks]...  3.32 us
    unnamed x12, local copies, waits for them, and re-layouts  1.6 us
    pallas_call x1, Pallas kernels, select(): pl.pallas_call(select_kernel, out_shape=(rows, rows, rows), in_specs=[sme...  0.57 us
  transfers between devices with their start and end apart: 16, of which 7 were waited for; matrix products, arithmetic and copies ran while one was open for 0% of the time, Pallas kernels for 3%

profile of v2, /device:TPU:0, one launch (start us, length us, event | category | flops | bytes accessed | tf_op | source)
XLA Modules:
  0.0 26.3 jit_solution(7997145283738012508)
XLA Ops:
  0.0 0.0 copy-start.3
  0.0 0.0 copy-start.5
  0.0 0.0 copy-start
  0.0 0.0 copy-start.1
  0.0 4.1 %collective-permute-start.3 = (f32[256,128]{1,0:T(8,128)}, f32[256,128]{1,0:T(8,128)S(1)}, u32[]{:S(2)}, u32[]{:S(2)}) collective-permute-start(f32[256,128]{1,0:T(8,128)} %bitcast.3), channel_id=1, source_target_pairs={{0,8},{1,9},{2,10},{3,11},{4,12},{5,13},{6,14},{7,15},{8,0},{9,1},... | collective-permute-start | bytes 393224 | tf_op jit(solution)/shard_map/ppermute | solution.py:43
  4.1 0.1 collective-permute-start.4
  4.2 0.0 copy-start.2
  4.2 0.9 %copy-done.2 = f32[2,128,2,64]{1,3,2,0:T(8,128)S(1)} copy-done((f32[2,128,2,64]{1,3,2,0:T(8,128)S(1)}, f32[2,128,2,64]{1,3,2,0:T(8,128)}, u32[]{:S(2)}) %copy-start.2) | copy-done | bytes 131096
  5.1 0.0 copy-start.4
  5.1 0.7 %copy-done.4 = f32[2,64]{1,0:T(2,128)S(1)} copy-done((f32[2,64]{1,0:T(2,128)S(1)}, f32[2,64]{1,0:T(2,128)}, u32[]{:S(2)}) %copy-start.4) | copy-done | bytes 536
  5.8 0.1 pack.2.refs_0_
  5.9 1.8 %collective-permute-start = (f32[264,128]{1,0:T(8,128)S(1)}, f32[264,128]{1,0:T(8,128)S(1)}, u32[]{:S(2)}, u32[]{:S(2)}) collective-permute-start(f32[264,128]{1,0:T(8,128)S(1)} %pack.2.refs_0_), channel_id=1, source_target_pairs={{0,4},{1,3},{2,6},{3,1},{4,0},{5,7},{6,2},{7,5},{8,12},{9,11},{10,... | collective-permute-start | bytes 405512 | tf_op jit(solution)/shard_map/ppermute | solution.py:43
  7.7 1.5 %collective-permute-start.1 = (f32[264,128]{1,0:T(8,128)S(1)}, f32[264,128]{1,0:T(8,128)S(1)}, u32[]{:S(2)}, u32[]{:S(2)}) collective-permute-start(f32[264,128]{1,0:T(8,128)S(1)} %pack.2.refs_0_), channel_id=1, source_target_pairs={{0,2},{1,5},{2,0},{3,7},{4,6},{5,1},{6,4},{7,3},{8,10},{9,13},{10,... | collective-permute-start | bytes 405512 | tf_op jit(solution)/shard_map/ppermute | solution.py:43
  9.2 0.0 collective-permute-start.8
  9.2 0.0 copy-done.3
  9.2 0.0 copy-done.5
  9.2 0.0 copy-done
  9.2 0.0 copy-done.1
  9.2 0.6 %select.1 = (f32[8,128]{1,0:T(8,128)S(1)}, f32[8,128]{1,0:T(8,128)S(1)}, f32[8,128]{1,0:T(8,128)S(1)}) custom-call(s32[8]{0:T(128)S(1)} %copy-done.5, f32[256]{0:T(256)S(1)} %copy-done.3, f32[256,128]{1,0:T(8,128)S(1)} %copy-done, f32[256,128]{1,0:T(8,128)S(1)} %copy-done.1), custom_call_target="tpu_custom_call" | custom-call | tf_op jit(solution)/shard_map/select/pallas_call | solution.py:98
  9.8 1.0 %collective-permute-done.3.modes_ref = f32[256,128]{1,0:T(8,128)S(1)} collective-permute-done((f32[256,128]{1,0:T(8,128)}, f32[256,128]{1,0:T(8,128)S(1)}, u32[]{:S(2)}, u32[]{:S(2)}) %collective-permute-start.3) | collective-permute-done | bytes 131104 | tf_op jit(solution)/shard_map/ppermute | solution.py:43
  10.8 0.1 collective-permute-done.4.weight_ref
  10.8 0.1 pack.3.refs_4_
  10.9 0.7 %collective-permute-start.5 = (f32[264,128]{1,0:T(8,128)S(1)}, f32[264,128]{1,0:T(8,128)S(1)}, u32[]{:S(2)}, u32[]{:S(2)}) collective-permute-start(f32[264,128]{1,0:T(8,128)S(1)} %pack.3.refs_4_), channel_id=1, source_target_pairs={{0,4},{1,3},{2,6},{3,1},{4,0},{5,7},{6,2},{7,5},{8,12},{9,11},{10,... | collective-permute-start | bytes 405512 | tf_op jit(solution)/shard_map/ppermute | solution.py:43
  11.6 1.5 %collective-permute-start.6 = (f32[264,128]{1,0:T(8,128)S(1)}, f32[264,128]{1,0:T(8,128)S(1)}, u32[]{:S(2)}, u32[]{:S(2)}) collective-permute-start(f32[264,128]{1,0:T(8,128)S(1)} %pack.3.refs_4_), channel_id=1, source_target_pairs={{0,2},{1,5},{2,0},{3,7},{4,6},{5,1},{6,4},{7,3},{8,10},{9,13},{10,... | collective-permute-start | bytes 405512 | tf_op jit(solution)/shard_map/ppermute | solution.py:43
  13.1 0.4 %collective-permute-done.refs_1_ = f32[264,128]{1,0:T(8,128)S(1)} collective-permute-done((f32[264,128]{1,0:T(8,128)S(1)}, f32[264,128]{1,0:T(8,128)S(1)}, u32[]{:S(2)}, u32[]{:S(2)}) %collective-permute-start) | collective-permute-done | bytes 135200 | tf_op jit(solution)/shard_map/ppermute | solution.py:43
  13.6 0.0 collective-permute-start.12
  13.6 0.0 collective-permute-done.1.refs_2_
  13.6 1.0 %collective-permute-start.2 = (f32[264,128]{1,0:T(8,128)S(1)}, f32[264,128]{1,0:T(8,128)S(1)}, u32[]{:S(2)}, u32[]{:S(2)}) collective-permute-start(f32[264,128]{1,0:T(8,128)S(1)} %collective-permute-done.refs_1_), channel_id=1, source_target_pairs={{0,2},{1,5},{2,0},{3,7},{4,6},{5,1},{6,4},{7,3},{8,10},{9,13},{10,... | collective-permute-start | bytes 405512 | tf_op jit(solution)/shard_map/ppermute | solution.py:43
  14.5 0.0 collective-permute-done.8.refs_8_
  14.5 0.2 collective-permute-start.9
  14.7 1.9 %collective-permute-done.5.refs_5_ = f32[264,128]{1,0:T(8,128)S(1)} collective-permute-done((f32[264,128]{1,0:T(8,128)S(1)}, f32[264,128]{1,0:T(8,128)S(1)}, u32[]{:S(2)}, u32[]{:S(2)}) %collective-permute-start.5) | collective-permute-done | bytes 135200 | tf_op jit(solution)/shard_map/ppermute | solution.py:43
  16.6 1.1 %collective-permute-start.7 = (f32[264,128]{1,0:T(8,128)S(1)}, f32[264,128]{1,0:T(8,128)S(1)}, u32[]{:S(2)}, u32[]{:S(2)}) collective-permute-start(f32[264,128]{1,0:T(8,128)S(1)} %collective-permute-done.5.refs_5_), channel_id=1, source_target_pairs={{0,2},{1,5},{2,0},{3,7},{4,6},{5,1},{6,4},{7,3},{8,10},{9,13},{10,... | collective-permute-start | bytes 405512 | tf_op jit(solution)/shard_map/ppermute | solution.py:43
  17.7 0.0 collective-permute-done.6.refs_6_
  17.7 0.0 collective-permute-start.10
  17.7 0.0 collective-permute-done.12.refs_12_
  17.7 0.5 %collective-permute-start.13 = (f32[264,128]{1,0:T(8,128)S(1)}, f32[264,128]{1,0:T(8,128)S(1)}, u32[]{:S(2)}, u32[]{:S(2)}) collective-permute-start(f32[264,128]{1,0:T(8,128)S(1)} %collective-permute-done.5.refs_5_), channel_id=1, source_target_pairs={{0,1},{1,0},{2,3},{3,2},{4,5},{5,4},{6,7},{7,6},{8,9},{9,8},{10,11... | collective-permute-start | bytes 405512 | tf_op jit(solution)/shard_map/ppermute | solution.py:43
  18.2 0.3 %collective-permute-done.2.refs_3_ = f32[264,128]{1,0:T(8,128)S(1)} collective-permute-done((f32[264,128]{1,0:T(8,128)S(1)}, f32[264,128]{1,0:T(8,128)S(1)}, u32[]{:S(2)}, u32[]{:S(2)}) %collective-permute-start.2) | collective-permute-done | bytes 135200 | tf_op jit(solution)/shard_map/ppermute | solution.py:43
  18.6 0.0 collective-permute-start.14
  18.6 0.0 collective-permute-done.9.refs_9_
  18.6 0.5 %collective-permute-start.11 = (f32[264,128]{1,0:T(8,128)S(1)}, f32[264,128]{1,0:T(8,128)S(1)}, u32[]{:S(2)}, u32[]{:S(2)}) collective-permute-start(f32[264,128]{1,0:T(8,128)S(1)} %collective-permute-done.2.refs_3_), channel_id=1, source_target_pairs={{0,1},{1,0},{2,3},{3,2},{4,5},{5,4},{6,7},{7,6},{8,9},{9,8},{10,11... | collective-permute-start | bytes 405512 | tf_op jit(solution)/shard_map/ppermute | solution.py:43
  19.1 2.5 %collective-permute-done.7.refs_7_ = f32[264,128]{1,0:T(8,128)S(1)} collective-permute-done((f32[264,128]{1,0:T(8,128)S(1)}, f32[264,128]{1,0:T(8,128)S(1)}, u32[]{:S(2)}, u32[]{:S(2)}) %collective-permute-start.7) | collective-permute-done | bytes 135200 | tf_op jit(solution)/shard_map/ppermute | solution.py:43
  21.6 0.0 collective-permute-start.15
  21.6 0.0 collective-permute-done.10.refs_10_
  21.6 0.0 collective-permute-done.13.refs_13_
  21.6 0.0 collective-permute-done.14.refs_14_
  21.6 0.0 collective-permute-done.11.refs_11_
  21.6 1.3 %collective-permute-done.15.refs_15_ = f32[264,128]{1,0:T(8,128)S(1)} collective-permute-done((f32[264,128]{1,0:T(8,128)S(1)}, f32[264,128]{1,0:T(8,128)S(1)}, u32[]{:S(2)}, u32[]{:S(2)}) %collective-permute-start.15) | collective-permute-done | bytes 135200 | tf_op jit(solution)/shard_map/ppermute | solution.py:43
  23.0 3.3 %steps.1 = f32[8,128]{1,0:T(8,128)} custom-call(s32[1,128]{1,0:T(1,128)S(1)} %broadcast_in_dim.3.me_ref, f32[8,128]{1,0:T(8,128)S(1)} %get-tuple-element.9.coeff_ref, f32[8,128]{1,0:T(8,128)S(1)} %get-tuple-element.10.force_ref, f32[8,128]{1,0:T(8,128)S(1)} %get-tuple-element.11.visc_ref, f32[264,128]{1,0:T(8,128)S(1)} %pack.2.refs_0_, ...), custom_call_target="tpu_custom_call" | custom-call | tf_op jit(solution)/shard_map/steps/pallas_call | solution.py:212
  (1 shorter events, 0.0 us)
Async XLA Ops:
  0.0 9.2 %copy-start.3 = (f32[256]{0:T(256)S(1)}, f32[256]{0:T(256)}, u32[]{:S(2)}) copy-start(f32[256]{0:T(256)} %visc_table_ref.1) | copy-start | bytes 3076
  0.0 9.2 %copy-start.5 = (s32[8]{0:T(128)S(1)}, s32[8]{0:T(128)}, u32[]{:S(2)}) copy-start(s32[8]{0:T(128)} %seeds_ref.1) | copy-start | bytes 100
  0.0 9.2 %copy-start = (f32[256,128]{1,0:T(8,128)S(1)}, f32[256,128]{1,0:T(8,128)}, u32[]{:S(2)}) copy-start(f32[256,128]{1,0:T(8,128)} %coeff_table_ref.1) | copy-start | bytes 393220
  0.0 9.2 %copy-start.1 = (f32[256,128]{1,0:T(8,128)S(1)}, f32[256,128]{1,0:T(8,128)}, u32[]{:S(2)}) copy-start(f32[256,128]{1,0:T(8,128)} %force_table_ref.1) | copy-start | bytes 393220
  0.0 10.7 %collective-permute-start.3 = (f32[256,128]{1,0:T(8,128)}, f32[256,128]{1,0:T(8,128)S(1)}, u32[]{:S(2)}, u32[]{:S(2)}) collective-permute-start(f32[256,128]{1,0:T(8,128)} %bitcast.3), channel_id=1, source_target_pairs={{0,8},{1,9},{2,10},{3,11},{4,12},{5,13},{6,14},{7,15},{8,0},{9,1},... | collective-permute-start | bytes 393224 | tf_op jit(solution)/shard_map/ppermute | solution.py:43
  4.1 6.7 %collective-permute-start.4 = (f32[2,64]{1,0:T(2,128)}, f32[2,64]{1,0:T(2,128)S(1)}, u32[]{:S(2)}, u32[]{:S(2)}) collective-permute-start(f32[2,64]{1,0:T(2,128)} %weight_ref.1), channel_id=1, source_target_pairs={{0,8},{1,9},{2,10},{3,11},{4,12},{5,13},{6,14},{7,15},{8,0},{9,1},... | collective-permute-start | bytes 1544 | tf_op jit(solution)/shard_map/ppermute | solution.py:43
  4.2 0.9 %copy-start.2 = (f32[2,128,2,64]{1,3,2,0:T(8,128)S(1)}, f32[2,128,2,64]{1,3,2,0:T(8,128)}, u32[]{:S(2)}) copy-start(f32[2,128,2,64]{1,3,2,0:T(8,128)} %param.6) | copy-start | bytes 393220
  5.1 0.7 %copy-start.4 = (f32[2,64]{1,0:T(2,128)S(1)}, f32[2,64]{1,0:T(2,128)}, u32[]{:S(2)}) copy-start(f32[2,64]{1,0:T(2,128)} %weight_ref.1) | copy-start | bytes 1540
  5.9 7.7 %collective-permute-start = (f32[264,128]{1,0:T(8,128)S(1)}, f32[264,128]{1,0:T(8,128)S(1)}, u32[]{:S(2)}, u32[]{:S(2)}) collective-permute-start(f32[264,128]{1,0:T(8,128)S(1)} %pack.2.refs_0_), channel_id=1, source_target_pairs={{0,4},{1,3},{2,6},{3,1},{4,0},{5,7},{6,2},{7,5},{8,12},{9,11},{10,... | collective-permute-start | bytes 405512 | tf_op jit(solution)/shard_map/ppermute | solution.py:43
  7.7 5.9 %collective-permute-start.1 = (f32[264,128]{1,0:T(8,128)S(1)}, f32[264,128]{1,0:T(8,128)S(1)}, u32[]{:S(2)}, u32[]{:S(2)}) collective-permute-start(f32[264,128]{1,0:T(8,128)S(1)} %pack.2.refs_0_), channel_id=1, source_target_pairs={{0,2},{1,5},{2,0},{3,7},{4,6},{5,1},{6,4},{7,3},{8,10},{9,13},{10,... | collective-permute-start | bytes 405512 | tf_op jit(solution)/shard_map/ppermute | solution.py:43
  9.2 5.3 %collective-permute-start.8 = (f32[264,128]{1,0:T(8,128)S(1)}, f32[264,128]{1,0:T(8,128)S(1)}, u32[]{:S(2)}, u32[]{:S(2)}) collective-permute-start(f32[264,128]{1,0:T(8,128)S(1)} %pack.2.refs_0_), channel_id=1, source_target_pairs={{0,1},{1,0},{2,3},{3,2},{4,5},{5,4},{6,7},{7,6},{8,9},{9,8},{10,11... | collective-permute-start | bytes 405512 | tf_op jit(solution)/shard_map/ppermute | solution.py:43
  10.9 5.7 %collective-permute-start.5 = (f32[264,128]{1,0:T(8,128)S(1)}, f32[264,128]{1,0:T(8,128)S(1)}, u32[]{:S(2)}, u32[]{:S(2)}) collective-permute-start(f32[264,128]{1,0:T(8,128)S(1)} %pack.3.refs_4_), channel_id=1, source_target_pairs={{0,4},{1,3},{2,6},{3,1},{4,0},{5,7},{6,2},{7,5},{8,12},{9,11},{10,... | collective-permute-start | bytes 405512 | tf_op jit(solution)/shard_map/ppermute | solution.py:43
  11.6 6.1 %collective-permute-start.6 = (f32[264,128]{1,0:T(8,128)S(1)}, f32[264,128]{1,0:T(8,128)S(1)}, u32[]{:S(2)}, u32[]{:S(2)}) collective-permute-start(f32[264,128]{1,0:T(8,128)S(1)} %pack.3.refs_4_), channel_id=1, source_target_pairs={{0,2},{1,5},{2,0},{3,7},{4,6},{5,1},{6,4},{7,3},{8,10},{9,13},{10,... | collective-permute-start | bytes 405512 | tf_op jit(solution)/shard_map/ppermute | solution.py:43
  13.6 4.2 %collective-permute-start.12 = (f32[264,128]{1,0:T(8,128)S(1)}, f32[264,128]{1,0:T(8,128)S(1)}, u32[]{:S(2)}, u32[]{:S(2)}) collective-permute-start(f32[264,128]{1,0:T(8,128)S(1)} %pack.3.refs_4_), channel_id=1, source_target_pairs={{0,1},{1,0},{2,3},{3,2},{4,5},{5,4},{6,7},{7,6},{8,9},{9,8},{10,11... | collective-permute-start | bytes 405512 | tf_op jit(solution)/shard_map/ppermute | solution.py:43
  13.6 5.0 %collective-permute-start.2 = (f32[264,128]{1,0:T(8,128)S(1)}, f32[264,128]{1,0:T(8,128)S(1)}, u32[]{:S(2)}, u32[]{:S(2)}) collective-permute-start(f32[264,128]{1,0:T(8,128)S(1)} %collective-permute-done.refs_1_), channel_id=1, source_target_pairs={{0,2},{1,5},{2,0},{3,7},{4,6},{5,1},{6,4},{7,3},{8,10},{9,13},{10,... | collective-permute-start | bytes 405512 | tf_op jit(solution)/shard_map/ppermute | solution.py:43
  14.5 4.1 %collective-permute-start.9 = (f32[264,128]{1,0:T(8,128)S(1)}, f32[264,128]{1,0:T(8,128)S(1)}, u32[]{:S(2)}, u32[]{:S(2)}) collective-permute-start(f32[264,128]{1,0:T(8,128)S(1)} %collective-permute-done.refs_1_), channel_id=1, source_target_pairs={{0,1},{1,0},{2,3},{3,2},{4,5},{5,4},{6,7},{7,6},{8,9},{9,8},{10,11... | collective-permute-start | bytes 405512 | tf_op jit(solution)/shard_map/ppermute | solution.py:43
  16.6 5.0 %collective-permute-start.7 = (f32[264,128]{1,0:T(8,128)S(1)}, f32[264,128]{1,0:T(8,128)S(1)}, u32[]{:S(2)}, u32[]{:S(2)}) collective-permute-start(f32[264,128]{1,0:T(8,128)S(1)} %collective-permute-done.5.refs_5_), channel_id=1, source_target_pairs={{0,2},{1,5},{2,0},{3,7},{4,6},{5,1},{6,4},{7,3},{8,10},{9,13},{10,... | collective-permute-start | bytes 405512 | tf_op jit(solution)/shard_map/ppermute | solution.py:43
  17.7 3.9 %collective-permute-start.10 = (f32[264,128]{1,0:T(8,128)S(1)}, f32[264,128]{1,0:T(8,128)S(1)}, u32[]{:S(2)}, u32[]{:S(2)}) collective-permute-start(f32[264,128]{1,0:T(8,128)S(1)} %collective-permute-done.1.refs_2_), channel_id=1, source_target_pairs={{0,1},{1,0},{2,3},{3,2},{4,5},{5,4},{6,7},{7,6},{8,9},{9,8},{10,11... | collective-permute-start | bytes 405512 | tf_op jit(solution)/shard_map/ppermute | solution.py:43
  17.7 3.9 %collective-permute-start.13 = (f32[264,128]{1,0:T(8,128)S(1)}, f32[264,128]{1,0:T(8,128)S(1)}, u32[]{:S(2)}, u32[]{:S(2)}) collective-permute-start(f32[264,128]{1,0:T(8,128)S(1)} %collective-permute-done.5.refs_5_), channel_id=1, source_target_pairs={{0,1},{1,0},{2,3},{3,2},{4,5},{5,4},{6,7},{7,6},{8,9},{9,8},{10,11... | collective-permute-start | bytes 405512 | tf_op jit(solution)/shard_map/ppermute | solution.py:43
  18.6 3.0 %collective-permute-start.14 = (f32[264,128]{1,0:T(8,128)S(1)}, f32[264,128]{1,0:T(8,128)S(1)}, u32[]{:S(2)}, u32[]{:S(2)}) collective-permute-start(f32[264,128]{1,0:T(8,128)S(1)} %collective-permute-done.6.refs_6_), channel_id=1, source_target_pairs={{0,1},{1,0},{2,3},{3,2},{4,5},{5,4},{6,7},{7,6},{8,9},{9,8},{10,11... | collective-permute-start | bytes 405512 | tf_op jit(solution)/shard_map/ppermute | solution.py:43
  18.6 3.0 %collective-permute-start.11 = (f32[264,128]{1,0:T(8,128)S(1)}, f32[264,128]{1,0:T(8,128)S(1)}, u32[]{:S(2)}, u32[]{:S(2)}) collective-permute-start(f32[264,128]{1,0:T(8,128)S(1)} %collective-permute-done.2.refs_3_), channel_id=1, source_target_pairs={{0,1},{1,0},{2,3},{3,2},{4,5},{5,4},{6,7},{7,6},{8,9},{9,8},{10,11... | collective-permute-start | bytes 405512 | tf_op jit(solution)/shard_map/ppermute | solution.py:43
  21.6 1.4 %collective-permute-start.15 = (f32[264,128]{1,0:T(8,128)S(1)}, f32[264,128]{1,0:T(8,128)S(1)}, u32[]{:S(2)}, u32[]{:S(2)}) collective-permute-start(f32[264,128]{1,0:T(8,128)S(1)} %collective-permute-done.7.refs_7_), channel_id=1, source_target_pairs={{0,1},{1,0},{2,3},{3,2},{4,5},{5,4},{6,7},{7,6},{8,9},{9,8},{10,11... | collective-permute-start | bytes 405512 | tf_op jit(solution)/shard_map/ppermute | solution.py:43

commit v3 on v2

v3 whole, which is shorter than its diff:
```python
import functools

import jax
import jax.numpy as jnp
from jax import lax
from jax.experimental import pallas as pl
from jax.experimental.pallas import tpu as pltpu
from jax.sharding import PartitionSpec as P

STEPS = 2


TIME_STEP = 0.5
SPARE_ROWS = 8
SLOPE_SCALE = 12.0
COMPONENTS = 2


def lay_kernel(weight_ref, row_ref):
    layers, across = weight_ref.shape
    for layer in range(layers):
        row_ref[:, layer * across : (layer + 1) * across] = jnp.broadcast_to(
            weight_ref[layer : layer + 1, :], (SPARE_ROWS, across)
        )


def lay(cell_weight):
    layers, across = cell_weight.shape
    return pl.pallas_call(
        lay_kernel,
        out_shape=jax.ShapeDtypeStruct((SPARE_ROWS, layers * across), jnp.float32),
        in_specs=[pl.BlockSpec(memory_space=pltpu.VMEM)],
        out_specs=pl.BlockSpec(memory_space=pltpu.VMEM),
        compiler_params=pltpu.CompilerParams(vmem_limit_bytes=1024 * 1024),
        name="lay",
    )(cell_weight)


def pack_kernel(modes_ref, row_ref, chunk_ref):
    rows = modes_ref.shape[0]
    chunk_ref[0:rows, :] = modes_ref[...]
    chunk_ref[rows : rows + SPARE_ROWS, :] = row_ref[...]


def pack(modes, weight_rows):
    rows, mode_count = modes.shape
    return pl.pallas_call(
        pack_kernel,
        out_shape=jax.ShapeDtypeStruct((rows + SPARE_ROWS, mode_count), jnp.float32),
        in_specs=[pl.BlockSpec(memory_space=pltpu.VMEM)] * 2,
        out_specs=pl.BlockSpec(memory_space=pltpu.VMEM),
        compiler_params=pltpu.CompilerParams(vmem_limit_bytes=2 * 1024 * 1024),
        name="pack",
    )(modes, weight_rows)


def exchange(held, even_mask, odd_mask):
    array, even, odd = held
    devices = lax.axis_size("space")
    pairs = [(i, i ^ (odd_mask if i & 1 else even_mask)) for i in range(devices)]
    array = lax.ppermute(array, "space", pairs)
    if even_mask & 1:
        even, odd = odd, even
    return array, even ^ even_mask, odd ^ odd_mask


def gather(modes, cell_weight, first_needed):
    components, mode_count, layers, across = modes.shape
    rows = modes.transpose(0, 2, 3, 1).reshape(components * layers * across, mode_count)
    devices = lax.axis_size("space")
    if devices < 16 or devices & (devices - 1):
        everyone = lax.all_gather(pack(rows, lay(cell_weight)), "space")
        return [[(everyone[j], j, j) for j in range(devices)]], False
    near = devices // 4
    side = near // 2
    far = devices // 2 + near
    far_rows, even, odd = exchange((rows, 0, 0), far, far)
    far_weight = exchange((cell_weight, 0, 0), far, far)[0]
    own = (pack(rows, lay(cell_weight)), 0, 0)
    far_rows, *_ = lax.optimization_barrier((far_rows, *first_needed))
    opposite = (pack(far_rows, lay(far_weight)), even, odd)
    held = []
    for start in (own, opposite):
        first = exchange(start, near, side)
        second = exchange(start, side, near)
        held += [start, first, second, exchange(first, side, near)]
    order = [0,0,0,1,0,0,0,2]
    mask = side // 2
    while mask:
        held += [exchange(one, mask, mask) for one in held]
        order += order
        mask //= 2
    groups = [[one for one, at in zip(held, order) if at == wanted] for wanted in range(3)]
    return groups, True


def halves(array):
    high = array.astype(jnp.bfloat16)
    low = (array - high.astype(jnp.float32)).astype(jnp.bfloat16)
    return high, low


def select_kernel(seeds_ref, visc_table_ref, coeff_table_ref, force_table_ref, coeff_ref, force_ref, visc_ref):
    own, mode_count = coeff_ref.shape
    row_id = lax.broadcasted_iota(jnp.int32, (own, mode_count), 0)
    visc = jnp.zeros((own, mode_count), jnp.float32)
    for n in range(own):
        seed = seeds_ref[n]
        coeff_ref[n : n + 1, :] = coeff_table_ref[pl.ds(seed, 1), :]
        force_ref[n : n + 1, :] = force_table_ref[pl.ds(seed, 1), :]
        visc = jnp.where(row_id == n, visc_table_ref[seed], visc)
    visc_ref[...] = visc


def select(seeds, coeff_table, force_table, visc_table):
    smem = pl.BlockSpec(memory_space=pltpu.SMEM)
    vmem = pl.BlockSpec(memory_space=pltpu.VMEM)
    rows = jax.ShapeDtypeStruct((seeds.shape[0], coeff_table.shape[1]), jnp.float32)
    return pl.pallas_call(
        select_kernel,
        out_shape=(rows, rows, rows),
        in_specs=[smem, smem, vmem, vmem],
        out_specs=(vmem, vmem, vmem),
        compiler_params=pltpu.CompilerParams(vmem_limit_bytes=2 * 1024 * 1024),
        name="select",
    )(seeds, visc_table, coeff_table, force_table)


def placing(me, offsets):
    odd = me % 2 == 1
    return [jnp.bitwise_xor(me, jnp.where(odd, odd_offset, even_offset)) for even_offset, odd_offset in offsets]


def take_in(coeffs, places, chunk_refs, flow_ref, weight_ref, mode_refs):
    own, mode_count = coeffs.shape
    components, devices, _, lanes = flow_ref.shape
    total_cells = devices * lanes
    high, low = halves(coeffs)
    left = jnp.concatenate([jnp.concatenate([high, high], axis=1), jnp.concatenate([low, low], axis=1)], axis=0)
    for place, chunk_ref in zip(places, chunk_refs):
        rows = pl.ds(pl.multiple_of(place * lanes, lanes), lanes)
        for a in range(components):
            split = jnp.concatenate(halves(chunk_ref[a * lanes : (a + 1) * lanes, :]), axis=1)
            mode_refs[a][rows, :] = split
            both = lax.dot_general(left, split, (((1,), (1,)), ((), ())), preferred_element_type=jnp.float32)
            flow_ref[a, place] = both[:own] + both[own:]
        last = components * lanes
        weight_ref[pl.ds(place, 1), :] = chunk_ref[last : last + 1, :] / (SLOPE_SCALE * total_cells)


def take_in_kernel(offsets, me_ref, coeff_ref, *refs):
    chunk_refs = refs[: len(offsets)]
    kept = refs[-2 - COMPONENTS :]
    take_in(coeff_ref[...], placing(me_ref[0, 0], offsets), chunk_refs, kept[0], kept[1], kept[2:])


def state_of(components, devices, own, lanes, mode_count):
    return (
        jax.ShapeDtypeStruct((components, devices, own, lanes), jnp.float32),
        jax.ShapeDtypeStruct((devices, lanes), jnp.float32),
        *[jax.ShapeDtypeStruct((devices * lanes, 2 * mode_count), jnp.bfloat16) for _ in range(components)],
    )


def absorb(me, coeffs, group, shapes, state):
    offsets = [one[1:] for one in group]
    vmem = pl.BlockSpec(memory_space=pltpu.VMEM)
    operands = (me, coeffs, *(one[0] for one in group), *state)
    size = sum(operand.size * operand.dtype.itemsize for operand in (*operands, *shapes))
    return pl.pallas_call(
        functools.partial(take_in_kernel, offsets),
        out_shape=shapes,
        in_specs=[vmem] * len(operands),
        out_specs=(vmem,) * len(shapes),
        input_output_aliases={len(operands) - len(state) + i: i for i in range(len(state))},
        compiler_params=pltpu.CompilerParams(vmem_limit_bytes=size + 4 * 1024 * 1024),
        name="absorb",
    )(*operands)


def step_kernel(offsets, across, me_ref, coeff_ref, force_ref, visc_ref, *refs):
    chunk_refs = refs[: len(offsets)]
    out_ref, flow_ref, weight_ref, *mode_refs = refs[-3 - COMPONENTS :]
    own, mode_count = out_ref.shape
    components, devices, _, lanes = flow_ref.shape
    layers = lanes // across
    coeffs = coeff_ref[...]
    forcing = force_ref[...]
    take_in(coeffs, placing(me_ref[0, 0], offsets), chunk_refs, flow_ref, weight_ref, mode_refs)
    visc = visc_ref[...] / SLOPE_SCALE
    lane = lax.broadcasted_iota(jnp.int32, (own, lanes), 1)
    y = lane % across

    def rolled(f, by):
        return pltpu.roll(f, by % lanes, 1) if by % lanes else f

    def slope(m2, m1, p1, p2):
        return 8.0 * (p1 - m1) - (p2 - m2)

    def slope_along(field):
        def ahead(shift):
            whole, part = divmod(shift, layers)
            moved = [field[(p + whole) % devices] for p in range(devices + 1)]
            if part:
                moved = [rolled(f, -part * across) for f in moved[:devices]]
                inside = lane < (layers - part) * across
                moved = [jnp.where(inside, moved[p], moved[(p + 1) % devices]) for p in range(devices)]
            return moved[:devices]

        shifted = [ahead(s) for s in (-2, -1, 1, 2)]
        return [slope(*(s[p] for s in shifted)) for p in range(devices)]

    def slope_across(field):
        def ahead(f, shift):
            if shift > 0:
                wrapped = jnp.where(y < shift, rolled(f, across), f)
            else:
                wrapped = jnp.where(y >= across + shift, rolled(f, -across), f)
            return rolled(wrapped, -shift)

        return [slope(*(ahead(f, s) for s in (-2, -1, 1, 2))) for f in field]

    weight = [weight_ref[p : p + 1, :] for p in range(devices)]

    for repeat in range(STEPS):
        flow = []
        for a in range(components):
            if repeat == 0:
                flow.append([flow_ref[a, p] for p in range(devices)])
                continue
            high, low = halves(coeffs)
            left = jnp.concatenate(
                [jnp.concatenate([high, high], axis=1), jnp.concatenate([low, low], axis=1)], axis=0
            )
            both = lax.dot_general(
                left, mode_refs[a][...], (((1,), (1,)), ((), ())), preferred_element_type=jnp.float32
            )
            both = both[:own] + both[own:]
            flow.append([both[:, p * lanes : (p + 1) * lanes] for p in range(devices)])
        change = jnp.zeros((own, mode_count), jnp.float32)
        for a in range(components):
            x_slope = slope_along(flow[a])
            y_slope = slope_across(flow[a])
            x_flux = [weight[p] * x_slope[p] for p in range(devices)]
            y_flux = [weight[p] * y_slope[p] for p in range(devices)]
            x_spread = slope_along(x_flux)
            y_spread = slope_across(y_flux)
            source = jnp.concatenate(
                [
                    flow[0][p] * x_flux[p] + flow[1][p] * y_flux[p] - visc * (x_spread[p] + y_spread[p])
                    for p in range(devices)
                ],
                axis=1,
            )
            high, low = halves(source)
            right = jnp.dot(
                jnp.concatenate([high, low], axis=0), mode_refs[a][...], preferred_element_type=jnp.float32
            )
            right = right[:own] + right[own:]
            change = change + right[:, :mode_count] + right[:, mode_count:]
        coeffs = coeffs + TIME_STEP * (forcing - change)
    out_ref[...] = coeffs


def shards(modes, cell_weight, seeds, coeff_table, force_table, visc_table):
    components, mode_count, layers, across = modes.shape
    own = seeds.shape[0]
    lanes = layers * across
    devices = lax.axis_size("space")
    rows = select(seeds, coeff_table, force_table, visc_table)
    groups, by_offset = gather(modes, cell_weight, rows)
    me = jnp.full((1, 128), lax.axis_index("space") if by_offset else 0, jnp.int32)
    shapes = state_of(components, devices, own, lanes, mode_count)
    state = ()
    for group in groups[:-1]:
        state = absorb(me, rows[0], group, shapes, state)
    late = groups[-1]
    vmem = pl.BlockSpec(memory_space=pltpu.VMEM)
    operands = (me, *rows, *(one[0] for one in late), *state)
    size = sum(operand.size * operand.dtype.itemsize for operand in (*operands, *shapes))
    out = jax.ShapeDtypeStruct((own, mode_count), jnp.float32)
    out, *_ = pl.pallas_call(
        functools.partial(step_kernel, [one[1:] for one in late], across),
        out_shape=(out, *shapes),
        in_specs=[vmem] * len(operands),
        out_specs=(vmem,) * (1 + len(shapes)),
        input_output_aliases={len(operands) - len(state) + i: 1 + i for i in range(len(state))},
        compiler_params=pltpu.CompilerParams(vmem_limit_bytes=size + 4 * 1024 * 1024),
        name="steps",
    )(*operands)
    return out


def solution(mesh):
    placed = (
        P("groups", None, "space", None),
        P("space", "groups"),
        P(("groups", "space")),
        P(),
        P(),
        P(),
    )
    return jax.shard_map(
        shards, mesh=mesh, in_specs=placed, out_specs=P(("groups", "space"), None), check_vma=False
    )
```

time: 26.4 us -> 25.2 us (0.955)
  local copies, waits for them, and re-layouts: 1.6 us -> 0.92 us
  starting transfers between devices: 13 us -> 12.5 us
    unnamed x12, local copies, waits for them, and re-layouts: 1.6 us -> 0.92 us
    ppermute x16, starting transfers between devices: 13 us -> 12.5 us  [exchange(): array = lax.ppermute(array, 'space', pairs)]
    pallas_call x1 -> x5, Pallas kernels: 3.32 us -> 3.69 us  [the longest x1 2.74 us: shards(): pl.pallas_call(functools.partial(step_kernel, [one[1:] for one in late],...]
  transfers between devices with their start and end apart: 16 -> 16, of which waited for: 7 -> 6; matrix products, arithmetic and copies ran while one was open for 0% -> 0% of each run, Pallas kernels for 3% -> 6%
where the time goes in v3:
time: 25.2 us; the launch traced here: 25.1 us
  starting transfers between devices  12.5 us (50%)
  waiting for transfers between devices  7.27 us (29%)
  Pallas kernels  4.29 us (17%)
  local copies, waits for them, and re-layouts  0.92 us (4%)
    ppermute x16, starting transfers between devices, exchange(): array = lax.ppermute(array, 'space', pairs)  12.5 us
    ppermute x16, waiting for transfers between devices, exchange(): array = lax.ppermute(array, 'space', pairs)  7.27 us
    pallas_call x1, Pallas kernels, shards(): pl.pallas_call(functools.partial(step_kernel, [one[1:] for one in late],...  2.74 us
    unnamed x12, local copies, waits for them, and re-layouts  0.92 us
    pallas_call x2, Pallas kernels, absorb(): pl.pallas_call(functools.partial(take_in_kernel, offsets), out_shape=shap...  0.82 us
    pallas_call x1, Pallas kernels, select(): pl.pallas_call(select_kernel, out_shape=(rows, rows, rows), in_specs=[sme...  0.57 us
  transfers between devices with their start and end apart: 16, of which 6 were waited for; matrix products, arithmetic and copies ran while one was open for 0% of the time, Pallas kernels for 6%

profile of v3, /device:TPU:0, one launch (start us, length us, event | category | flops | bytes accessed | tf_op | source)
XLA Modules:
  0.0 25.1 jit_solution(1141501179207989211)
XLA Ops:
  0.0 0.0 copy-start.4
  0.0 5.0 %collective-permute-start = (f32[256,128]{1,0:T(8,128)}, f32[256,128]{1,0:T(8,128)S(1)}, u32[]{:S(2)}, u32[]{:S(2)}) collective-permute-start(f32[256,128]{1,0:T(8,128)} %bitcast.3), channel_id=1, source_target_pairs={{0,12},{1,13},{2,14},{3,15},{4,8},{5,9},{6,10},{7,11},{8,4},{9,5},... | collective-permute-start | bytes 393224 | tf_op jit(solution)/shard_map/ppermute | solution.py:61
  5.1 0.0 copy-done.4
  5.1 0.7 %collective-permute-start.1 = (f32[2,64]{1,0:T(2,128)S(1)}, f32[2,64]{1,0:T(2,128)S(1)}, u32[]{:S(2)}, u32[]{:S(2)}) collective-permute-start(f32[2,64]{1,0:T(2,128)S(1)} %copy-done.4), channel_id=1, source_target_pairs={{0,12},{1,13},{2,14},{3,15},{4,8},{5,9},{6,10},{7,11},{8,4},{9,5},... | collective-permute-start | bytes 1544 | tf_op jit(solution)/shard_map/ppermute | solution.py:61
  5.7 0.1 lay.3.row_ref
  5.8 0.0 copy-start.2
  5.8 0.9 %copy-done.2 = f32[2,128,2,64]{1,3,2,0:T(8,128)S(1)} copy-done((f32[2,128,2,64]{1,3,2,0:T(8,128)S(1)}, f32[2,128,2,64]{1,3,2,0:T(8,128)}, u32[]{:S(2)}) %copy-start.2) | copy-done | bytes 131096
  6.7 0.0 copy-start
  6.7 0.0 copy-start.1
  6.7 0.0 copy-start.3
  6.7 0.0 copy-start.5
  6.7 0.1 collective-permute-start.5
  6.8 1.6 %collective-permute-start.8 = (f32[264,128]{1,0:T(8,128)S(1)}, f32[264,128]{1,0:T(8,128)S(1)}, u32[]{:S(2)}, u32[]{:S(2)}) collective-permute-start(f32[264,128]{1,0:T(8,128)S(1)} %pack.3.refs_0_), channel_id=1, source_target_pairs={{0,2},{1,5},{2,0},{3,7},{4,6},{5,1},{6,4},{7,3},{8,10},{9,13},{10,... | collective-permute-start | bytes 405512 | tf_op jit(solution)/shard_map/ppermute | solution.py:61
  8.4 0.0 collective-permute-start.10
  8.4 0.0 copy-done
  8.4 0.0 copy-done.1
  8.4 0.0 copy-done.3
  8.4 0.0 copy-done.5
  8.4 0.6 %select.1 = (f32[8,128]{1,0:T(8,128)S(1)}, f32[8,128]{1,0:T(8,128)S(1)}, f32[8,128]{1,0:T(8,128)S(1)}) custom-call(s32[8]{0:T(128)S(1)} %copy-done.5, f32[256]{0:T(256)S(1)} %copy-done.3, f32[256,128]{1,0:T(8,128)S(1)} %copy-done, f32[256,128]{1,0:T(8,128)S(1)} %copy-done.1), custom_call_target="tpu_custom_call" | custom-call | tf_op jit(solution)/shard_map/select/pallas_call | solution.py:119
  9.0 1.4 %collective-permute-done.1.weight_ref = f32[2,64]{1,0:T(2,128)S(1)} collective-permute-done((f32[2,64]{1,0:T(2,128)S(1)}, f32[2,64]{1,0:T(2,128)S(1)}, u32[]{:S(2)}, u32[]{:S(2)}) %collective-permute-start.1) | collective-permute-done | bytes 544 | tf_op jit(solution)/shard_map/ppermute | solution.py:61
  10.4 0.1 lay.2.row_ref
  10.5 0.0 collective-permute-done.modes_ref
  10.5 1.0 %collective-permute-start.2 = (f32[264,128]{1,0:T(8,128)S(1)}, f32[264,128]{1,0:T(8,128)S(1)}, u32[]{:S(2)}, u32[]{:S(2)}) collective-permute-start(f32[264,128]{1,0:T(8,128)S(1)} %pack.2.refs_3_), channel_id=1, source_target_pairs={{0,4},{1,3},{2,6},{3,1},{4,0},{5,7},{6,2},{7,5},{8,12},{9,11},{10,... | collective-permute-start | bytes 405512 | tf_op jit(solution)/shard_map/ppermute | solution.py:61
  11.5 1.5 %collective-permute-start.9 = (f32[264,128]{1,0:T(8,128)S(1)}, f32[264,128]{1,0:T(8,128)S(1)}, u32[]{:S(2)}, u32[]{:S(2)}) collective-permute-start(f32[264,128]{1,0:T(8,128)S(1)} %pack.2.refs_3_), channel_id=1, source_target_pairs={{0,2},{1,5},{2,0},{3,7},{4,6},{5,1},{6,4},{7,3},{8,10},{9,13},{10,... | collective-permute-start | bytes 405512 | tf_op jit(solution)/shard_map/ppermute | solution.py:61
  13.0 0.2 collective-permute-done.5.refs_1_
  13.2 0.0 collective-permute-start.13
  13.2 0.0 collective-permute-done.8.refs_2_
  13.2 0.5 %collective-permute-start.11 = (f32[264,128]{1,0:T(8,128)S(1)}, f32[264,128]{1,0:T(8,128)S(1)}, u32[]{:S(2)}, u32[]{:S(2)}) collective-permute-start(f32[264,128]{1,0:T(8,128)S(1)} %collective-permute-done.5.refs_1_), channel_id=1, source_target_pairs={{0,1},{1,0},{2,3},{3,2},{4,5},{5,4},{6,7},{7,6},{8,9},{9,8},{10,11... | collective-permute-start | bytes 405512 | tf_op jit(solution)/shard_map/ppermute | solution.py:61
  13.7 0.0 collective-permute-done.10.refs_6_
  13.7 0.4 %collective-permute-start.6 = (f32[264,128]{1,0:T(8,128)S(1)}, f32[264,128]{1,0:T(8,128)S(1)}, u32[]{:S(2)}, u32[]{:S(2)}) collective-permute-start(f32[264,128]{1,0:T(8,128)S(1)} %collective-permute-done.5.refs_1_), channel_id=1, source_target_pairs={{0,2},{1,5},{2,0},{3,7},{4,6},{5,1},{6,4},{7,3},{8,10},{9,13},{10,... | collective-permute-start | bytes 405512 | tf_op jit(solution)/shard_map/ppermute | solution.py:61
  14.1 1.8 %collective-permute-done.2.refs_4_ = f32[264,128]{1,0:T(8,128)S(1)} collective-permute-done((f32[264,128]{1,0:T(8,128)S(1)}, f32[264,128]{1,0:T(8,128)S(1)}, u32[]{:S(2)}, u32[]{:S(2)}) %collective-permute-start.2) | collective-permute-done | bytes 135200 | tf_op jit(solution)/shard_map/ppermute | solution.py:61
  16.0 1.1 %collective-permute-start.3 = (f32[264,128]{1,0:T(8,128)S(1)}, f32[264,128]{1,0:T(8,128)S(1)}, u32[]{:S(2)}, u32[]{:S(2)}) collective-permute-start(f32[264,128]{1,0:T(8,128)S(1)} %collective-permute-done.2.refs_4_), channel_id=1, source_target_pairs={{0,2},{1,5},{2,0},{3,7},{4,6},{5,1},{6,4},{7,3},{8,10},{9,13},{10,... | collective-permute-start | bytes 405512 | tf_op jit(solution)/shard_map/ppermute | solution.py:61
  17.1 0.0 collective-permute-done.9.refs_5_
  17.1 0.0 collective-permute-start.12
  17.1 0.0 collective-permute-done.13.refs_9_
  17.1 0.5 %collective-permute-start.14 = (f32[264,128]{1,0:T(8,128)S(1)}, f32[264,128]{1,0:T(8,128)S(1)}, u32[]{:S(2)}, u32[]{:S(2)}) collective-permute-start(f32[264,128]{1,0:T(8,128)S(1)} %collective-permute-done.2.refs_4_), channel_id=1, source_target_pairs={{0,1},{1,0},{2,3},{3,2},{4,5},{5,4},{6,7},{7,6},{8,9},{9,8},{10,11... | collective-permute-start | bytes 405512 | tf_op jit(solution)/shard_map/ppermute | solution.py:61
  17.6 0.0 collective-permute-done.11.refs_7_
  17.6 0.1 collective-permute-start.15
  17.7 1.0 %collective-permute-done.6.refs_0_ = f32[264,128]{1,0:T(8,128)S(1)} collective-permute-done((f32[264,128]{1,0:T(8,128)S(1)}, f32[264,128]{1,0:T(8,128)S(1)}, u32[]{:S(2)}, u32[]{:S(2)}) %collective-permute-start.6) | collective-permute-done | bytes 135200 | tf_op jit(solution)/shard_map/ppermute | solution.py:61
  18.7 0.0 collective-permute-start.7
  18.7 2.3 %collective-permute-done.3.refs_0_ = f32[264,128]{1,0:T(8,128)S(1)} collective-permute-done((f32[264,128]{1,0:T(8,128)S(1)}, f32[264,128]{1,0:T(8,128)S(1)}, u32[]{:S(2)}, u32[]{:S(2)}) %collective-permute-start.3) | collective-permute-done | bytes 135200 | tf_op jit(solution)/shard_map/ppermute | solution.py:61
  21.0 0.0 collective-permute-start.4
  21.0 0.0 collective-permute-done.12.refs_8_
  21.0 0.0 collective-permute-done.14.refs_10_
  21.0 0.0 collective-permute-done.15.refs_11_
  21.0 0.6 %absorb.2 = (f32[2,16,8,128]{3,2,1,0:T(8,128)S(1)}, f32[16,128]{1,0:T(8,128)S(1)}, bf16[2048,256]{1,0:T(8,128)(2,1)S(1)}, bf16[2048,256]{1,0:T(8,128)(2,1)S(1)}) custom-call(s32[1,128]{1,0:T(1,128)S(1)} %broadcast_in_dim.3.me_ref, f32[8,128]{1,0:T(8,128)S(1)} %get-tuple-element.18.coeff_ref, f32[264,128]{1,0:T(8,128)S(1)} %pack.3.refs_0_, ...), custom_call_target="tpu_custom_call" | custom-call | tf_op jit(solution)/shard_map/absorb/pallas_call | solution.py:170
  21.6 0.0 collective-permute-done.7.refs_1_
  21.6 0.2 absorb.3
  21.8 0.5 %collective-permute-done.4.refs_1_ = f32[264,128]{1,0:T(8,128)S(1)} collective-permute-done((f32[264,128]{1,0:T(8,128)S(1)}, f32[264,128]{1,0:T(8,128)S(1)}, u32[]{:S(2)}, u32[]{:S(2)}) %collective-permute-start.4) | collective-permute-done | bytes 135200 | tf_op jit(solution)/shard_map/ppermute | solution.py:61
  22.3 2.7 %steps.1 = (f32[8,128]{1,0:T(8,128)}, f32[2,16,8,128]{3,2,1,0:T(8,128)S(1)}, f32[16,128]{1,0:T(8,128)S(1)}, bf16[2048,256]{1,0:T(8,128)(2,1)S(1)}, bf16[2048,256]{1,0:T(8,128)(2,1)S(1)}) custom-call(s32[1,128]{1,0:T(1,128)S(1)} %broadcast_in_dim.3.me_ref, ...), custom_call_target="tpu_custom_call", output_to_operand_aliasing={{1}: (6, {}), {2}: (7, {}), {3}: (8, {}), {4}: (9, {})} | custom-call | tf_op jit(solution)/shard_map/steps/pallas_call | solution.py:282
  (3 shorter events, 0.0 us)
Async XLA Ops:
  0.0 5.1 %copy-start.4 = (f32[2,64]{1,0:T(2,128)S(1)}, f32[2,64]{1,0:T(2,128)}, u32[]{:S(2)}) copy-start(f32[2,64]{1,0:T(2,128)} %weight_ref.1) | copy-start | bytes 1540
  0.0 10.5 %collective-permute-start = (f32[256,128]{1,0:T(8,128)}, f32[256,128]{1,0:T(8,128)S(1)}, u32[]{:S(2)}, u32[]{:S(2)}) collective-permute-start(f32[256,128]{1,0:T(8,128)} %bitcast.3), channel_id=1, source_target_pairs={{0,12},{1,13},{2,14},{3,15},{4,8},{5,9},{6,10},{7,11},{8,4},{9,5},... | collective-permute-start | bytes 393224 | tf_op jit(solution)/shard_map/ppermute | solution.py:61
  5.1 5.4 %collective-permute-start.1 = (f32[2,64]{1,0:T(2,128)S(1)}, f32[2,64]{1,0:T(2,128)S(1)}, u32[]{:S(2)}, u32[]{:S(2)}) collective-permute-start(f32[2,64]{1,0:T(2,128)S(1)} %copy-done.4), channel_id=1, source_target_pairs={{0,12},{1,13},{2,14},{3,15},{4,8},{5,9},{6,10},{7,11},{8,4},{9,5},... | collective-permute-start | bytes 1544 | tf_op jit(solution)/shard_map/ppermute | solution.py:61
  5.8 0.9 %copy-start.2 = (f32[2,128,2,64]{1,3,2,0:T(8,128)S(1)}, f32[2,128,2,64]{1,3,2,0:T(8,128)}, u32[]{:S(2)}) copy-start(f32[2,128,2,64]{1,3,2,0:T(8,128)} %param.6) | copy-start | bytes 393220
  6.7 1.7 %copy-start = (f32[256,128]{1,0:T(8,128)S(1)}, f32[256,128]{1,0:T(8,128)}, u32[]{:S(2)}) copy-start(f32[256,128]{1,0:T(8,128)} %coeff_table_ref.1) | copy-start | bytes 393220
  6.7 1.7 %copy-start.1 = (f32[256,128]{1,0:T(8,128)S(1)}, f32[256,128]{1,0:T(8,128)}, u32[]{:S(2)}) copy-start(f32[256,128]{1,0:T(8,128)} %force_table_ref.1) | copy-start | bytes 393220
  6.7 1.7 %copy-start.3 = (f32[256]{0:T(256)S(1)}, f32[256]{0:T(256)}, u32[]{:S(2)}) copy-start(f32[256]{0:T(256)} %visc_table_ref.1) | copy-start | bytes 3076
  6.7 1.7 %copy-start.5 = (s32[8]{0:T(128)S(1)}, s32[8]{0:T(128)}, u32[]{:S(2)}) copy-start(s32[8]{0:T(128)} %seeds_ref.1) | copy-start | bytes 100
  6.7 6.5 %collective-permute-start.5 = (f32[264,128]{1,0:T(8,128)S(1)}, f32[264,128]{1,0:T(8,128)S(1)}, u32[]{:S(2)}, u32[]{:S(2)}) collective-permute-start(f32[264,128]{1,0:T(8,128)S(1)} %pack.3.refs_0_), channel_id=1, source_target_pairs={{0,4},{1,3},{2,6},{3,1},{4,0},{5,7},{6,2},{7,5},{8,12},{9,11},{10,... | collective-permute-start | bytes 405512 | tf_op jit(solution)/shard_map/ppermute | solution.py:61
  6.8 6.4 %collective-permute-start.8 = (f32[264,128]{1,0:T(8,128)S(1)}, f32[264,128]{1,0:T(8,128)S(1)}, u32[]{:S(2)}, u32[]{:S(2)}) collective-permute-start(f32[264,128]{1,0:T(8,128)S(1)} %pack.3.refs_0_), channel_id=1, source_target_pairs={{0,2},{1,5},{2,0},{3,7},{4,6},{5,1},{6,4},{7,3},{8,10},{9,13},{10,... | collective-permute-start | bytes 405512 | tf_op jit(solution)/shard_map/ppermute | solution.py:61
  8.4 5.3 %collective-permute-start.10 = (f32[264,128]{1,0:T(8,128)S(1)}, f32[264,128]{1,0:T(8,128)S(1)}, u32[]{:S(2)}, u32[]{:S(2)}) collective-permute-start(f32[264,128]{1,0:T(8,128)S(1)} %pack.3.refs_0_), channel_id=1, source_target_pairs={{0,1},{1,0},{2,3},{3,2},{4,5},{5,4},{6,7},{7,6},{8,9},{9,8},{10,11... | collective-permute-start | bytes 405512 | tf_op jit(solution)/shard_map/ppermute | solution.py:61
  10.5 5.5 %collective-permute-start.2 = (f32[264,128]{1,0:T(8,128)S(1)}, f32[264,128]{1,0:T(8,128)S(1)}, u32[]{:S(2)}, u32[]{:S(2)}) collective-permute-start(f32[264,128]{1,0:T(8,128)S(1)} %pack.2.refs_3_), channel_id=1, source_target_pairs={{0,4},{1,3},{2,6},{3,1},{4,0},{5,7},{6,2},{7,5},{8,12},{9,11},{10,... | collective-permute-start | bytes 405512 | tf_op jit(solution)/shard_map/ppermute | solution.py:61
  11.5 5.6 %collective-permute-start.9 = (f32[264,128]{1,0:T(8,128)S(1)}, f32[264,128]{1,0:T(8,128)S(1)}, u32[]{:S(2)}, u32[]{:S(2)}) collective-permute-start(f32[264,128]{1,0:T(8,128)S(1)} %pack.2.refs_3_), channel_id=1, source_target_pairs={{0,2},{1,5},{2,0},{3,7},{4,6},{5,1},{6,4},{7,3},{8,10},{9,13},{10,... | collective-permute-start | bytes 405512 | tf_op jit(solution)/shard_map/ppermute | solution.py:61
  13.2 3.9 %collective-permute-start.13 = (f32[264,128]{1,0:T(8,128)S(1)}, f32[264,128]{1,0:T(8,128)S(1)}, u32[]{:S(2)}, u32[]{:S(2)}) collective-permute-start(f32[264,128]{1,0:T(8,128)S(1)} %pack.2.refs_3_), channel_id=1, source_target_pairs={{0,1},{1,0},{2,3},{3,2},{4,5},{5,4},{6,7},{7,6},{8,9},{9,8},{10,11... | collective-permute-start | bytes 405512 | tf_op jit(solution)/shard_map/ppermute | solution.py:61
  13.2 4.4 %collective-permute-start.11 = (f32[264,128]{1,0:T(8,128)S(1)}, f32[264,128]{1,0:T(8,128)S(1)}, u32[]{:S(2)}, u32[]{:S(2)}) collective-permute-start(f32[264,128]{1,0:T(8,128)S(1)} %collective-permute-done.5.refs_1_), channel_id=1, source_target_pairs={{0,1},{1,0},{2,3},{3,2},{4,5},{5,4},{6,7},{7,6},{8,9},{9,8},{10,11... | collective-permute-start | bytes 405512 | tf_op jit(solution)/shard_map/ppermute | solution.py:61
  13.7 5.0 %collective-permute-start.6 = (f32[264,128]{1,0:T(8,128)S(1)}, f32[264,128]{1,0:T(8,128)S(1)}, u32[]{:S(2)}, u32[]{:S(2)}) collective-permute-start(f32[264,128]{1,0:T(8,128)S(1)} %collective-permute-done.5.refs_1_), channel_id=1, source_target_pairs={{0,2},{1,5},{2,0},{3,7},{4,6},{5,1},{6,4},{7,3},{8,10},{9,13},{10,... | collective-permute-start | bytes 405512 | tf_op jit(solution)/shard_map/ppermute | solution.py:61
  16.0 5.0 %collective-permute-start.3 = (f32[264,128]{1,0:T(8,128)S(1)}, f32[264,128]{1,0:T(8,128)S(1)}, u32[]{:S(2)}, u32[]{:S(2)}) collective-permute-start(f32[264,128]{1,0:T(8,128)S(1)} %collective-permute-done.2.refs_4_), channel_id=1, source_target_pairs={{0,2},{1,5},{2,0},{3,7},{4,6},{5,1},{6,4},{7,3},{8,10},{9,13},{10,... | collective-permute-start | bytes 405512 | tf_op jit(solution)/shard_map/ppermute | solution.py:61
  17.1 3.9 %collective-permute-start.12 = (f32[264,128]{1,0:T(8,128)S(1)}, f32[264,128]{1,0:T(8,128)S(1)}, u32[]{:S(2)}, u32[]{:S(2)}) collective-permute-start(f32[264,128]{1,0:T(8,128)S(1)} %collective-permute-done.8.refs_2_), channel_id=1, source_target_pairs={{0,1},{1,0},{2,3},{3,2},{4,5},{5,4},{6,7},{7,6},{8,9},{9,8},{10,11... | collective-permute-start | bytes 405512 | tf_op jit(solution)/shard_map/ppermute | solution.py:61
  17.1 3.9 %collective-permute-start.14 = (f32[264,128]{1,0:T(8,128)S(1)}, f32[264,128]{1,0:T(8,128)S(1)}, u32[]{:S(2)}, u32[]{:S(2)}) collective-permute-start(f32[264,128]{1,0:T(8,128)S(1)} %collective-permute-done.2.refs_4_), channel_id=1, source_target_pairs={{0,1},{1,0},{2,3},{3,2},{4,5},{5,4},{6,7},{7,6},{8,9},{9,8},{10,11... | collective-permute-start | bytes 405512 | tf_op jit(solution)/shard_map/ppermute | solution.py:61
  17.6 3.4 %collective-permute-start.15 = (f32[264,128]{1,0:T(8,128)S(1)}, f32[264,128]{1,0:T(8,128)S(1)}, u32[]{:S(2)}, u32[]{:S(2)}) collective-permute-start(f32[264,128]{1,0:T(8,128)S(1)} %collective-permute-done.9.refs_5_), channel_id=1, source_target_pairs={{0,1},{1,0},{2,3},{3,2},{4,5},{5,4},{6,7},{7,6},{8,9},{9,8},{10,11... | collective-permute-start | bytes 405512 | tf_op jit(solution)/shard_map/ppermute | solution.py:61
  18.7 2.9 %collective-permute-start.7 = (f32[264,128]{1,0:T(8,128)S(1)}, f32[264,128]{1,0:T(8,128)S(1)}, u32[]{:S(2)}, u32[]{:S(2)}) collective-permute-start(f32[264,128]{1,0:T(8,128)S(1)} %collective-permute-done.6.refs_0_), channel_id=1, source_target_pairs={{0,1},{1,0},{2,3},{3,2},{4,5},{5,4},{6,7},{7,6},{8,9},{9,8},{10,11... | collective-permute-start | bytes 405512 | tf_op jit(solution)/shard_map/ppermute | solution.py:61
  21.0 1.4 %collective-permute-start.4 = (f32[264,128]{1,0:T(8,128)S(1)}, f32[264,128]{1,0:T(8,128)S(1)}, u32[]{:S(2)}, u32[]{:S(2)}) collective-permute-start(f32[264,128]{1,0:T(8,128)S(1)} %collective-permute-done.3.refs_0_), channel_id=1, source_target_pairs={{0,1},{1,0},{2,3},{3,2},{4,5},{5,4},{6,7},{7,6},{8,9},{9,8},{10,11... | collective-permute-start | bytes 405512 | tf_op jit(solution)/shard_map/ppermute | solution.py:61

commit v4 on v3

--- a/solution.py
+++ b/solution.py
@@ -52,6 +52,26 @@
         compiler_params=pltpu.CompilerParams(vmem_limit_bytes=2 * 1024 * 1024),
         name="pack",
     )(modes, weight_rows)
+
+
+def center_kernel(components, chunk_ref, center_ref):
+    cells = (chunk_ref.shape[0] - SPARE_ROWS) // components
+    center_ref[...] = jnp.zeros_like(center_ref)
+    for a in range(components):
+        rows = chunk_ref[a * cells : (a + 1) * cells, :]
+        center_ref[a : a + 1, :] = jnp.sum(rows, axis=0, keepdims=True) * (1.0 / cells)
+
+
+def center(chunk, components):
+    vmem = pl.BlockSpec(memory_space=pltpu.VMEM)
+    return pl.pallas_call(
+        functools.partial(center_kernel, components),
+        out_shape=jax.ShapeDtypeStruct((SPARE_ROWS, chunk.shape[1]), jnp.float32),
+        in_specs=[vmem],
+        out_specs=vmem,
+        compiler_params=pltpu.CompilerParams(vmem_limit_bytes=1024 * 1024),
+        name="center",
+    )(chunk)
 
 
 def exchange(held, even_mask, odd_mask):
@@ -131,7 +151,7 @@
     return [jnp.bitwise_xor(me, jnp.where(odd, odd_offset, even_offset)) for even_offset, odd_offset in offsets]
 
 
-def take_in(coeffs, places, chunk_refs, flow_ref, weight_ref, mode_refs):
+def take_in(coeffs, center_ref, places, chunk_refs, flow_ref, weight_ref, mode_refs):
     own, mode_count = coeffs.shape
     components, devices, _, lanes = flow_ref.shape
     total_cells = devices * lanes
@@ -140,7 +160,8 @@
     for place, chunk_ref in zip(places, chunk_refs):
         rows = pl.ds(pl.multiple_of(place * lanes, lanes), lanes)
         for a in range(components):
-            split = jnp.concatenate(halves(chunk_ref[a * lanes : (a + 1) * lanes, :]), axis=1)
+            beyond = chunk_ref[a * lanes : (a + 1) * lanes, :] - center_ref[a : a + 1, :]
+            split = jnp.concatenate(halves(beyond), axis=1)
             mode_refs[a][rows, :] = split
             both = lax.dot_general(left, split, (((1,), (1,)), ((), ())), preferred_element_type=jnp.float32)
             flow_ref[a, place] = both[:own] + both[own:]
@@ -148,10 +169,10 @@
         weight_ref[pl.ds(place, 1), :] = chunk_ref[last : last + 1, :] / (SLOPE_SCALE * total_cells)
 
 
-def take_in_kernel(offsets, me_ref, coeff_ref, *refs):
+def take_in_kernel(offsets, me_ref, coeff_ref, center_ref, *refs):
     chunk_refs = refs[: len(offsets)]
     kept = refs[-2 - COMPONENTS :]
-    take_in(coeff_ref[...], placing(me_ref[0, 0], offsets), chunk_refs, kept[0], kept[1], kept[2:])
+    take_in(coeff_ref[...], center_ref, placing(me_ref[0, 0], offsets), chunk_refs, kept[0], kept[1], kept[2:])
 
 
 def state_of(components, devices, own, lanes, mode_count):
@@ -162,10 +183,10 @@
     )
 
 
-def absorb(me, coeffs, group, shapes, state):
+def absorb(me, coeffs, middle, group, shapes, state):
     offsets = [one[1:] for one in group]
     vmem = pl.BlockSpec(memory_space=pltpu.VMEM)
-    operands = (me, coeffs, *(one[0] for one in group), *state)
+    operands = (me, coeffs, middle, *(one[0] for one in group), *state)
     size = sum(operand.size * operand.dtype.itemsize for operand in (*operands, *shapes))
     return pl.pallas_call(
         functools.partial(take_in_kernel, offsets),
@@ -178,7 +199,7 @@
     )(*operands)
 
 
-def step_kernel(offsets, across, me_ref, coeff_ref, force_ref, visc_ref, *refs):
+def step_kernel(offsets, across, me_ref, coeff_ref, force_ref, visc_ref, center_ref, *refs):
     chunk_refs = refs[: len(offsets)]
     out_ref, flow_ref, weight_ref, *mode_refs = refs[-3 - COMPONENTS :]
     own, mode_count = out_ref.shape
@@ -186,7 +207,7 @@
     layers = lanes // across
     coeffs = coeff_ref[...]
     forcing = force_ref[...]
-    take_in(coeffs, placing(me_ref[0, 0], offsets), chunk_refs, flow_ref, weight_ref, mode_refs)
+    take_in(coeffs, center_ref, placing(me_ref[0, 0], offsets), chunk_refs, flow_ref, weight_ref, mode_refs)
     visc = visc_ref[...] / SLOPE_SCALE
     lane = lax.broadcasted_iota(jnp.int32, (own, lanes), 1)
     y = lane % across
@@ -237,6 +258,9 @@
             )
             both = both[:own] + both[own:]
             flow.append([both[:, p * lanes : (p + 1) * lanes] for p in range(devices)])
+        centers = [center_ref[a : a + 1, :] for a in range(components)]
+        base = [jnp.sum(coeffs * centers[a], axis=1, keepdims=True) for a in range(components)]
+        whole = [[f + base[a] for f in flow[a]] for a in range(components)]
         change = jnp.zeros((own, mode_count), jnp.float32)
         for a in range(components):
             x_slope = slope_along(flow[a])
@@ -245,14 +269,12 @@
             y_flux = [weight[p] * y_slope[p] for p in range(devices)]
             x_spread = slope_along(x_flux)
             y_spread = slope_across(y_flux)
-            source = jnp.concatenate(
-                [
-                    flow[0][p] * x_flux[p] + flow[1][p] * y_flux[p] - visc * (x_spread[p] + y_spread[p])
-                    for p in range(devices)
-                ],
-                axis=1,
-            )
-            high, low = halves(source)
+            source = [
+                whole[0][p] * x_flux[p] + whole[1][p] * y_flux[p] - visc * (x_spread[p] + y_spread[p])
+                for p in range(devices)
+            ]
+            change = change + jnp.sum(sum(source), axis=1, keepdims=True) * centers[a]
+            high, low = halves(jnp.concatenate(source, axis=1))
             right = jnp.dot(
                 jnp.concatenate([high, low], axis=0), mode_refs[a][...], preferred_element_type=jnp.float32
             )
@@ -270,13 +292,14 @@
     rows = select(seeds, coeff_table, force_table, visc_table)
     groups, by_offset = gather(modes, cell_weight, rows)
     me = jnp.full((1, 128), lax.axis_index("space") if by_offset else 0, jnp.int32)
+    middle = center(groups[0][0][0], components)
     shapes = state_of(components, devices, own, lanes, mode_count)
     state = ()
     for group in groups[:-1]:
-        state = absorb(me, rows[0], group, shapes, state)
+        state = absorb(me, rows[0], middle, group, shapes, state)
     late = groups[-1]
     vmem = pl.BlockSpec(memory_space=pltpu.VMEM)
-    operands = (me, *rows, *(one[0] for one in late), *state)
+    operands = (me, *rows, middle, *(one[0] for one in late), *state)
     size = sum(operand.size * operand.dtype.itemsize for operand in (*operands, *shapes))
     out = jax.ShapeDtypeStruct((own, mode_count), jnp.float32)
     out, *_ = pl.pallas_call(

time: 25.2 us -> 25.2 us (level)
  no operation moved by 1% of the time
where the time goes in v4:
time: 25.2 us; the launch traced here: 25.1 us
  starting transfers between devices  12.5 us (50%)
  waiting for transfers between devices  7.24 us (29%)
  Pallas kernels  4.34 us (17%)
  local copies, waits for them, and re-layouts  0.92 us (4%)
    ppermute x16, starting transfers between devices, exchange(): array = lax.ppermute(array, 'space', pairs)  12.5 us
    ppermute x16, waiting for transfers between devices, exchange(): array = lax.ppermute(array, 'space', pairs)  7.24 us
    pallas_call x1, Pallas kernels, shards(): pl.pallas_call(functools.partial(step_kernel, [one[1:] for one in late],...  2.77 us
    unnamed x12, local copies, waits for them, and re-layouts  0.92 us
    pallas_call x2, Pallas kernels, absorb(): pl.pallas_call(functools.partial(take_in_kernel, offsets), out_shape=shap...  0.82 us
    pallas_call x1, Pallas kernels, select(): pl.pallas_call(select_kernel, out_shape=(rows, rows, rows), in_specs=[sme...  0.57 us
  transfers between devices with their start and end apart: 16, of which 6 were waited for; matrix products, arithmetic and copies ran while one was open for 0% of the time, Pallas kernels for 6%

profile of v4, /device:TPU:0, one launch (start us, length us, event | category | flops | bytes accessed | tf_op | source)
XLA Modules:
  0.0 25.1 jit_solution(6805940023324276675)
XLA Ops:
  0.0 0.0 copy-start.4
  0.0 5.0 %collective-permute-start = (f32[256,128]{1,0:T(8,128)}, f32[256,128]{1,0:T(8,128)S(1)}, u32[]{:S(2)}, u32[]{:S(2)}) collective-permute-start(f32[256,128]{1,0:T(8,128)} %bitcast.3), channel_id=1, source_target_pairs={{0,12},{1,13},{2,14},{3,15},{4,8},{5,9},{6,10},{7,11},{8,4},{9,5},... | collective-permute-start | bytes 393224 | tf_op jit(solution)/shard_map/ppermute | solution.py:81
  5.1 0.0 copy-done.4
  5.1 0.7 %collective-permute-start.1 = (f32[2,64]{1,0:T(2,128)S(1)}, f32[2,64]{1,0:T(2,128)S(1)}, u32[]{:S(2)}, u32[]{:S(2)}) collective-permute-start(f32[2,64]{1,0:T(2,128)S(1)} %copy-done.4), channel_id=1, source_target_pairs={{0,12},{1,13},{2,14},{3,15},{4,8},{5,9},{6,10},{7,11},{8,4},{9,5},... | collective-permute-start | bytes 1544 | tf_op jit(solution)/shard_map/ppermute | solution.py:81
  5.7 0.1 lay.2.row_ref
  5.8 0.0 copy-start.2
  5.8 0.9 %copy-done.2 = f32[2,128,2,64]{1,3,2,0:T(8,128)S(1)} copy-done((f32[2,128,2,64]{1,3,2,0:T(8,128)S(1)}, f32[2,128,2,64]{1,3,2,0:T(8,128)}, u32[]{:S(2)}) %copy-start.2) | copy-done | bytes 131096
  6.7 0.0 copy-start
  6.7 0.0 copy-start.1
  6.7 0.0 copy-start.3
  6.7 0.0 copy-start.5
  6.7 0.1 collective-permute-start.5
  6.8 1.6 %collective-permute-start.8 = (f32[264,128]{1,0:T(8,128)S(1)}, f32[264,128]{1,0:T(8,128)S(1)}, u32[]{:S(2)}, u32[]{:S(2)}) collective-permute-start(f32[264,128]{1,0:T(8,128)S(1)} %pack.2.chunk_ref.refs_0_), channel_id=1, source_target_pairs={{0,2},{1,5},{2,0},{3,7},{4,6},{5,1},{6,4},{7,3},{8,10},{9,13},{10,... | collective-permute-start | bytes 405512 | tf_op jit(solution)/shard_map/ppermute | solution.py:81
  8.4 0.0 collective-permute-start.10
  8.4 0.0 copy-done
  8.4 0.0 copy-done.1
  8.4 0.0 copy-done.3
  8.4 0.0 copy-done.5
  8.4 0.6 %select.1 = (f32[8,128]{1,0:T(8,128)S(1)}, f32[8,128]{1,0:T(8,128)S(1)}, f32[8,128]{1,0:T(8,128)S(1)}) custom-call(s32[8]{0:T(128)S(1)} %copy-done.5, f32[256]{0:T(256)S(1)} %copy-done.3, f32[256,128]{1,0:T(8,128)S(1)} %copy-done, f32[256,128]{1,0:T(8,128)S(1)} %copy-done.1), custom_call_target="tpu_custom_call" | custom-call | tf_op jit(solution)/shard_map/select/pallas_call | solution.py:139
  9.0 1.4 %collective-permute-done.1.weight_ref = f32[2,64]{1,0:T(2,128)S(1)} collective-permute-done((f32[2,64]{1,0:T(2,128)S(1)}, f32[2,64]{1,0:T(2,128)S(1)}, u32[]{:S(2)}, u32[]{:S(2)}) %collective-permute-start.1) | collective-permute-done | bytes 544 | tf_op jit(solution)/shard_map/ppermute | solution.py:81
  10.4 0.1 lay.3.row_ref
  10.5 0.0 collective-permute-done.modes_ref
  10.5 1.0 %collective-permute-start.2 = (f32[264,128]{1,0:T(8,128)S(1)}, f32[264,128]{1,0:T(8,128)S(1)}, u32[]{:S(2)}, u32[]{:S(2)}) collective-permute-start(f32[264,128]{1,0:T(8,128)S(1)} %pack.3.refs_3_), channel_id=1, source_target_pairs={{0,4},{1,3},{2,6},{3,1},{4,0},{5,7},{6,2},{7,5},{8,12},{9,11},{10,... | collective-permute-start | bytes 405512 | tf_op jit(solution)/shard_map/ppermute | solution.py:81
  11.5 1.5 %collective-permute-start.9 = (f32[264,128]{1,0:T(8,128)S(1)}, f32[264,128]{1,0:T(8,128)S(1)}, u32[]{:S(2)}, u32[]{:S(2)}) collective-permute-start(f32[264,128]{1,0:T(8,128)S(1)} %pack.3.refs_3_), channel_id=1, source_target_pairs={{0,2},{1,5},{2,0},{3,7},{4,6},{5,1},{6,4},{7,3},{8,10},{9,13},{10,... | collective-permute-start | bytes 405512 | tf_op jit(solution)/shard_map/ppermute | solution.py:81
  13.0 0.2 collective-permute-done.5.refs_1_
  13.2 0.0 collective-permute-start.13
  13.2 0.0 collective-permute-done.8.refs_2_
  13.2 0.5 %collective-permute-start.11 = (f32[264,128]{1,0:T(8,128)S(1)}, f32[264,128]{1,0:T(8,128)S(1)}, u32[]{:S(2)}, u32[]{:S(2)}) collective-permute-start(f32[264,128]{1,0:T(8,128)S(1)} %collective-permute-done.5.refs_1_), channel_id=1, source_target_pairs={{0,1},{1,0},{2,3},{3,2},{4,5},{5,4},{6,7},{7,6},{8,9},{9,8},{10,11... | collective-permute-start | bytes 405512 | tf_op jit(solution)/shard_map/ppermute | solution.py:81
  13.7 0.0 collective-permute-done.10.refs_6_
  13.7 0.4 %collective-permute-start.6 = (f32[264,128]{1,0:T(8,128)S(1)}, f32[264,128]{1,0:T(8,128)S(1)}, u32[]{:S(2)}, u32[]{:S(2)}) collective-permute-start(f32[264,128]{1,0:T(8,128)S(1)} %collective-permute-done.5.refs_1_), channel_id=1, source_target_pairs={{0,2},{1,5},{2,0},{3,7},{4,6},{5,1},{6,4},{7,3},{8,10},{9,13},{10,... | collective-permute-start | bytes 405512 | tf_op jit(solution)/shard_map/ppermute | solution.py:81
  14.1 1.8 %collective-permute-done.2.refs_4_ = f32[264,128]{1,0:T(8,128)S(1)} collective-permute-done((f32[264,128]{1,0:T(8,128)S(1)}, f32[264,128]{1,0:T(8,128)S(1)}, u32[]{:S(2)}, u32[]{:S(2)}) %collective-permute-start.2) | collective-permute-done | bytes 135200 | tf_op jit(solution)/shard_map/ppermute | solution.py:81
  16.0 1.1 %collective-permute-start.3 = (f32[264,128]{1,0:T(8,128)S(1)}, f32[264,128]{1,0:T(8,128)S(1)}, u32[]{:S(2)}, u32[]{:S(2)}) collective-permute-start(f32[264,128]{1,0:T(8,128)S(1)} %collective-permute-done.2.refs_4_), channel_id=1, source_target_pairs={{0,2},{1,5},{2,0},{3,7},{4,6},{5,1},{6,4},{7,3},{8,10},{9,13},{10,... | collective-permute-start | bytes 405512 | tf_op jit(solution)/shard_map/ppermute | solution.py:81
  17.1 0.0 collective-permute-done.9.refs_5_
  17.1 0.0 collective-permute-start.12
  17.1 0.0 collective-permute-done.13.refs_9_
  17.1 0.5 %collective-permute-start.14 = (f32[264,128]{1,0:T(8,128)S(1)}, f32[264,128]{1,0:T(8,128)S(1)}, u32[]{:S(2)}, u32[]{:S(2)}) collective-permute-start(f32[264,128]{1,0:T(8,128)S(1)} %collective-permute-done.2.refs_4_), channel_id=1, source_target_pairs={{0,1},{1,0},{2,3},{3,2},{4,5},{5,4},{6,7},{7,6},{8,9},{9,8},{10,11... | collective-permute-start | bytes 405512 | tf_op jit(solution)/shard_map/ppermute | solution.py:81
  17.6 0.0 collective-permute-done.11.refs_7_
  17.6 0.1 collective-permute-start.15
  17.7 1.0 %collective-permute-done.6.refs_0_ = f32[264,128]{1,0:T(8,128)S(1)} collective-permute-done((f32[264,128]{1,0:T(8,128)S(1)}, f32[264,128]{1,0:T(8,128)S(1)}, u32[]{:S(2)}, u32[]{:S(2)}) %collective-permute-start.6) | collective-permute-done | bytes 135200 | tf_op jit(solution)/shard_map/ppermute | solution.py:81
  18.7 0.0 collective-permute-start.7
  18.7 2.3 %collective-permute-done.3.refs_0_ = f32[264,128]{1,0:T(8,128)S(1)} collective-permute-done((f32[264,128]{1,0:T(8,128)S(1)}, f32[264,128]{1,0:T(8,128)S(1)}, u32[]{:S(2)}, u32[]{:S(2)}) %collective-permute-start.3) | collective-permute-done | bytes 135200 | tf_op jit(solution)/shard_map/ppermute | solution.py:81
  21.0 0.0 collective-permute-start.4
  21.0 0.0 collective-permute-done.12.refs_8_
  21.0 0.0 collective-permute-done.14.refs_10_
  21.0 0.0 collective-permute-done.15.refs_11_
  21.0 0.6 %absorb.2 = (f32[2,16,8,128]{3,2,1,0:T(8,128)S(1)}, f32[16,128]{1,0:T(8,128)S(1)}, bf16[2048,256]{1,0:T(8,128)(2,1)S(1)}, bf16[2048,256]{1,0:T(8,128)(2,1)S(1)}) custom-call(s32[1,128]{1,0:T(1,128)S(1)} %broadcast_in_dim.3.me_ref, f32[8,128]{1,0:T(8,128)S(1)} %get-tuple-element.18.coeff_ref, f32[8,128]{1,0:T(8,128)S(1)} %center.1.center_ref, ...), custom_call_target="tpu_custom_call" | custom-call | tf_op jit(solution)/shard_map/absorb/pallas_call | solution.py:191
  21.6 0.0 collective-permute-done.7.refs_1_
  21.6 0.2 absorb.3
  21.9 0.5 %collective-permute-done.4.refs_1_ = f32[264,128]{1,0:T(8,128)S(1)} collective-permute-done((f32[264,128]{1,0:T(8,128)S(1)}, f32[264,128]{1,0:T(8,128)S(1)}, u32[]{:S(2)}, u32[]{:S(2)}) %collective-permute-start.4) | collective-permute-done | bytes 135200 | tf_op jit(solution)/shard_map/ppermute | solution.py:81
  22.3 2.8 %steps.1 = (f32[8,128]{1,0:T(8,128)}, f32[2,16,8,128]{3,2,1,0:T(8,128)S(1)}, f32[16,128]{1,0:T(8,128)S(1)}, bf16[2048,256]{1,0:T(8,128)(2,1)S(1)}, bf16[2048,256]{1,0:T(8,128)(2,1)S(1)}) custom-call(s32[1,128]{1,0:T(1,128)S(1)} %broadcast_in_dim.3.me_ref, ...), custom_call_target="tpu_custom_call", output_to_operand_aliasing={{1}: (7, {}), {2}: (8, {}), {3}: (9, {}), {4}: (10, {})} | custom-call | tf_op jit(solution)/shard_map/steps/pallas_call | solution.py:305
  (4 shorter events, 0.1 us)
Async XLA Ops:
  0.0 5.1 %copy-start.4 = (f32[2,64]{1,0:T(2,128)S(1)}, f32[2,64]{1,0:T(2,128)}, u32[]{:S(2)}) copy-start(f32[2,64]{1,0:T(2,128)} %weight_ref.1) | copy-start | bytes 1540
  0.0 10.5 %collective-permute-start = (f32[256,128]{1,0:T(8,128)}, f32[256,128]{1,0:T(8,128)S(1)}, u32[]{:S(2)}, u32[]{:S(2)}) collective-permute-start(f32[256,128]{1,0:T(8,128)} %bitcast.3), channel_id=1, source_target_pairs={{0,12},{1,13},{2,14},{3,15},{4,8},{5,9},{6,10},{7,11},{8,4},{9,5},... | collective-permute-start | bytes 393224 | tf_op jit(solution)/shard_map/ppermute | solution.py:81
  5.1 5.4 %collective-permute-start.1 = (f32[2,64]{1,0:T(2,128)S(1)}, f32[2,64]{1,0:T(2,128)S(1)}, u32[]{:S(2)}, u32[]{:S(2)}) collective-permute-start(f32[2,64]{1,0:T(2,128)S(1)} %copy-done.4), channel_id=1, source_target_pairs={{0,12},{1,13},{2,14},{3,15},{4,8},{5,9},{6,10},{7,11},{8,4},{9,5},... | collective-permute-start | bytes 1544 | tf_op jit(solution)/shard_map/ppermute | solution.py:81
  5.8 0.9 %copy-start.2 = (f32[2,128,2,64]{1,3,2,0:T(8,128)S(1)}, f32[2,128,2,64]{1,3,2,0:T(8,128)}, u32[]{:S(2)}) copy-start(f32[2,128,2,64]{1,3,2,0:T(8,128)} %param.6) | copy-start | bytes 393220
  6.7 1.7 %copy-start = (f32[256,128]{1,0:T(8,128)S(1)}, f32[256,128]{1,0:T(8,128)}, u32[]{:S(2)}) copy-start(f32[256,128]{1,0:T(8,128)} %coeff_table_ref.1) | copy-start | bytes 393220
  6.7 1.7 %copy-start.1 = (f32[256,128]{1,0:T(8,128)S(1)}, f32[256,128]{1,0:T(8,128)}, u32[]{:S(2)}) copy-start(f32[256,128]{1,0:T(8,128)} %force_table_ref.1) | copy-start | bytes 393220
  6.7 1.7 %copy-start.3 = (f32[256]{0:T(256)S(1)}, f32[256]{0:T(256)}, u32[]{:S(2)}) copy-start(f32[256]{0:T(256)} %visc_table_ref.1) | copy-start | bytes 3076
  6.7 1.7 %copy-start.5 = (s32[8]{0:T(128)S(1)}, s32[8]{0:T(128)}, u32[]{:S(2)}) copy-start(s32[8]{0:T(128)} %seeds_ref.1) | copy-start | bytes 100
  6.7 6.5 %collective-permute-start.5 = (f32[264,128]{1,0:T(8,128)S(1)}, f32[264,128]{1,0:T(8,128)S(1)}, u32[]{:S(2)}, u32[]{:S(2)}) collective-permute-start(f32[264,128]{1,0:T(8,128)S(1)} %pack.2.chunk_ref.refs_0_), channel_id=1, source_target_pairs={{0,4},{1,3},{2,6},{3,1},{4,0},{5,7},{6,2},{7,5},{8,12},{9,11},{10,... | collective-permute-start | bytes 405512 | tf_op jit(solution)/shard_map/ppermute | solution.py:81
  6.8 6.4 %collective-permute-start.8 = (f32[264,128]{1,0:T(8,128)S(1)}, f32[264,128]{1,0:T(8,128)S(1)}, u32[]{:S(2)}, u32[]{:S(2)}) collective-permute-start(f32[264,128]{1,0:T(8,128)S(1)} %pack.2.chunk_ref.refs_0_), channel_id=1, source_target_pairs={{0,2},{1,5},{2,0},{3,7},{4,6},{5,1},{6,4},{7,3},{8,10},{9,13},{10,... | collective-permute-start | bytes 405512 | tf_op jit(solution)/shard_map/ppermute | solution.py:81
  8.4 5.3 %collective-permute-start.10 = (f32[264,128]{1,0:T(8,128)S(1)}, f32[264,128]{1,0:T(8,128)S(1)}, u32[]{:S(2)}, u32[]{:S(2)}) collective-permute-start(f32[264,128]{1,0:T(8,128)S(1)} %pack.2.chunk_ref.refs_0_), channel_id=1, source_target_pairs={{0,1},{1,0},{2,3},{3,2},{4,5},{5,4},{6,7},{7,6},{8,9},{9,8},{10,11... | collective-permute-start | bytes 405512 | tf_op jit(solution)/shard_map/ppermute | solution.py:81
  10.5 5.5 %collective-permute-start.2 = (f32[264,128]{1,0:T(8,128)S(1)}, f32[264,128]{1,0:T(8,128)S(1)}, u32[]{:S(2)}, u32[]{:S(2)}) collective-permute-start(f32[264,128]{1,0:T(8,128)S(1)} %pack.3.refs_3_), channel_id=1, source_target_pairs={{0,4},{1,3},{2,6},{3,1},{4,0},{5,7},{6,2},{7,5},{8,12},{9,11},{10,... | collective-permute-start | bytes 405512 | tf_op jit(solution)/shard_map/ppermute | solution.py:81
  11.5 5.6 %collective-permute-start.9 = (f32[264,128]{1,0:T(8,128)S(1)}, f32[264,128]{1,0:T(8,128)S(1)}, u32[]{:S(2)}, u32[]{:S(2)}) collective-permute-start(f32[264,128]{1,0:T(8,128)S(1)} %pack.3.refs_3_), channel_id=1, source_target_pairs={{0,2},{1,5},{2,0},{3,7},{4,6},{5,1},{6,4},{7,3},{8,10},{9,13},{10,... | collective-permute-start | bytes 405512 | tf_op jit(solution)/shard_map/ppermute | solution.py:81
  13.2 3.9 %collective-permute-start.13 = (f32[264,128]{1,0:T(8,128)S(1)}, f32[264,128]{1,0:T(8,128)S(1)}, u32[]{:S(2)}, u32[]{:S(2)}) collective-permute-start(f32[264,128]{1,0:T(8,128)S(1)} %pack.3.refs_3_), channel_id=1, source_target_pairs={{0,1},{1,0},{2,3},{3,2},{4,5},{5,4},{6,7},{7,6},{8,9},{9,8},{10,11... | collective-permute-start | bytes 405512 | tf_op jit(solution)/shard_map/ppermute | solution.py:81
  13.2 4.4 %collective-permute-start.11 = (f32[264,128]{1,0:T(8,128)S(1)}, f32[264,128]{1,0:T(8,128)S(1)}, u32[]{:S(2)}, u32[]{:S(2)}) collective-permute-start(f32[264,128]{1,0:T(8,128)S(1)} %collective-permute-done.5.refs_1_), channel_id=1, source_target_pairs={{0,1},{1,0},{2,3},{3,2},{4,5},{5,4},{6,7},{7,6},{8,9},{9,8},{10,11... | collective-permute-start | bytes 405512 | tf_op jit(solution)/shard_map/ppermute | solution.py:81
  13.7 5.0 %collective-permute-start.6 = (f32[264,128]{1,0:T(8,128)S(1)}, f32[264,128]{1,0:T(8,128)S(1)}, u32[]{:S(2)}, u32[]{:S(2)}) collective-permute-start(f32[264,128]{1,0:T(8,128)S(1)} %collective-permute-done.5.refs_1_), channel_id=1, source_target_pairs={{0,2},{1,5},{2,0},{3,7},{4,6},{5,1},{6,4},{7,3},{8,10},{9,13},{10,... | collective-permute-start | bytes 405512 | tf_op jit(solution)/shard_map/ppermute | solution.py:81
  16.0 5.0 %collective-permute-start.3 = (f32[264,128]{1,0:T(8,128)S(1)}, f32[264,128]{1,0:T(8,128)S(1)}, u32[]{:S(2)}, u32[]{:S(2)}) collective-permute-start(f32[264,128]{1,0:T(8,128)S(1)} %collective-permute-done.2.refs_4_), channel_id=1, source_target_pairs={{0,2},{1,5},{2,0},{3,7},{4,6},{5,1},{6,4},{7,3},{8,10},{9,13},{10,... | collective-permute-start | bytes 405512 | tf_op jit(solution)/shard_map/ppermute | solution.py:81
  17.1 3.9 %collective-permute-start.12 = (f32[264,128]{1,0:T(8,128)S(1)}, f32[264,128]{1,0:T(8,128)S(1)}, u32[]{:S(2)}, u32[]{:S(2)}) collective-permute-start(f32[264,128]{1,0:T(8,128)S(1)} %collective-permute-done.8.refs_2_), channel_id=1, source_target_pairs={{0,1},{1,0},{2,3},{3,2},{4,5},{5,4},{6,7},{7,6},{8,9},{9,8},{10,11... | collective-permute-start | bytes 405512 | tf_op jit(solution)/shard_map/ppermute | solution.py:81
  17.1 3.9 %collective-permute-start.14 = (f32[264,128]{1,0:T(8,128)S(1)}, f32[264,128]{1,0:T(8,128)S(1)}, u32[]{:S(2)}, u32[]{:S(2)}) collective-permute-start(f32[264,128]{1,0:T(8,128)S(1)} %collective-permute-done.2.refs_4_), channel_id=1, source_target_pairs={{0,1},{1,0},{2,3},{3,2},{4,5},{5,4},{6,7},{7,6},{8,9},{9,8},{10,11... | collective-permute-start | bytes 405512 | tf_op jit(solution)/shard_map/ppermute | solution.py:81
  17.6 3.4 %collective-permute-start.15 = (f32[264,128]{1,0:T(8,128)S(1)}, f32[264,128]{1,0:T(8,128)S(1)}, u32[]{:S(2)}, u32[]{:S(2)}) collective-permute-start(f32[264,128]{1,0:T(8,128)S(1)} %collective-permute-done.9.refs_5_), channel_id=1, source_target_pairs={{0,1},{1,0},{2,3},{3,2},{4,5},{5,4},{6,7},{7,6},{8,9},{9,8},{10,11... | collective-permute-start | bytes 405512 | tf_op jit(solution)/shard_map/ppermute | solution.py:81
  18.7 2.9 %collective-permute-start.7 = (f32[264,128]{1,0:T(8,128)S(1)}, f32[264,128]{1,0:T(8,128)S(1)}, u32[]{:S(2)}, u32[]{:S(2)}) collective-permute-start(f32[264,128]{1,0:T(8,128)S(1)} %collective-permute-done.6.refs_0_), channel_id=1, source_target_pairs={{0,1},{1,0},{2,3},{3,2},{4,5},{5,4},{6,7},{7,6},{8,9},{9,8},{10,11... | collective-permute-start | bytes 405512 | tf_op jit(solution)/shard_map/ppermute | solution.py:81
  21.0 1.4 %collective-permute-start.4 = (f32[264,128]{1,0:T(8,128)S(1)}, f32[264,128]{1,0:T(8,128)S(1)}, u32[]{:S(2)}, u32[]{:S(2)}) collective-permute-start(f32[264,128]{1,0:T(8,128)S(1)} %collective-permute-done.3.refs_0_), channel_id=1, source_target_pairs={{0,1},{1,0},{2,3},{3,2},{4,5},{5,4},{6,7},{7,6},{8,9},{9,8},{10,11... | collective-permute-start | bytes 405512 | tf_op jit(solution)/shard_map/ppermute | solution.py:81

commit v5 on v4

--- a/solution.py
+++ b/solution.py
@@ -14,6 +14,7 @@
 SPARE_ROWS = 8
 SLOPE_SCALE = 12.0
 COMPONENTS = 2
+COPIES_LIMIT = 8 * 1024 * 1024
 
 
 def lay_kernel(weight_ref, row_ref):
@@ -163,33 +164,39 @@
             beyond = chunk_ref[a * lanes : (a + 1) * lanes, :] - center_ref[a : a + 1, :]
             split = jnp.concatenate(halves(beyond), axis=1)
             mode_refs[a][rows, :] = split
+            if len(mode_refs) > components:
+                mode_refs[components + a][:, rows] = jnp.concatenate(halves(beyond.T), axis=0)
             both = lax.dot_general(left, split, (((1,), (1,)), ((), ())), preferred_element_type=jnp.float32)
             flow_ref[a, place] = both[:own] + both[own:]
         last = components * lanes
         weight_ref[pl.ds(place, 1), :] = chunk_ref[last : last + 1, :] / (SLOPE_SCALE * total_cells)
 
 
-def take_in_kernel(offsets, me_ref, coeff_ref, center_ref, *refs):
+def take_in_kernel(offsets, copies, me_ref, coeff_ref, center_ref, *refs):
     chunk_refs = refs[: len(offsets)]
-    kept = refs[-2 - COMPONENTS :]
+    kept = refs[-2 - copies * COMPONENTS :]
     take_in(coeff_ref[...], center_ref, placing(me_ref[0, 0], offsets), chunk_refs, kept[0], kept[1], kept[2:])
 
 
-def state_of(components, devices, own, lanes, mode_count):
+def state_of(copies, components, devices, own, lanes, mode_count):
     return (
         jax.ShapeDtypeStruct((components, devices, own, lanes), jnp.float32),
         jax.ShapeDtypeStruct((devices, lanes), jnp.float32),
-        *[jax.ShapeDtypeStruct((devices * lanes, 2 * mode_count), jnp.bfloat16) for _ in range(components)],
+        *[
+            jax.ShapeDtypeStruct(shape, jnp.bfloat16)
+            for shape in ((devices * lanes, 2 * mode_count), (2 * mode_count, devices * lanes))[:copies]
+            for _ in range(components)
+        ],
     )
 
 
-def absorb(me, coeffs, middle, group, shapes, state):
+def absorb(copies, me, coeffs, middle, group, shapes, state):
     offsets = [one[1:] for one in group]
     vmem = pl.BlockSpec(memory_space=pltpu.VMEM)
     operands = (me, coeffs, middle, *(one[0] for one in group), *state)
     size = sum(operand.size * operand.dtype.itemsize for operand in (*operands, *shapes))
     return pl.pallas_call(
-        functools.partial(take_in_kernel, offsets),
+        functools.partial(take_in_kernel, offsets, copies),
         out_shape=shapes,
         in_specs=[vmem] * len(operands),
         out_specs=(vmem,) * len(shapes),
@@ -199,9 +206,9 @@
     )(*operands)
 
 
-def step_kernel(offsets, across, me_ref, coeff_ref, force_ref, visc_ref, center_ref, *refs):
+def step_kernel(offsets, copies, across, me_ref, coeff_ref, force_ref, visc_ref, center_ref, *refs):
     chunk_refs = refs[: len(offsets)]
-    out_ref, flow_ref, weight_ref, *mode_refs = refs[-3 - COMPONENTS :]
+    out_ref, flow_ref, weight_ref, *mode_refs = refs[-3 - copies * COMPONENTS :]
     own, mode_count = out_ref.shape
     components, devices, _, lanes = flow_ref.shape
     layers = lanes // across
@@ -243,36 +250,39 @@
 
     weight = [weight_ref[p : p + 1, :] for p in range(devices)]
 
+    centers = [center_ref[a : a + 1, :] for a in range(components)]
     for repeat in range(STEPS):
-        flow = []
+        high, low = halves(coeffs)
+        left = jnp.concatenate(
+            [jnp.concatenate([high, high], axis=1), jnp.concatenate([low, low], axis=1)], axis=0
+        )
+        whole = []
+        fluxes = []
         for a in range(components):
             if repeat == 0:
-                flow.append([flow_ref[a, p] for p in range(devices)])
-                continue
-            high, low = halves(coeffs)
-            left = jnp.concatenate(
-                [jnp.concatenate([high, high], axis=1), jnp.concatenate([low, low], axis=1)], axis=0
-            )
-            both = lax.dot_general(
-                left, mode_refs[a][...], (((1,), (1,)), ((), ())), preferred_element_type=jnp.float32
-            )
-            both = both[:own] + both[own:]
-            flow.append([both[:, p * lanes : (p + 1) * lanes] for p in range(devices)])
-        centers = [center_ref[a : a + 1, :] for a in range(components)]
-        base = [jnp.sum(coeffs * centers[a], axis=1, keepdims=True) for a in range(components)]
-        whole = [[f + base[a] for f in flow[a]] for a in range(components)]
-        change = jnp.zeros((own, mode_count), jnp.float32)
-        for a in range(components):
-            x_slope = slope_along(flow[a])
-            y_slope = slope_across(flow[a])
+                flow = [flow_ref[a, p] for p in range(devices)]
+            else:
+                if copies > 1:
+                    both = jnp.dot(left, mode_refs[components + a][...], preferred_element_type=jnp.float32)
+                else:
+                    both = lax.dot_general(
+                        left, mode_refs[a][...], (((1,), (1,)), ((), ())), preferred_element_type=jnp.float32
+                    )
+                both = both[:own] + both[own:]
+                flow = [both[:, p * lanes : (p + 1) * lanes] for p in range(devices)]
+            base = jnp.sum(coeffs * centers[a], axis=1, keepdims=True)
+            whole.append([f + base for f in flow])
+            x_slope = slope_along(flow)
+            y_slope = slope_across(flow)
             x_flux = [weight[p] * x_slope[p] for p in range(devices)]
             y_flux = [weight[p] * y_slope[p] for p in range(devices)]
             x_spread = slope_along(x_flux)
             y_spread = slope_across(y_flux)
-            source = [
-                whole[0][p] * x_flux[p] + whole[1][p] * y_flux[p] - visc * (x_spread[p] + y_spread[p])
-                for p in range(devices)
-            ]
+            viscous = [visc * (x_spread[p] + y_spread[p]) for p in range(devices)]
+            fluxes.append((x_flux, y_flux, viscous))
+        change = jnp.zeros((own, mode_count), jnp.float32)
+        for a, (x_flux, y_flux, viscous) in enumerate(fluxes):
+            source = [whole[0][p] * x_flux[p] + whole[1][p] * y_flux[p] - viscous[p] for p in range(devices)]
             change = change + jnp.sum(sum(source), axis=1, keepdims=True) * centers[a]
             high, low = halves(jnp.concatenate(source, axis=1))
             right = jnp.dot(
@@ -293,17 +303,18 @@
     groups, by_offset = gather(modes, cell_weight, rows)
     me = jnp.full((1, 128), lax.axis_index("space") if by_offset else 0, jnp.int32)
     middle = center(groups[0][0][0], components)
-    shapes = state_of(components, devices, own, lanes, mode_count)
+    copies = 2 if 8 * components * devices * lanes * mode_count <= COPIES_LIMIT else 1
+    shapes = state_of(copies, components, devices, own, lanes, mode_count)
     state = ()
     for group in groups[:-1]:
-        state = absorb(me, rows[0], middle, group, shapes, state)
+        state = absorb(copies, me, rows[0], middle, group, shapes, state)
     late = groups[-1]
     vmem = pl.BlockSpec(memory_space=pltpu.VMEM)
     operands = (me, *rows, middle, *(one[0] for one in late), *state)
     size = sum(operand.size * operand.dtype.itemsize for operand in (*operands, *shapes))
     out = jax.ShapeDtypeStruct((own, mode_count), jnp.float32)
     out, *_ = pl.pallas_call(
-        functools.partial(step_kernel, [one[1:] for one in late], across),
+        functools.partial(step_kernel, [one[1:] for one in late], copies, across),
         out_shape=(out, *shapes),
         in_specs=[vmem] * len(operands),
         out_specs=(vmem,) * (1 + len(shapes)),

time: 25.2 us -> 25 us (level)
  transfers between devices with their start and end apart: 16 -> 16, of which waited for: 6 -> 6; matrix products, arithmetic and copies ran while one was open for 0% -> 0% of each run, Pallas kernels for 6% -> 7%
where the time goes in v5:
time: 25 us; the launch traced here: 24.9 us
  starting transfers between devices  12.5 us (50%)
  waiting for transfers between devices  7.1 us (28%)
  Pallas kernels  4.26 us (17%)
  local copies, waits for them, and re-layouts  0.92 us (4%)
    ppermute x16, starting transfers between devices, exchange(): array = lax.ppermute(array, 'space', pairs)  12.5 us
    ppermute x16, waiting for transfers between devices, exchange(): array = lax.ppermute(array, 'space', pairs)  7.1 us
    pallas_call x1, Pallas kernels, shards(): pl.pallas_call(functools.partial(step_kernel, [one[1:] for one in late],...  2.56 us
    pallas_call x2, Pallas kernels, absorb(): pl.pallas_call(functools.partial(take_in_kernel, offsets, copies), out_sh...  0.94 us
    unnamed x12, local copies, waits for them, and re-layouts  0.92 us
    pallas_call x1, Pallas kernels, select(): pl.pallas_call(select_kernel, out_shape=(rows, rows, rows), in_specs=[sme...  0.57 us
  transfers between devices with their start and end apart: 16, of which 6 were waited for; matrix products, arithmetic and copies ran while one was open for 0% of the time, Pallas kernels for 7%

profile of v5, /device:TPU:0, one launch (start us, length us, event | category | flops | bytes accessed | tf_op | source)
XLA Modules:
  0.0 24.9 jit_solution(7101469214714476277)
XLA Ops:
  0.0 0.0 copy-start.4
  0.0 5.0 %collective-permute-start = (f32[256,128]{1,0:T(8,128)}, f32[256,128]{1,0:T(8,128)S(1)}, u32[]{:S(2)}, u32[]{:S(2)}) collective-permute-start(f32[256,128]{1,0:T(8,128)} %bitcast.3), channel_id=1, source_target_pairs={{0,12},{1,13},{2,14},{3,15},{4,8},{5,9},{6,10},{7,11},{8,4},{9,5},... | collective-permute-start | bytes 393224 | tf_op jit(solution)/shard_map/ppermute | solution.py:82
  5.1 0.0 copy-done.4
  5.1 0.7 %collective-permute-start.1 = (f32[2,64]{1,0:T(2,128)S(1)}, f32[2,64]{1,0:T(2,128)S(1)}, u32[]{:S(2)}, u32[]{:S(2)}) collective-permute-start(f32[2,64]{1,0:T(2,128)S(1)} %copy-done.4), channel_id=1, source_target_pairs={{0,12},{1,13},{2,14},{3,15},{4,8},{5,9},{6,10},{7,11},{8,4},{9,5},... | collective-permute-start | bytes 1544 | tf_op jit(solution)/shard_map/ppermute | solution.py:82
  5.7 0.1 lay.2.row_ref
  5.8 0.0 copy-start.2
  5.8 0.9 %copy-done.2 = f32[2,128,2,64]{1,3,2,0:T(8,128)S(1)} copy-done((f32[2,128,2,64]{1,3,2,0:T(8,128)S(1)}, f32[2,128,2,64]{1,3,2,0:T(8,128)}, u32[]{:S(2)}) %copy-start.2) | copy-done | bytes 131096
  6.7 0.0 copy-start
  6.7 0.0 copy-start.1
  6.7 0.0 copy-start.3
  6.7 0.0 copy-start.5
  6.7 0.1 collective-permute-start.5
  6.8 1.6 %collective-permute-start.8 = (f32[264,128]{1,0:T(8,128)S(1)}, f32[264,128]{1,0:T(8,128)S(1)}, u32[]{:S(2)}, u32[]{:S(2)}) collective-permute-start(f32[264,128]{1,0:T(8,128)S(1)} %pack.2.chunk_ref.refs_0_), channel_id=1, source_target_pairs={{0,2},{1,5},{2,0},{3,7},{4,6},{5,1},{6,4},{7,3},{8,10},{9,13},{10,... | collective-permute-start | bytes 405512 | tf_op jit(solution)/shard_map/ppermute | solution.py:82
  8.4 0.0 collective-permute-start.10
  8.4 0.0 copy-done
  8.4 0.0 copy-done.1
  8.4 0.0 copy-done.3
  8.4 0.0 copy-done.5
  8.4 0.6 %select.1 = (f32[8,128]{1,0:T(8,128)S(1)}, f32[8,128]{1,0:T(8,128)S(1)}, f32[8,128]{1,0:T(8,128)S(1)}) custom-call(s32[8]{0:T(128)S(1)} %copy-done.5, f32[256]{0:T(256)S(1)} %copy-done.3, f32[256,128]{1,0:T(8,128)S(1)} %copy-done, f32[256,128]{1,0:T(8,128)S(1)} %copy-done.1), custom_call_target="tpu_custom_call" | custom-call | tf_op jit(solution)/shard_map/select/pallas_call | solution.py:140
  9.0 1.4 %collective-permute-done.1.weight_ref = f32[2,64]{1,0:T(2,128)S(1)} collective-permute-done((f32[2,64]{1,0:T(2,128)S(1)}, f32[2,64]{1,0:T(2,128)S(1)}, u32[]{:S(2)}, u32[]{:S(2)}) %collective-permute-start.1) | collective-permute-done | bytes 544 | tf_op jit(solution)/shard_map/ppermute | solution.py:82
  10.4 0.1 lay.3.row_ref
  10.5 0.0 collective-permute-done.modes_ref
  10.5 1.0 %collective-permute-start.2 = (f32[264,128]{1,0:T(8,128)S(1)}, f32[264,128]{1,0:T(8,128)S(1)}, u32[]{:S(2)}, u32[]{:S(2)}) collective-permute-start(f32[264,128]{1,0:T(8,128)S(1)} %pack.3.refs_3_), channel_id=1, source_target_pairs={{0,4},{1,3},{2,6},{3,1},{4,0},{5,7},{6,2},{7,5},{8,12},{9,11},{10,... | collective-permute-start | bytes 405512 | tf_op jit(solution)/shard_map/ppermute | solution.py:82
  11.5 1.5 %collective-permute-start.9 = (f32[264,128]{1,0:T(8,128)S(1)}, f32[264,128]{1,0:T(8,128)S(1)}, u32[]{:S(2)}, u32[]{:S(2)}) collective-permute-start(f32[264,128]{1,0:T(8,128)S(1)} %pack.3.refs_3_), channel_id=1, source_target_pairs={{0,2},{1,5},{2,0},{3,7},{4,6},{5,1},{6,4},{7,3},{8,10},{9,13},{10,... | collective-permute-start | bytes 405512 | tf_op jit(solution)/shard_map/ppermute | solution.py:82
  13.0 0.2 collective-permute-done.5.refs_1_
  13.2 0.0 collective-permute-start.13
  13.2 0.0 collective-permute-done.8.refs_2_
  13.2 0.5 %collective-permute-start.11 = (f32[264,128]{1,0:T(8,128)S(1)}, f32[264,128]{1,0:T(8,128)S(1)}, u32[]{:S(2)}, u32[]{:S(2)}) collective-permute-start(f32[264,128]{1,0:T(8,128)S(1)} %collective-permute-done.5.refs_1_), channel_id=1, source_target_pairs={{0,1},{1,0},{2,3},{3,2},{4,5},{5,4},{6,7},{7,6},{8,9},{9,8},{10,11... | collective-permute-start | bytes 405512 | tf_op jit(solution)/shard_map/ppermute | solution.py:82
  13.7 0.0 collective-permute-done.10.refs_6_
  13.7 0.4 %collective-permute-start.6 = (f32[264,128]{1,0:T(8,128)S(1)}, f32[264,128]{1,0:T(8,128)S(1)}, u32[]{:S(2)}, u32[]{:S(2)}) collective-permute-start(f32[264,128]{1,0:T(8,128)S(1)} %collective-permute-done.5.refs_1_), channel_id=1, source_target_pairs={{0,2},{1,5},{2,0},{3,7},{4,6},{5,1},{6,4},{7,3},{8,10},{9,13},{10,... | collective-permute-start | bytes 405512 | tf_op jit(solution)/shard_map/ppermute | solution.py:82
  14.1 1.8 %collective-permute-done.2.refs_4_ = f32[264,128]{1,0:T(8,128)S(1)} collective-permute-done((f32[264,128]{1,0:T(8,128)S(1)}, f32[264,128]{1,0:T(8,128)S(1)}, u32[]{:S(2)}, u32[]{:S(2)}) %collective-permute-start.2) | collective-permute-done | bytes 135200 | tf_op jit(solution)/shard_map/ppermute | solution.py:82
  16.0 1.1 %collective-permute-start.3 = (f32[264,128]{1,0:T(8,128)S(1)}, f32[264,128]{1,0:T(8,128)S(1)}, u32[]{:S(2)}, u32[]{:S(2)}) collective-permute-start(f32[264,128]{1,0:T(8,128)S(1)} %collective-permute-done.2.refs_4_), channel_id=1, source_target_pairs={{0,2},{1,5},{2,0},{3,7},{4,6},{5,1},{6,4},{7,3},{8,10},{9,13},{10,... | collective-permute-start | bytes 405512 | tf_op jit(solution)/shard_map/ppermute | solution.py:82
  17.1 0.0 collective-permute-done.9.refs_5_
  17.1 0.0 collective-permute-start.12
  17.1 0.0 collective-permute-done.13.refs_9_
  17.1 0.5 %collective-permute-start.14 = (f32[264,128]{1,0:T(8,128)S(1)}, f32[264,128]{1,0:T(8,128)S(1)}, u32[]{:S(2)}, u32[]{:S(2)}) collective-permute-start(f32[264,128]{1,0:T(8,128)S(1)} %collective-permute-done.2.refs_4_), channel_id=1, source_target_pairs={{0,1},{1,0},{2,3},{3,2},{4,5},{5,4},{6,7},{7,6},{8,9},{9,8},{10,11... | collective-permute-start | bytes 405512 | tf_op jit(solution)/shard_map/ppermute | solution.py:82
  17.6 0.0 collective-permute-done.11.refs_7_
  17.6 0.1 collective-permute-start.15
  17.7 1.0 %collective-permute-done.6.refs_0_ = f32[264,128]{1,0:T(8,128)S(1)} collective-permute-done((f32[264,128]{1,0:T(8,128)S(1)}, f32[264,128]{1,0:T(8,128)S(1)}, u32[]{:S(2)}, u32[]{:S(2)}) %collective-permute-start.6) | collective-permute-done | bytes 135200 | tf_op jit(solution)/shard_map/ppermute | solution.py:82
  18.7 0.0 collective-permute-start.7
  18.7 2.3 %collective-permute-done.3.refs_0_ = f32[264,128]{1,0:T(8,128)S(1)} collective-permute-done((f32[264,128]{1,0:T(8,128)S(1)}, f32[264,128]{1,0:T(8,128)S(1)}, u32[]{:S(2)}, u32[]{:S(2)}) %collective-permute-start.3) | collective-permute-done | bytes 135200 | tf_op jit(solution)/shard_map/ppermute | solution.py:82
  21.0 0.0 collective-permute-start.4
  21.0 0.0 collective-permute-done.12.refs_8_
  21.0 0.0 collective-permute-done.14.refs_10_
  21.0 0.0 collective-permute-done.15.refs_11_
  21.0 0.7 %absorb.2 = (f32[2,16,8,128]{3,2,1,0:T(8,128)S(1)}, f32[16,128]{1,0:T(8,128)S(1)}, bf16[2048,256]{1,0:T(8,128)(2,1)S(1)}, bf16[2048,256]{1,0:T(8,128)(2,1)S(1)},...) custom-call(s32[1,128]{1,0:T(1,128)S(1)} %broadcast_in_dim.3.me_ref, ...), custom_call_target="tpu_custom_call" | custom-call | tf_op jit(solution)/shard_map/absorb/pallas_call | solution.py:198
  21.8 0.0 collective-permute-done.7.refs_1_
  21.8 0.2 absorb.3
  22.0 0.3 %collective-permute-done.4.refs_1_ = f32[264,128]{1,0:T(8,128)S(1)} collective-permute-done((f32[264,128]{1,0:T(8,128)S(1)}, f32[264,128]{1,0:T(8,128)S(1)}, u32[]{:S(2)}, u32[]{:S(2)}) %collective-permute-start.4) | collective-permute-done | bytes 135200 | tf_op jit(solution)/shard_map/ppermute | solution.py:82
  22.3 2.6 %steps.1 = (f32[8,128]{1,0:T(8,128)}, f32[2,16,8,128]{3,2,1,0:T(8,128)S(1)}, f32[16,128]{1,0:T(8,128)S(1)}, bf16[2048,256]{1,0:T(8,128)(2,1)S(1)}, bf16[2048,256...) custom-call(s32[1,128]{1,0:T(1,128)S(1)} %broadcast_in_dim.3.me_ref,, ...), custom_call_target="tpu_custom_call", output_to_operand_aliasing={{1}: (7, {}), {2}: (8, {}), {3}: (9, {}), {4}: (10, {}), {5... | custom-call | tf_op jit(solution)/shard_map/steps/pallas_call | solution.py:316
  (4 shorter events, 0.1 us)
Async XLA Ops:
  0.0 5.1 %copy-start.4 = (f32[2,64]{1,0:T(2,128)S(1)}, f32[2,64]{1,0:T(2,128)}, u32[]{:S(2)}) copy-start(f32[2,64]{1,0:T(2,128)} %weight_ref.1) | copy-start | bytes 1540
  0.0 10.5 %collective-permute-start = (f32[256,128]{1,0:T(8,128)}, f32[256,128]{1,0:T(8,128)S(1)}, u32[]{:S(2)}, u32[]{:S(2)}) collective-permute-start(f32[256,128]{1,0:T(8,128)} %bitcast.3), channel_id=1, source_target_pairs={{0,12},{1,13},{2,14},{3,15},{4,8},{5,9},{6,10},{7,11},{8,4},{9,5},... | collective-permute-start | bytes 393224 | tf_op jit(solution)/shard_map/ppermute | solution.py:82
  5.1 5.4 %collective-permute-start.1 = (f32[2,64]{1,0:T(2,128)S(1)}, f32[2,64]{1,0:T(2,128)S(1)}, u32[]{:S(2)}, u32[]{:S(2)}) collective-permute-start(f32[2,64]{1,0:T(2,128)S(1)} %copy-done.4), channel_id=1, source_target_pairs={{0,12},{1,13},{2,14},{3,15},{4,8},{5,9},{6,10},{7,11},{8,4},{9,5},... | collective-permute-start | bytes 1544 | tf_op jit(solution)/shard_map/ppermute | solution.py:82
  5.8 0.9 %copy-start.2 = (f32[2,128,2,64]{1,3,2,0:T(8,128)S(1)}, f32[2,128,2,64]{1,3,2,0:T(8,128)}, u32[]{:S(2)}) copy-start(f32[2,128,2,64]{1,3,2,0:T(8,128)} %param.6) | copy-start | bytes 393220
  6.7 1.7 %copy-start = (f32[256,128]{1,0:T(8,128)S(1)}, f32[256,128]{1,0:T(8,128)}, u32[]{:S(2)}) copy-start(f32[256,128]{1,0:T(8,128)} %coeff_table_ref.1) | copy-start | bytes 393220
  6.7 1.7 %copy-start.1 = (f32[256,128]{1,0:T(8,128)S(1)}, f32[256,128]{1,0:T(8,128)}, u32[]{:S(2)}) copy-start(f32[256,128]{1,0:T(8,128)} %force_table_ref.1) | copy-start | bytes 393220
  6.7 1.7 %copy-start.3 = (f32[256]{0:T(256)S(1)}, f32[256]{0:T(256)}, u32[]{:S(2)}) copy-start(f32[256]{0:T(256)} %visc_table_ref.1) | copy-start | bytes 3076
  6.7 1.7 %copy-start.5 = (s32[8]{0:T(128)S(1)}, s32[8]{0:T(128)}, u32[]{:S(2)}) copy-start(s32[8]{0:T(128)} %seeds_ref.1) | copy-start | bytes 100
  6.7 6.5 %collective-permute-start.5 = (f32[264,128]{1,0:T(8,128)S(1)}, f32[264,128]{1,0:T(8,128)S(1)}, u32[]{:S(2)}, u32[]{:S(2)}) collective-permute-start(f32[264,128]{1,0:T(8,128)S(1)} %pack.2.chunk_ref.refs_0_), channel_id=1, source_target_pairs={{0,4},{1,3},{2,6},{3,1},{4,0},{5,7},{6,2},{7,5},{8,12},{9,11},{10,... | collective-permute-start | bytes 405512 | tf_op jit(solution)/shard_map/ppermute | solution.py:82
  6.8 6.4 %collective-permute-start.8 = (f32[264,128]{1,0:T(8,128)S(1)}, f32[264,128]{1,0:T(8,128)S(1)}, u32[]{:S(2)}, u32[]{:S(2)}) collective-permute-start(f32[264,128]{1,0:T(8,128)S(1)} %pack.2.chunk_ref.refs_0_), channel_id=1, source_target_pairs={{0,2},{1,5},{2,0},{3,7},{4,6},{5,1},{6,4},{7,3},{8,10},{9,13},{10,... | collective-permute-start | bytes 405512 | tf_op jit(solution)/shard_map/ppermute | solution.py:82
  8.4 5.3 %collective-permute-start.10 = (f32[264,128]{1,0:T(8,128)S(1)}, f32[264,128]{1,0:T(8,128)S(1)}, u32[]{:S(2)}, u32[]{:S(2)}) collective-permute-start(f32[264,128]{1,0:T(8,128)S(1)} %pack.2.chunk_ref.refs_0_), channel_id=1, source_target_pairs={{0,1},{1,0},{2,3},{3,2},{4,5},{5,4},{6,7},{7,6},{8,9},{9,8},{10,11... | collective-permute-start | bytes 405512 | tf_op jit(solution)/shard_map/ppermute | solution.py:82
  10.5 5.5 %collective-permute-start.2 = (f32[264,128]{1,0:T(8,128)S(1)}, f32[264,128]{1,0:T(8,128)S(1)}, u32[]{:S(2)}, u32[]{:S(2)}) collective-permute-start(f32[264,128]{1,0:T(8,128)S(1)} %pack.3.refs_3_), channel_id=1, source_target_pairs={{0,4},{1,3},{2,6},{3,1},{4,0},{5,7},{6,2},{7,5},{8,12},{9,11},{10,... | collective-permute-start | bytes 405512 | tf_op jit(solution)/shard_map/ppermute | solution.py:82
  11.5 5.6 %collective-permute-start.9 = (f32[264,128]{1,0:T(8,128)S(1)}, f32[264,128]{1,0:T(8,128)S(1)}, u32[]{:S(2)}, u32[]{:S(2)}) collective-permute-start(f32[264,128]{1,0:T(8,128)S(1)} %pack.3.refs_3_), channel_id=1, source_target_pairs={{0,2},{1,5},{2,0},{3,7},{4,6},{5,1},{6,4},{7,3},{8,10},{9,13},{10,... | collective-permute-start | bytes 405512 | tf_op jit(solution)/shard_map/ppermute | solution.py:82
  13.2 3.9 %collective-permute-start.13 = (f32[264,128]{1,0:T(8,128)S(1)}, f32[264,128]{1,0:T(8,128)S(1)}, u32[]{:S(2)}, u32[]{:S(2)}) collective-permute-start(f32[264,128]{1,0:T(8,128)S(1)} %pack.3.refs_3_), channel_id=1, source_target_pairs={{0,1},{1,0},{2,3},{3,2},{4,5},{5,4},{6,7},{7,6},{8,9},{9,8},{10,11... | collective-permute-start | bytes 405512 | tf_op jit(solution)/shard_map/ppermute | solution.py:82
  13.2 4.4 %collective-permute-start.11 = (f32[264,128]{1,0:T(8,128)S(1)}, f32[264,128]{1,0:T(8,128)S(1)}, u32[]{:S(2)}, u32[]{:S(2)}) collective-permute-start(f32[264,128]{1,0:T(8,128)S(1)} %collective-permute-done.5.refs_1_), channel_id=1, source_target_pairs={{0,1},{1,0},{2,3},{3,2},{4,5},{5,4},{6,7},{7,6},{8,9},{9,8},{10,11... | collective-permute-start | bytes 405512 | tf_op jit(solution)/shard_map/ppermute | solution.py:82
  13.7 5.0 %collective-permute-start.6 = (f32[264,128]{1,0:T(8,128)S(1)}, f32[264,128]{1,0:T(8,128)S(1)}, u32[]{:S(2)}, u32[]{:S(2)}) collective-permute-start(f32[264,128]{1,0:T(8,128)S(1)} %collective-permute-done.5.refs_1_), channel_id=1, source_target_pairs={{0,2},{1,5},{2,0},{3,7},{4,6},{5,1},{6,4},{7,3},{8,10},{9,13},{10,... | collective-permute-start | bytes 405512 | tf_op jit(solution)/shard_map/ppermute | solution.py:82
  16.0 5.0 %collective-permute-start.3 = (f32[264,128]{1,0:T(8,128)S(1)}, f32[264,128]{1,0:T(8,128)S(1)}, u32[]{:S(2)}, u32[]{:S(2)}) collective-permute-start(f32[264,128]{1,0:T(8,128)S(1)} %collective-permute-done.2.refs_4_), channel_id=1, source_target_pairs={{0,2},{1,5},{2,0},{3,7},{4,6},{5,1},{6,4},{7,3},{8,10},{9,13},{10,... | collective-permute-start | bytes 405512 | tf_op jit(solution)/shard_map/ppermute | solution.py:82
  17.1 3.9 %collective-permute-start.12 = (f32[264,128]{1,0:T(8,128)S(1)}, f32[264,128]{1,0:T(8,128)S(1)}, u32[]{:S(2)}, u32[]{:S(2)}) collective-permute-start(f32[264,128]{1,0:T(8,128)S(1)} %collective-permute-done.8.refs_2_), channel_id=1, source_target_pairs={{0,1},{1,0},{2,3},{3,2},{4,5},{5,4},{6,7},{7,6},{8,9},{9,8},{10,11... | collective-permute-start | bytes 405512 | tf_op jit(solution)/shard_map/ppermute | solution.py:82
  17.1 3.9 %collective-permute-start.14 = (f32[264,128]{1,0:T(8,128)S(1)}, f32[264,128]{1,0:T(8,128)S(1)}, u32[]{:S(2)}, u32[]{:S(2)}) collective-permute-start(f32[264,128]{1,0:T(8,128)S(1)} %collective-permute-done.2.refs_4_), channel_id=1, source_target_pairs={{0,1},{1,0},{2,3},{3,2},{4,5},{5,4},{6,7},{7,6},{8,9},{9,8},{10,11... | collective-permute-start | bytes 405512 | tf_op jit(solution)/shard_map/ppermute | solution.py:82
  17.6 3.4 %collective-permute-start.15 = (f32[264,128]{1,0:T(8,128)S(1)}, f32[264,128]{1,0:T(8,128)S(1)}, u32[]{:S(2)}, u32[]{:S(2)}) collective-permute-start(f32[264,128]{1,0:T(8,128)S(1)} %collective-permute-done.9.refs_5_), channel_id=1, source_target_pairs={{0,1},{1,0},{2,3},{3,2},{4,5},{5,4},{6,7},{7,6},{8,9},{9,8},{10,11... | collective-permute-start | bytes 405512 | tf_op jit(solution)/shard_map/ppermute | solution.py:82
  18.7 3.1 %collective-permute-start.7 = (f32[264,128]{1,0:T(8,128)S(1)}, f32[264,128]{1,0:T(8,128)S(1)}, u32[]{:S(2)}, u32[]{:S(2)}) collective-permute-start(f32[264,128]{1,0:T(8,128)S(1)} %collective-permute-done.6.refs_0_), channel_id=1, source_target_pairs={{0,1},{1,0},{2,3},{3,2},{4,5},{5,4},{6,7},{7,6},{8,9},{9,8},{10,11... | collective-permute-start | bytes 405512 | tf_op jit(solution)/shard_map/ppermute | solution.py:82
  21.0 1.4 %collective-permute-start.4 = (f32[264,128]{1,0:T(8,128)S(1)}, f32[264,128]{1,0:T(8,128)S(1)}, u32[]{:S(2)}, u32[]{:S(2)}) collective-permute-start(f32[264,128]{1,0:T(8,128)S(1)} %collective-permute-done.3.refs_0_), channel_id=1, source_target_pairs={{0,1},{1,0},{2,3},{3,2},{4,5},{5,4},{6,7},{7,6},{8,9},{9,8},{10,11... | collective-permute-start | bytes 405512 | tf_op jit(solution)/shard_map/ppermute | solution.py:82

commit v6 on v5

--- a/solution.py
+++ b/solution.py
@@ -37,10 +37,13 @@
     )(cell_weight)
 
 
-def pack_kernel(modes_ref, row_ref, chunk_ref):
+def pack_kernel(modes_ref, weight_ref, chunk_ref):
     rows = modes_ref.shape[0]
     chunk_ref[0:rows, :] = modes_ref[...]
-    chunk_ref[rows : rows + SPARE_ROWS, :] = row_ref[...]
+    if weight_ref.shape == (SPARE_ROWS, modes_ref.shape[1]):
+        chunk_ref[rows : rows + SPARE_ROWS, :] = weight_ref[...]
+    else:
+        lay_kernel(weight_ref, chunk_ref.at[rows : rows + SPARE_ROWS, :])
 
 
 def pack(modes, weight_rows):
@@ -99,7 +102,7 @@
     far_weight = exchange((cell_weight, 0, 0), far, far)[0]
     own = (pack(rows, lay(cell_weight)), 0, 0)
     far_rows, *_ = lax.optimization_barrier((far_rows, *first_needed))
-    opposite = (pack(far_rows, lay(far_weight)), even, odd)
+    opposite = (pack(far_rows, far_weight), even, odd)
     held = []
     for start in (own, opposite):
         first = exchange(start, near, side)

time: 25 us -> 25 us (level)
  no operation moved by 1% of the time
where the time goes in v6:
time: 25 us; the launch traced here: 24.9 us
  starting transfers between devices  12.3 us (49%)
  waiting for transfers between devices  7.32 us (29%)
  Pallas kernels  4.25 us (17%)
  local copies, waits for them, and re-layouts  0.92 us (4%)
    ppermute x16, starting transfers between devices, exchange(): array = lax.ppermute(array, 'space', pairs)  12.3 us
    ppermute x16, waiting for transfers between devices, exchange(): array = lax.ppermute(array, 'space', pairs)  7.32 us
    pallas_call x1, Pallas kernels, shards(): pl.pallas_call(functools.partial(step_kernel, [one[1:] for one in late],...  2.56 us
    pallas_call x2, Pallas kernels, absorb(): pl.pallas_call(functools.partial(take_in_kernel, offsets, copies), out_sh...  0.94 us
    unnamed x12, local copies, waits for them, and re-layouts  0.92 us
    pallas_call x1, Pallas kernels, select(): pl.pallas_call(select_kernel, out_shape=(rows, rows, rows), in_specs=[sme...  0.57 us
  transfers between devices with their start and end apart: 16, of which 6 were waited for; matrix products, arithmetic and copies ran while one was open for 0% of the time, Pallas kernels for 7%

profile of v6, /device:TPU:0, one launch (start us, length us, event | category | flops | bytes accessed | tf_op | source)
XLA Modules:
  0.0 24.9 jit_solution(17614469930392410073)
XLA Ops:
  0.0 0.0 copy-start.4
  0.0 5.0 %collective-permute-start = (f32[256,128]{1,0:T(8,128)}, f32[256,128]{1,0:T(8,128)S(1)}, u32[]{:S(2)}, u32[]{:S(2)}) collective-permute-start(f32[256,128]{1,0:T(8,128)} %bitcast.3), channel_id=1, source_target_pairs={{0,12},{1,13},{2,14},{3,15},{4,8},{5,9},{6,10},{7,11},{8,4},{9,5},... | collective-permute-start | bytes 393224 | tf_op jit(solution)/shard_map/ppermute | solution.py:85
  5.1 0.0 copy-done.4
  5.1 0.7 %collective-permute-start.1 = (f32[2,64]{1,0:T(2,128)S(1)}, f32[2,64]{1,0:T(2,128)S(1)}, u32[]{:S(2)}, u32[]{:S(2)}) collective-permute-start(f32[2,64]{1,0:T(2,128)S(1)} %copy-done.4), channel_id=1, source_target_pairs={{0,12},{1,13},{2,14},{3,15},{4,8},{5,9},{6,10},{7,11},{8,4},{9,5},... | collective-permute-start | bytes 1544 | tf_op jit(solution)/shard_map/ppermute | solution.py:85
  5.7 0.1 lay.1.weight_ref
  5.8 0.0 copy-start.2
  5.8 0.9 %copy-done.2 = f32[2,128,2,64]{1,3,2,0:T(8,128)S(1)} copy-done((f32[2,128,2,64]{1,3,2,0:T(8,128)S(1)}, f32[2,128,2,64]{1,3,2,0:T(8,128)}, u32[]{:S(2)}) %copy-start.2) | copy-done | bytes 131096
  6.7 0.0 copy-start
  6.7 0.0 copy-start.1
  6.7 0.0 copy-start.3
  6.7 0.0 copy-start.5
  6.7 0.1 collective-permute-start.5
  6.8 1.6 %collective-permute-start.8 = (f32[264,128]{1,0:T(8,128)S(1)}, f32[264,128]{1,0:T(8,128)S(1)}, u32[]{:S(2)}, u32[]{:S(2)}) collective-permute-start(f32[264,128]{1,0:T(8,128)S(1)} %pack.2.chunk_ref.refs_0_), channel_id=1, source_target_pairs={{0,2},{1,5},{2,0},{3,7},{4,6},{5,1},{6,4},{7,3},{8,10},{9,13},{10,... | collective-permute-start | bytes 405512 | tf_op jit(solution)/shard_map/ppermute | solution.py:85
  8.4 0.0 collective-permute-start.10
  8.4 0.0 copy-done
  8.4 0.0 copy-done.1
  8.4 0.0 copy-done.3
  8.4 0.0 copy-done.5
  8.4 0.6 %select.1 = (f32[8,128]{1,0:T(8,128)S(1)}, f32[8,128]{1,0:T(8,128)S(1)}, f32[8,128]{1,0:T(8,128)S(1)}) custom-call(s32[8]{0:T(128)S(1)} %copy-done.5, f32[256]{0:T(256)S(1)} %copy-done.3, f32[256,128]{1,0:T(8,128)S(1)} %copy-done, f32[256,128]{1,0:T(8,128)S(1)} %copy-done.1), custom_call_target="tpu_custom_call" | custom-call | tf_op jit(solution)/shard_map/select/pallas_call | solution.py:143
  9.0 0.0 collective-permute-done.modes_ref
  9.0 1.4 %collective-permute-done.1.weight_ref = f32[2,64]{1,0:T(2,128)S(1)} collective-permute-done((f32[2,64]{1,0:T(2,128)S(1)}, f32[2,64]{1,0:T(2,128)S(1)}, u32[]{:S(2)}, u32[]{:S(2)}) %collective-permute-start.1) | collective-permute-done | bytes 544 | tf_op jit(solution)/shard_map/ppermute | solution.py:85
  10.4 0.1 pack.3.refs_3_
  10.5 1.0 %collective-permute-start.2 = (f32[264,128]{1,0:T(8,128)S(1)}, f32[264,128]{1,0:T(8,128)S(1)}, u32[]{:S(2)}, u32[]{:S(2)}) collective-permute-start(f32[264,128]{1,0:T(8,128)S(1)} %pack.3.refs_3_), channel_id=1, source_target_pairs={{0,4},{1,3},{2,6},{3,1},{4,0},{5,7},{6,2},{7,5},{8,12},{9,11},{10,... | collective-permute-start | bytes 405512 | tf_op jit(solution)/shard_map/ppermute | solution.py:85
  11.4 1.5 %collective-permute-start.9 = (f32[264,128]{1,0:T(8,128)S(1)}, f32[264,128]{1,0:T(8,128)S(1)}, u32[]{:S(2)}, u32[]{:S(2)}) collective-permute-start(f32[264,128]{1,0:T(8,128)S(1)} %pack.3.refs_3_), channel_id=1, source_target_pairs={{0,2},{1,5},{2,0},{3,7},{4,6},{5,1},{6,4},{7,3},{8,10},{9,13},{10,... | collective-permute-start | bytes 405512 | tf_op jit(solution)/shard_map/ppermute | solution.py:85
  12.9 0.3 %collective-permute-done.5.refs_1_ = f32[264,128]{1,0:T(8,128)S(1)} collective-permute-done((f32[264,128]{1,0:T(8,128)S(1)}, f32[264,128]{1,0:T(8,128)S(1)}, u32[]{:S(2)}, u32[]{:S(2)}) %collective-permute-start.5) | collective-permute-done | bytes 135200 | tf_op jit(solution)/shard_map/ppermute | solution.py:85
  13.3 0.0 collective-permute-start.13
  13.3 0.0 collective-permute-done.8.refs_2_
  13.3 0.5 %collective-permute-start.11 = (f32[264,128]{1,0:T(8,128)S(1)}, f32[264,128]{1,0:T(8,128)S(1)}, u32[]{:S(2)}, u32[]{:S(2)}) collective-permute-start(f32[264,128]{1,0:T(8,128)S(1)} %collective-permute-done.5.refs_1_), channel_id=1, source_target_pairs={{0,1},{1,0},{2,3},{3,2},{4,5},{5,4},{6,7},{7,6},{8,9},{9,8},{10,11... | collective-permute-start | bytes 405512 | tf_op jit(solution)/shard_map/ppermute | solution.py:85
  13.8 0.0 collective-permute-done.10.refs_6_
  13.8 0.3 %collective-permute-start.6 = (f32[264,128]{1,0:T(8,128)S(1)}, f32[264,128]{1,0:T(8,128)S(1)}, u32[]{:S(2)}, u32[]{:S(2)}) collective-permute-start(f32[264,128]{1,0:T(8,128)S(1)} %collective-permute-done.5.refs_1_), channel_id=1, source_target_pairs={{0,2},{1,5},{2,0},{3,7},{4,6},{5,1},{6,4},{7,3},{8,10},{9,13},{10,... | collective-permute-start | bytes 405512 | tf_op jit(solution)/shard_map/ppermute | solution.py:85
  14.1 1.8 %collective-permute-done.2.refs_4_ = f32[264,128]{1,0:T(8,128)S(1)} collective-permute-done((f32[264,128]{1,0:T(8,128)S(1)}, f32[264,128]{1,0:T(8,128)S(1)}, u32[]{:S(2)}, u32[]{:S(2)}) %collective-permute-start.2) | collective-permute-done | bytes 135200 | tf_op jit(solution)/shard_map/ppermute | solution.py:85
  16.0 1.1 %collective-permute-start.3 = (f32[264,128]{1,0:T(8,128)S(1)}, f32[264,128]{1,0:T(8,128)S(1)}, u32[]{:S(2)}, u32[]{:S(2)}) collective-permute-start(f32[264,128]{1,0:T(8,128)S(1)} %collective-permute-done.2.refs_4_), channel_id=1, source_target_pairs={{0,2},{1,5},{2,0},{3,7},{4,6},{5,1},{6,4},{7,3},{8,10},{9,13},{10,... | collective-permute-start | bytes 405512 | tf_op jit(solution)/shard_map/ppermute | solution.py:85
  17.0 0.0 collective-permute-done.9.refs_5_
  17.0 0.0 collective-permute-start.12
  17.0 0.0 collective-permute-done.13.refs_9_
  17.0 0.5 %collective-permute-start.14 = (f32[264,128]{1,0:T(8,128)S(1)}, f32[264,128]{1,0:T(8,128)S(1)}, u32[]{:S(2)}, u32[]{:S(2)}) collective-permute-start(f32[264,128]{1,0:T(8,128)S(1)} %collective-permute-done.2.refs_4_), channel_id=1, source_target_pairs={{0,1},{1,0},{2,3},{3,2},{4,5},{5,4},{6,7},{7,6},{8,9},{9,8},{10,11... | collective-permute-start | bytes 405512 | tf_op jit(solution)/shard_map/ppermute | solution.py:85
  17.5 0.0 collective-permute-done.11.refs_7_
  17.5 0.1 collective-permute-start.15
  17.6 1.2 %collective-permute-done.6.refs_0_ = f32[264,128]{1,0:T(8,128)S(1)} collective-permute-done((f32[264,128]{1,0:T(8,128)S(1)}, f32[264,128]{1,0:T(8,128)S(1)}, u32[]{:S(2)}, u32[]{:S(2)}) %collective-permute-start.6) | collective-permute-done | bytes 135200 | tf_op jit(solution)/shard_map/ppermute | solution.py:85
  18.8 0.0 collective-permute-start.7
  18.8 2.2 %collective-permute-done.3.refs_0_ = f32[264,128]{1,0:T(8,128)S(1)} collective-permute-done((f32[264,128]{1,0:T(8,128)S(1)}, f32[264,128]{1,0:T(8,128)S(1)}, u32[]{:S(2)}, u32[]{:S(2)}) %collective-permute-start.3) | collective-permute-done | bytes 135200 | tf_op jit(solution)/shard_map/ppermute | solution.py:85
  21.0 0.0 collective-permute-start.4
  21.0 0.0 collective-permute-done.12.refs_8_
  21.0 0.0 collective-permute-done.14.refs_10_
  21.0 0.0 collective-permute-done.15.refs_11_
  21.0 0.7 %absorb.2 = (f32[2,16,8,128]{3,2,1,0:T(8,128)S(1)}, f32[16,128]{1,0:T(8,128)S(1)}, bf16[2048,256]{1,0:T(8,128)(2,1)S(1)}, bf16[2048,256]{1,0:T(8,128)(2,1)S(1)},...) custom-call(s32[1,128]{1,0:T(1,128)S(1)} %broadcast_in_dim.3.me_ref, ...), custom_call_target="tpu_custom_call" | custom-call | tf_op jit(solution)/shard_map/absorb/pallas_call | solution.py:201
  21.8 0.0 collective-permute-done.7.refs_1_
  21.8 0.2 absorb.3
  22.0 0.3 %collective-permute-done.4.refs_1_ = f32[264,128]{1,0:T(8,128)S(1)} collective-permute-done((f32[264,128]{1,0:T(8,128)S(1)}, f32[264,128]{1,0:T(8,128)S(1)}, u32[]{:S(2)}, u32[]{:S(2)}) %collective-permute-start.4) | collective-permute-done | bytes 135200 | tf_op jit(solution)/shard_map/ppermute | solution.py:85
  22.3 2.6 %steps.1 = (f32[8,128]{1,0:T(8,128)}, f32[2,16,8,128]{3,2,1,0:T(8,128)S(1)}, f32[16,128]{1,0:T(8,128)S(1)}, bf16[2048,256]{1,0:T(8,128)(2,1)S(1)}, bf16[2048,256...) custom-call(s32[1,128]{1,0:T(1,128)S(1)} %broadcast_in_dim.3.me_ref,, ...), custom_call_target="tpu_custom_call", output_to_operand_aliasing={{1}: (7, {}), {2}: (8, {}), {3}: (9, {}), {4}: (10, {}), {5... | custom-call | tf_op jit(solution)/shard_map/steps/pallas_call | solution.py:319
  (3 shorter events, 0.0 us)
Async XLA Ops:
  0.0 5.1 %copy-start.4 = (f32[2,64]{1,0:T(2,128)S(1)}, f32[2,64]{1,0:T(2,128)}, u32[]{:S(2)}) copy-start(f32[2,64]{1,0:T(2,128)} %weight_ref.1) | copy-start | bytes 1540
  0.0 9.0 %collective-permute-start = (f32[256,128]{1,0:T(8,128)}, f32[256,128]{1,0:T(8,128)S(1)}, u32[]{:S(2)}, u32[]{:S(2)}) collective-permute-start(f32[256,128]{1,0:T(8,128)} %bitcast.3), channel_id=1, source_target_pairs={{0,12},{1,13},{2,14},{3,15},{4,8},{5,9},{6,10},{7,11},{8,4},{9,5},... | collective-permute-start | bytes 393224 | tf_op jit(solution)/shard_map/ppermute | solution.py:85
  5.1 5.4 %collective-permute-start.1 = (f32[2,64]{1,0:T(2,128)S(1)}, f32[2,64]{1,0:T(2,128)S(1)}, u32[]{:S(2)}, u32[]{:S(2)}) collective-permute-start(f32[2,64]{1,0:T(2,128)S(1)} %copy-done.4), channel_id=1, source_target_pairs={{0,12},{1,13},{2,14},{3,15},{4,8},{5,9},{6,10},{7,11},{8,4},{9,5},... | collective-permute-start | bytes 1544 | tf_op jit(solution)/shard_map/ppermute | solution.py:85
  5.8 0.9 %copy-start.2 = (f32[2,128,2,64]{1,3,2,0:T(8,128)S(1)}, f32[2,128,2,64]{1,3,2,0:T(8,128)}, u32[]{:S(2)}) copy-start(f32[2,128,2,64]{1,3,2,0:T(8,128)} %param.6) | copy-start | bytes 393220
  6.7 1.7 %copy-start = (f32[256,128]{1,0:T(8,128)S(1)}, f32[256,128]{1,0:T(8,128)}, u32[]{:S(2)}) copy-start(f32[256,128]{1,0:T(8,128)} %coeff_table_ref.1) | copy-start | bytes 393220
  6.7 1.7 %copy-start.1 = (f32[256,128]{1,0:T(8,128)S(1)}, f32[256,128]{1,0:T(8,128)}, u32[]{:S(2)}) copy-start(f32[256,128]{1,0:T(8,128)} %force_table_ref.1) | copy-start | bytes 393220
  6.7 1.7 %copy-start.3 = (f32[256]{0:T(256)S(1)}, f32[256]{0:T(256)}, u32[]{:S(2)}) copy-start(f32[256]{0:T(256)} %visc_table_ref.1) | copy-start | bytes 3076
  6.7 1.7 %copy-start.5 = (s32[8]{0:T(128)S(1)}, s32[8]{0:T(128)}, u32[]{:S(2)}) copy-start(s32[8]{0:T(128)} %seeds_ref.1) | copy-start | bytes 100
  6.7 6.5 %collective-permute-start.5 = (f32[264,128]{1,0:T(8,128)S(1)}, f32[264,128]{1,0:T(8,128)S(1)}, u32[]{:S(2)}, u32[]{:S(2)}) collective-permute-start(f32[264,128]{1,0:T(8,128)S(1)} %pack.2.chunk_ref.refs_0_), channel_id=1, source_target_pairs={{0,4},{1,3},{2,6},{3,1},{4,0},{5,7},{6,2},{7,5},{8,12},{9,11},{10,... | collective-permute-start | bytes 405512 | tf_op jit(solution)/shard_map/ppermute | solution.py:85
  6.8 6.5 %collective-permute-start.8 = (f32[264,128]{1,0:T(8,128)S(1)}, f32[264,128]{1,0:T(8,128)S(1)}, u32[]{:S(2)}, u32[]{:S(2)}) collective-permute-start(f32[264,128]{1,0:T(8,128)S(1)} %pack.2.chunk_ref.refs_0_), channel_id=1, source_target_pairs={{0,2},{1,5},{2,0},{3,7},{4,6},{5,1},{6,4},{7,3},{8,10},{9,13},{10,... | collective-permute-start | bytes 405512 | tf_op jit(solution)/shard_map/ppermute | solution.py:85
  8.4 5.4 %collective-permute-start.10 = (f32[264,128]{1,0:T(8,128)S(1)}, f32[264,128]{1,0:T(8,128)S(1)}, u32[]{:S(2)}, u32[]{:S(2)}) collective-permute-start(f32[264,128]{1,0:T(8,128)S(1)} %pack.2.chunk_ref.refs_0_), channel_id=1, source_target_pairs={{0,1},{1,0},{2,3},{3,2},{4,5},{5,4},{6,7},{7,6},{8,9},{9,8},{10,11... | collective-permute-start | bytes 405512 | tf_op jit(solution)/shard_map/ppermute | solution.py:85
  10.5 5.5 %collective-permute-start.2 = (f32[264,128]{1,0:T(8,128)S(1)}, f32[264,128]{1,0:T(8,128)S(1)}, u32[]{:S(2)}, u32[]{:S(2)}) collective-permute-start(f32[264,128]{1,0:T(8,128)S(1)} %pack.3.refs_3_), channel_id=1, source_target_pairs={{0,4},{1,3},{2,6},{3,1},{4,0},{5,7},{6,2},{7,5},{8,12},{9,11},{10,... | collective-permute-start | bytes 405512 | tf_op jit(solution)/shard_map/ppermute | solution.py:85
  11.4 5.6 %collective-permute-start.9 = (f32[264,128]{1,0:T(8,128)S(1)}, f32[264,128]{1,0:T(8,128)S(1)}, u32[]{:S(2)}, u32[]{:S(2)}) collective-permute-start(f32[264,128]{1,0:T(8,128)S(1)} %pack.3.refs_3_), channel_id=1, source_target_pairs={{0,2},{1,5},{2,0},{3,7},{4,6},{5,1},{6,4},{7,3},{8,10},{9,13},{10,... | collective-permute-start | bytes 405512 | tf_op jit(solution)/shard_map/ppermute | solution.py:85
  13.3 3.8 %collective-permute-start.13 = (f32[264,128]{1,0:T(8,128)S(1)}, f32[264,128]{1,0:T(8,128)S(1)}, u32[]{:S(2)}, u32[]{:S(2)}) collective-permute-start(f32[264,128]{1,0:T(8,128)S(1)} %pack.3.refs_3_), channel_id=1, source_target_pairs={{0,1},{1,0},{2,3},{3,2},{4,5},{5,4},{6,7},{7,6},{8,9},{9,8},{10,11... | collective-permute-start | bytes 405512 | tf_op jit(solution)/shard_map/ppermute | solution.py:85
  13.3 4.3 %collective-permute-start.11 = (f32[264,128]{1,0:T(8,128)S(1)}, f32[264,128]{1,0:T(8,128)S(1)}, u32[]{:S(2)}, u32[]{:S(2)}) collective-permute-start(f32[264,128]{1,0:T(8,128)S(1)} %collective-permute-done.5.refs_1_), channel_id=1, source_target_pairs={{0,1},{1,0},{2,3},{3,2},{4,5},{5,4},{6,7},{7,6},{8,9},{9,8},{10,11... | collective-permute-start | bytes 405512 | tf_op jit(solution)/shard_map/ppermute | solution.py:85
  13.8 5.0 %collective-permute-start.6 = (f32[264,128]{1,0:T(8,128)S(1)}, f32[264,128]{1,0:T(8,128)S(1)}, u32[]{:S(2)}, u32[]{:S(2)}) collective-permute-start(f32[264,128]{1,0:T(8,128)S(1)} %collective-permute-done.5.refs_1_), channel_id=1, source_target_pairs={{0,2},{1,5},{2,0},{3,7},{4,6},{5,1},{6,4},{7,3},{8,10},{9,13},{10,... | collective-permute-start | bytes 405512 | tf_op jit(solution)/shard_map/ppermute | solution.py:85
  16.0 5.0 %collective-permute-start.3 = (f32[264,128]{1,0:T(8,128)S(1)}, f32[264,128]{1,0:T(8,128)S(1)}, u32[]{:S(2)}, u32[]{:S(2)}) collective-permute-start(f32[264,128]{1,0:T(8,128)S(1)} %collective-permute-done.2.refs_4_), channel_id=1, source_target_pairs={{0,2},{1,5},{2,0},{3,7},{4,6},{5,1},{6,4},{7,3},{8,10},{9,13},{10,... | collective-permute-start | bytes 405512 | tf_op jit(solution)/shard_map/ppermute | solution.py:85
  17.0 4.0 %collective-permute-start.12 = (f32[264,128]{1,0:T(8,128)S(1)}, f32[264,128]{1,0:T(8,128)S(1)}, u32[]{:S(2)}, u32[]{:S(2)}) collective-permute-start(f32[264,128]{1,0:T(8,128)S(1)} %collective-permute-done.8.refs_2_), channel_id=1, source_target_pairs={{0,1},{1,0},{2,3},{3,2},{4,5},{5,4},{6,7},{7,6},{8,9},{9,8},{10,11... | collective-permute-start | bytes 405512 | tf_op jit(solution)/shard_map/ppermute | solution.py:85
  17.0 4.0 %collective-permute-start.14 = (f32[264,128]{1,0:T(8,128)S(1)}, f32[264,128]{1,0:T(8,128)S(1)}, u32[]{:S(2)}, u32[]{:S(2)}) collective-permute-start(f32[264,128]{1,0:T(8,128)S(1)} %collective-permute-done.2.refs_4_), channel_id=1, source_target_pairs={{0,1},{1,0},{2,3},{3,2},{4,5},{5,4},{6,7},{7,6},{8,9},{9,8},{10,11... | collective-permute-start | bytes 405512 | tf_op jit(solution)/shard_map/ppermute | solution.py:85
  17.5 3.5 %collective-permute-start.15 = (f32[264,128]{1,0:T(8,128)S(1)}, f32[264,128]{1,0:T(8,128)S(1)}, u32[]{:S(2)}, u32[]{:S(2)}) collective-permute-start(f32[264,128]{1,0:T(8,128)S(1)} %collective-permute-done.9.refs_5_), channel_id=1, source_target_pairs={{0,1},{1,0},{2,3},{3,2},{4,5},{5,4},{6,7},{7,6},{8,9},{9,8},{10,11... | collective-permute-start | bytes 405512 | tf_op jit(solution)/shard_map/ppermute | solution.py:85
  18.8 3.0 %collective-permute-start.7 = (f32[264,128]{1,0:T(8,128)S(1)}, f32[264,128]{1,0:T(8,128)S(1)}, u32[]{:S(2)}, u32[]{:S(2)}) collective-permute-start(f32[264,128]{1,0:T(8,128)S(1)} %collective-permute-done.6.refs_0_), channel_id=1, source_target_pairs={{0,1},{1,0},{2,3},{3,2},{4,5},{5,4},{6,7},{7,6},{8,9},{9,8},{10,11... | collective-permute-start | bytes 405512 | tf_op jit(solution)/shard_map/ppermute | solution.py:85
  21.0 1.4 %collective-permute-start.4 = (f32[264,128]{1,0:T(8,128)S(1)}, f32[264,128]{1,0:T(8,128)S(1)}, u32[]{:S(2)}, u32[]{:S(2)}) collective-permute-start(f32[264,128]{1,0:T(8,128)S(1)} %collective-permute-done.3.refs_0_), channel_id=1, source_target_pairs={{0,1},{1,0},{2,3},{3,2},{4,5},{5,4},{6,7},{7,6},{8,9},{9,8},{10,11... | collective-permute-start | bytes 405512 | tf_op jit(solution)/shard_map/ppermute | solution.py:85
